TPU v7x, 256 devices: a whole 4x4x8 slice. The times are simulated.
256 devices in a mesh: pipe: 8 (over x, y_hi), ep: 32 (over z, y_lo, core).
Axes of the slice: x: 4, y: 4 (y_hi: 2, y_lo: 2; y = y_hi * 2 + y_lo), z: 8, core: 2. Of those that a mesh axis runs over, the one named last changes fastest.
Arguments:
- acts: bfloat16 [32768, 3584], P(('pipe', 'ep')), may hold values from -6 to 6
- cotan: bfloat16 [32768, 3584], P(('pipe', 'ep')), may hold values from -6 to 6
- routes: int32 [32768, 8], P(('pipe', 'ep')), may hold values from 0 to 255, all different within a row; in each aligned block of 128 rows (0 to 127, 128 to 255, ...) at most 8 rows name the same one
- scores: float32 [32768, 8], P(('pipe', 'ep')), may hold values from 0.05 to 1
- w_gate: bfloat16 [8, 3584, 12288], P('pipe', None, 'ep'), may hold values from -0.09375 to 0.09375
- w_up: bfloat16 [8, 3584, 12288], P('pipe', None, 'ep'), may hold values from -0.09375 to 0.09375
- w_down: bfloat16 [8, 12288, 3584], P('pipe', 'ep'), may hold values from -0.15625 to 0.15625
Outputs:
- next_acts: bfloat16 [32768, 3584], P(('pipe', 'ep'))
- prev_grads: bfloat16 [32768, 3584], P(('pipe', 'ep'))
Inputs may be any that keep to these rules, and one draw needn't show every extreme that they name: `routes`: in the rows of one device no expert is named by more than 8 rows; a row names 8 different experts.
All inputs are finite; a program needn't handle non-finite values.
Results may differ from a plain program's by a relative error of at most 0.015.
Values may be sent and summed in bfloat16 or wider, within the bound.
No kernel may reach another device: no remote copies, remote signals or barrier semaphores. Data moves between devices by JAX's collectives and lax.ppermute only.
A program may use at most 64 MiB of HBM per device.

v0:
```python
import jax
import jax.numpy as jnp
from jax import lax
from jax.sharding import PartitionSpec as P

SHARDS = 4


ROUTE_SCALE = 2.5


def shifted(block, axis, distance):
    devices = range(lax.axis_size(axis))
    route = [((i - distance) % len(devices), i) for i in devices]
    return lax.ppermute(block, axis, route)


def pass_right(values):
    return shifted(values, "pipe", 1)


def pass_left(values):
    return shifted(values, "pipe", -1)


def shards(acts, cotan, routes, scores, w_gate, w_up, w_down):
    groups = lax.axis_size("ep") // SHARDS
    tok_rows = acts.shape[0]
    width = acts.shape[1]
    capacity = tok_rows // 16
    gate_mat = w_gate[0]
    up_mat = w_up[0]
    down_mat = w_down[0]
    norm_w = scores / jnp.sum(scores, axis=1, keepdims=True) * ROUTE_SCALE
    match = routes[:, :, None] == jnp.arange(groups, dtype=jnp.int32)
    member = jnp.sum(match.astype(jnp.int32), axis=1)
    weight_te = jnp.sum(jnp.where(match, norm_w[:, :, None], 0.0), axis=1)
    slot_of = jnp.cumsum(member, axis=0) - member
    placed = (member[:, :, None] == 1) & (
        slot_of[:, :, None] == jnp.arange(capacity, dtype=jnp.int32)
    )
    dispatch = placed.reshape(tok_rows, groups * capacity).T.astype(jnp.bfloat16)
    combine = (placed.astype(jnp.float32) * weight_te[:, :, None]).reshape(
        tok_rows, groups * capacity
    )

    def pack_rows(values):
        buffer = jnp.dot(dispatch, values, preferred_element_type=jnp.float32).astype(jnp.bfloat16)
        return jnp.repeat(buffer.reshape(groups, capacity, width), SHARDS, axis=0)

    def unpack_rows(returned):
        summed = returned.reshape(groups, SHARDS, capacity, width).astype(jnp.float32).sum(axis=1)
        summed = summed.reshape(groups * capacity, width)
        return jnp.dot(combine, summed, precision=lax.Precision.HIGHEST).astype(jnp.bfloat16)

    send_x = pack_rows(acts)
    send_g = pack_rows(cotan)
    token_part = lax.all_to_all(send_x, "ep", split_axis=0, concat_axis=0, tiled=True)
    grad_part = lax.all_to_all(send_g, "ep", split_axis=0, concat_axis=0, tiled=True)
    flat_rows = token_part.reshape(-1, width)
    gate_val = jnp.dot(flat_rows, gate_mat, preferred_element_type=jnp.float32)
    up_val = jnp.dot(flat_rows, up_mat, preferred_element_type=jnp.float32)
    sig_val = jax.nn.sigmoid(gate_val)
    hidden = (gate_val * sig_val * up_val).astype(jnp.bfloat16)
    expert_out = jnp.dot(hidden, down_mat, preferred_element_type=jnp.float32).astype(jnp.bfloat16)
    expert_out, gate_val, up_val = (expert_out.reshape(token_part.shape), gate_val, up_val)
    flat_grads = grad_part.reshape(-1, width)
    contract = (((1,), (1,)), ((), ()))
    d_hidden = lax.dot_general(flat_grads, down_mat, contract, preferred_element_type=jnp.float32)
    sig_val = jax.nn.sigmoid(gate_val)
    d_gate = (d_hidden * up_val * sig_val * (1.0 + gate_val * (1.0 - sig_val))).astype(jnp.bfloat16)
    d_up = (d_hidden * gate_val * sig_val).astype(jnp.bfloat16)
    grad_in = lax.dot_general(d_gate, gate_mat, contract, preferred_element_type=jnp.float32)
    grad_in = grad_in + lax.dot_general(d_up, up_mat, contract, preferred_element_type=jnp.float32)
    grad_in = grad_in.astype(jnp.bfloat16).reshape(grad_part.shape)
    out_back = lax.all_to_all(expert_out, "ep", split_axis=0, concat_axis=0, tiled=True)
    grad_back = lax.all_to_all(grad_in, "ep", split_axis=0, concat_axis=0, tiled=True)
    next_acts = pass_right(unpack_rows(out_back))
    prev_grads = pass_left(unpack_rows(grad_back))
    return (next_acts, prev_grads)


def solution(mesh):
    in_specs = (
        P(("pipe", "ep"), None),
        P(("pipe", "ep"), None),
        P(("pipe", "ep"), None),
        P(("pipe", "ep"), None),
        P("pipe", None, "ep"),
        P("pipe", None, "ep"),
        P("pipe", "ep", None),
    )
    out_specs = (P(("pipe", "ep"), None), P(("pipe", "ep"), None))
    return jax.shard_map(shards, mesh=mesh, in_specs=in_specs, out_specs=out_specs, check_vma=False)
```

profile of v0, /device:TPU:32, one launch (start us, length us, event | category | flops | bytes accessed | tf_op | source)
XLA Modules:
  0.0 251.8 jit_solution(648982693762153061)
XLA Ops:
  0.6 0.0 copy-start
  0.6 0.9 convert_reduce_fusion.2
  1.5 0.1 copy.11
  1.6 0.2 reduce_window_sum.11
  1.8 0.1 eq.58
  1.9 1.5 fusion.5
  3.5 1.4 broadcast_in_dim.28
  4.8 9.8 %all-to-all-start = ((bf16[32,8,3584]{2,1,0:T(8,128)(2,1)}), bf16[32,8,3584]{2,1,0:T(8,128)(2,1)}, u32[]{:S(2)}, u32[]{:S(2)}) async-start(bf16[32,8,3584]{2,1,0:T(8,128)(2,1)} %bitcast.62), calls=%async_computation | async-start | bytes 3670016 | tf_op jit(solution)/shard_map/all_to_all | solution.py:58
  14.6 1.5 fusion.6
  16.1 43.4 %all-to-all-done = bf16[32,8,3584]{2,1,0:T(8,128)(2,1)} async-done(((bf16[32,8,3584]{2,1,0:T(8,128)(2,1)}), bf16[32,8,3584]{2,1,0:T(8,128)(2,1)}, u32[]{:S(2)}, u32[]{:S(2)}) %all-to-all-start) | async-done | bytes 1835040 | tf_op jit(solution)/shard_map/all_to_all | solution.py:58
  59.6 1.4 broadcast_in_dim.29
  61.0 4.5 %all-to-all-start.2 = ((bf16[32,8,3584]{2,1,0:T(8,128)(2,1)}), bf16[32,8,3584]{2,1,0:T(8,128)(2,1)}, u32[]{:S(2)}, u32[]{:S(2)}) async-start(bf16[32,8,3584]{2,1,0:T(8,128)(2,1)} %bitcast.61), calls=%async_computation.2 | async-start | bytes 3670016 | tf_op jit(solution)/shard_map/all_to_all | solution.py:59
  65.5 0.0 copy-done
  65.5 0.0 copy-start.1
  65.6 2.8 %fusion.15 = f32[256,384]{1,0:T(8,128)S(1)} fusion(bf16[1,3584,384]{2,1,0:T(8,128)(2,1)S(1)} %copy-done, bf16[32,8,3584]{2,1,0:T(8,128)(2,1)} %all-to-all-done), kind=kOutput, calls=%fused_computation.23 | convolution fusion | flops 704643072 | bytes 4980736 | tf_op jit(solution)/shard_map/dot_general | solution.py:61
  68.3 0.0 copy-done.1
  68.3 2.6 %fusion.11 = f32[256,384]{1,0:T(8,128)S(1)} fusion(bf16[1,3584,384]{2,1,0:T(8,128)(2,1)S(1)} %copy-done.1, bf16[32,8,3584]{2,1,0:T(8,128)(2,1)} %all-to-all-done), kind=kOutput, calls=%fused_computation.19 | convolution fusion | flops 704643072 | bytes 4980736 | tf_op jit(solution)/shard_map/dot_general | solution.py:62
  70.9 39.6 %all-to-all-done.2 = bf16[32,8,3584]{2,1,0:T(8,128)(2,1)} async-done(((bf16[32,8,3584]{2,1,0:T(8,128)(2,1)}), bf16[32,8,3584]{2,1,0:T(8,128)(2,1)}, u32[]{:S(2)}, u32[]{:S(2)}) %all-to-all-start.2) | async-done | bytes 1835040 | tf_op jit(solution)/shard_map/all_to_all | solution.py:59
  110.6 3.5 %fusion.7 = f32[256,384]{1,0:T(8,128)S(1)} fusion(bf16[1,384,3584]{2,1,0:T(8,128)(2,1)} %param.13, bf16[32,8,3584]{2,1,0:T(8,128)(2,1)} %all-to-all-done.2), kind=kOutput, calls=%fused_computation.15 | convolution fusion | flops 704643072 | bytes 4980736 | tf_op jit(solution)/shard_map/dot_general | solution.py:69
  114.0 0.0 copy-start.2
  114.1 1.2 fusion.13
  115.2 0.6 copy-done.2
  115.8 2.4 fusion.2
  118.2 5.7 %all-to-all-start.3 = ((bf16[32,8,3584]{2,1,0:T(8,128)(2,1)}), bf16[32,8,3584]{2,1,0:T(8,128)(2,1)}, u32[]{:S(2)}, u32[]{:S(2)}) async-start(bf16[32,8,3584]{2,1,0:T(8,128)(2,1)} %fusion.2), calls=%async_computation.3 | async-start | bytes 3670016 | tf_op jit(solution)/shard_map/all_to_all | solution.py:77
  124.0 4.2 %fusion.1 = bf16[32,8,3584]{2,1,0:T(8,128)(2,1)} fusion(bf16[1,384,3584]{2,1,0:T(8,128)(2,1)} %param.13, f32[256,384]{1,0:T(8,128)S(1)} %fusion.11, f32[256,384]{1,0:T(8,128)S(1)} %fusion.15), kind=kOutput, calls=%fused_computation.3 | convolution fusion | flops 706150400 | bytes 5373952 | tf_op jit(solution)/shard_map/dot_general | solution.py:65
  128.1 0.0 copy-start.4
  128.1 0.0 copy-start.3
  128.1 40.9 %all-to-all-done.3 = bf16[32,8,3584]{2,1,0:T(8,128)(2,1)} async-done(((bf16[32,8,3584]{2,1,0:T(8,128)(2,1)}), bf16[32,8,3584]{2,1,0:T(8,128)(2,1)}, u32[]{:S(2)}, u32[]{:S(2)}) %all-to-all-start.3) | async-done | bytes 1835040 | tf_op jit(solution)/shard_map/all_to_all | solution.py:77
  169.0 5.7 %all-to-all-start.1 = ((bf16[32,8,3584]{2,1,0:T(8,128)(2,1)}), bf16[32,8,3584]{2,1,0:T(8,128)(2,1)}, u32[]{:S(2)}, u32[]{:S(2)}) async-start(bf16[32,8,3584]{2,1,0:T(8,128)(2,1)} %fusion.1), calls=%async_computation.1 | async-start | bytes 3670016 | tf_op jit(solution)/shard_map/all_to_all | solution.py:76
  174.8 0.0 copy-done.4
  174.8 0.0 copy-done.3
  174.8 1.9 convert_reduce_fusion
  176.7 2.6 %fusion.4 = bf16[128,3584]{1,0:T(8,128)(2,1)} fusion(f32[8,8,3584]{2,1,0:T(8,128)S(1)} %convert_reduce_fusion, f32[128,8]{0,1:T(8,128)S(1)} %select_reduce_fusion, s32[128,8]{0,1:T(8,128)S(1)} %copy.13, pred[128,8]{0,1:T(8,128)(4,1)S(1)} %broadcast_compare_fusion), kind=kOutput, calls=%fused_computation.8 | convolution fusion | flops 352804864 | bytes 1844224 | tf_op jit(solution)/shard_map/dot_general | solution.py:54
  179.3 5.1 %collective-permute-start.1 = (bf16[128,3584]{1,0:T(8,128)(2,1)}, bf16[128,3584]{1,0:T(8,128)(2,1)}, u32[]{:S(2)}, u32[]{:S(2)}) collective-permute-start(bf16[128,3584]{1,0:T(8,128)(2,1)} %fusion.4), channel_id=1, source_target_pairs={{32,0},{64,32},{96,64},{128,96},{160,128},{192,160},{224,192},{0,2... | collective-permute-start | bytes 2752520 | tf_op jit(solution)/shard_map/ppermute | solution.py:15
  184.4 35.4 %all-to-all-done.1 = bf16[32,8,3584]{2,1,0:T(8,128)(2,1)} async-done(((bf16[32,8,3584]{2,1,0:T(8,128)(2,1)}), bf16[32,8,3584]{2,1,0:T(8,128)(2,1)}, u32[]{:S(2)}, u32[]{:S(2)}) %all-to-all-start.1) | async-done | bytes 1835040 | tf_op jit(solution)/shard_map/all_to_all | solution.py:76
  219.8 1.9 convert_reduce_fusion.1
  221.7 1.6 fusion.3
  223.3 3.0 %collective-permute-start = (bf16[128,3584]{1,0:T(8,128)(2,1)S(1)}, bf16[128,3584]{1,0:T(8,128)(2,1)S(1)}, u32[]{:S(2)}, u32[]{:S(2)}) collective-permute-start(bf16[128,3584]{1,0:T(8,128)(2,1)S(1)} %fusion.3), channel_id=1, source_target_pairs={{224,0},{0,32},{32,64},{64,96},{96,128},{128,160},{160,192},{192,2... | collective-permute-start | bytes 2752520 | tf_op jit(solution)/shard_map/ppermute | solution.py:15
  226.3 0.0 collective-permute-done.1
  226.3 22.3 %collective-permute-done = bf16[128,3584]{1,0:T(8,128)(2,1)S(1)} collective-permute-done((bf16[128,3584]{1,0:T(8,128)(2,1)S(1)}, bf16[128,3584]{1,0:T(8,128)(2,1)S(1)}, u32[]{:S(2)}, u32[]{:S(2)}) %collective-permute-start) | collective-permute-done | bytes 917536 | tf_op jit(solution)/shard_map/ppermute | solution.py:15
  248.7 0.9 copy.16
  249.6 2.2 copy.17
  (7 shorter events, 0.1 us)
Async XLA Ops:
  0.6 64.9 %copy-start = (bf16[1,3584,384]{2,1,0:T(8,128)(2,1)S(1)}, bf16[1,3584,384]{2,1,0:T(8,128)(2,1)}, u32[]{:S(2)}) copy-start(bf16[1,3584,384]{2,1,0:T(8,128)(2,1)} %param.11) | copy-start | bytes 8257540
  4.8 54.8 %all-to-all-start = ((bf16[32,8,3584]{2,1,0:T(8,128)(2,1)}), bf16[32,8,3584]{2,1,0:T(8,128)(2,1)}, u32[]{:S(2)}, u32[]{:S(2)}) async-start(bf16[32,8,3584]{2,1,0:T(8,128)(2,1)} %bitcast.62), calls=%async_computation | async-start | bytes 3670016 | tf_op jit(solution)/shard_map/all_to_all | solution.py:58
  61.0 49.6 %all-to-all-start.2 = ((bf16[32,8,3584]{2,1,0:T(8,128)(2,1)}), bf16[32,8,3584]{2,1,0:T(8,128)(2,1)}, u32[]{:S(2)}, u32[]{:S(2)}) async-start(bf16[32,8,3584]{2,1,0:T(8,128)(2,1)} %bitcast.61), calls=%async_computation.2 | async-start | bytes 3670016 | tf_op jit(solution)/shard_map/all_to_all | solution.py:59
  65.5 2.8 %copy-start.1 = (bf16[1,3584,384]{2,1,0:T(8,128)(2,1)S(1)}, bf16[1,3584,384]{2,1,0:T(8,128)(2,1)}, u32[]{:S(2)}) copy-start(bf16[1,3584,384]{2,1,0:T(8,128)(2,1)} %param.12) | copy-start | bytes 8257540
  114.0 1.8 copy-start.2
  118.2 50.8 %all-to-all-start.3 = ((bf16[32,8,3584]{2,1,0:T(8,128)(2,1)}), bf16[32,8,3584]{2,1,0:T(8,128)(2,1)}, u32[]{:S(2)}, u32[]{:S(2)}) async-start(bf16[32,8,3584]{2,1,0:T(8,128)(2,1)} %fusion.2), calls=%async_computation.3 | async-start | bytes 3670016 | tf_op jit(solution)/shard_map/all_to_all | solution.py:77
  128.1 46.6 %copy-start.4 = (f32[128,8]{0,1:T(8,128)S(1)}, f32[128,8]{0,1:T(8,128)}, u32[]{:S(2)}) copy-start(f32[128,8]{0,1:T(8,128)} %param.10) | copy-start | bytes 12292
  128.1 46.7 %copy-start.3 = (s32[128,8]{0,1:T(8,128)S(1)}, s32[128,8]{0,1:T(8,128)}, u32[]{:S(2)}) copy-start(s32[128,8]{0,1:T(8,128)} %param.9) | copy-start | bytes 12292
  169.0 50.8 %all-to-all-start.1 = ((bf16[32,8,3584]{2,1,0:T(8,128)(2,1)}), bf16[32,8,3584]{2,1,0:T(8,128)(2,1)}, u32[]{:S(2)}, u32[]{:S(2)}) async-start(bf16[32,8,3584]{2,1,0:T(8,128)(2,1)} %fusion.1), calls=%async_computation.1 | async-start | bytes 3670016 | tf_op jit(solution)/shard_map/all_to_all | solution.py:76
  179.3 47.0 %collective-permute-start.1 = (bf16[128,3584]{1,0:T(8,128)(2,1)}, bf16[128,3584]{1,0:T(8,128)(2,1)}, u32[]{:S(2)}, u32[]{:S(2)}) collective-permute-start(bf16[128,3584]{1,0:T(8,128)(2,1)} %fusion.4), channel_id=1, source_target_pairs={{32,0},{64,32},{96,64},{128,96},{160,128},{192,160},{224,192},{0,2... | collective-permute-start | bytes 2752520 | tf_op jit(solution)/shard_map/ppermute | solution.py:15
  223.3 25.4 %collective-permute-start = (bf16[128,3584]{1,0:T(8,128)(2,1)S(1)}, bf16[128,3584]{1,0:T(8,128)(2,1)S(1)}, u32[]{:S(2)}, u32[]{:S(2)}) collective-permute-start(bf16[128,3584]{1,0:T(8,128)(2,1)S(1)} %fusion.3), channel_id=1, source_target_pairs={{224,0},{0,32},{32,64},{64,96},{96,128},{128,160},{160,192},{192,2... | collective-permute-start | bytes 2752520 | tf_op jit(solution)/shard_map/ppermute | solution.py:15
where the time goes:
time: 255 us; the launch traced here: 252 us
  waiting for transfers between devices  182 us (71%)
  starting transfers between devices  33.9 us (13%)
  matrix products  23.8 us (9%)
  local copies, waits for them, and re-layouts  6.67 us (3%)
  other arithmetic  4.84 us (2%)
    all_to_all x1, waiting for transfers between devices, shards(): lax.all_to_all(send_x, 'ep', split_axis=0, concat_axis=0, tiled=True)  43.4 us
    all_to_all x1, waiting for transfers between devices, shards(): lax.all_to_all(grad_in, 'ep', split_axis=0, concat_axis=0, tiled=True)  40.9 us
    all_to_all x1, waiting for transfers between devices, shards(): lax.all_to_all(send_g, 'ep', split_axis=0, concat_axis=0, tiled=True)  39.6 us
    all_to_all x1, waiting for transfers between devices, shards(): lax.all_to_all(expert_out, 'ep', split_axis=0, concat_axis=0, tiled=True)  35.4 us
    ppermute x2, waiting for transfers between devices, shifted(): return lax.ppermute(block, axis, route)  22.3 us
    all_to_all x1, starting transfers between devices, shards(): lax.all_to_all(send_x, 'ep', split_axis=0, concat_axis=0, tiled=True)  9.79 us
    ppermute x2, starting transfers between devices, shifted(): return lax.ppermute(block, axis, route)  8.1 us
    all_to_all x1, starting transfers between devices, shards(): lax.all_to_all(expert_out, 'ep', split_axis=0, concat_axis=0, tiled=True)  5.75 us
  transfers between devices with their start and end apart: 6, of which 5 were waited for; matrix products, arithmetic and copies ran while one was open for 8% of the time, Pallas kernels for 0%

commit v1 on v0

v1 whole, which is shorter than its diff:
```python
import jax
import jax.numpy as jnp
from jax import lax
from jax.sharding import PartitionSpec as P

ROUTE_SCALE = 2.5
N_X, N_YH, N_Z, N_Y, N_C = 4, 2, 8, 2, 2
N_EP = N_Z * N_Y * N_C
AXES = ("pipe", "ep")
SLOTS = 8


def permutation(target):
    pairs = []
    for s in range(N_X * N_YH):
        for i in range(N_EP):
            z, y, c = i // 4, (i // 2) % 2, i % 2
            s2, z2, y2, c2 = target(s, z, y, c)
            pairs.append((s * N_EP + i, (s2 % 8) * N_EP + (z2 % N_Z) * 4 + y2 * 2 + c2))
    return pairs


TO_Y = permutation(lambda s, z, y, c: (s, z, 1 - y, c))
TO_CORE = permutation(lambda s, z, y, c: (s, z, y, 1 - c))
NEXT_FLIP = permutation(lambda s, z, y, c: (s + 1, z, 1 - y, c))
PREV_FLIP = permutation(lambda s, z, y, c: (s - 1, z, 1 - y, c))
NEXT = permutation(lambda s, z, y, c: (s + 1, z, y, c))
PREV = permutation(lambda s, z, y, c: (s - 1, z, y, c))
Z_GROUPS = [[z * 4 + q for z in range(N_Z)] for q in range(4)]


def over_z(values):
    return lax.all_to_all(values, "ep", 0, 0, axis_index_groups=Z_GROUPS, tiled=True)


def gather_quad(own):
    both = jnp.concatenate([own, lax.ppermute(own, AXES, TO_Y)], axis=0)
    return jnp.concatenate([both, lax.ppermute(both, AXES, TO_CORE)], axis=0)


def scatter_quad(parts, flip):
    width = parts.shape[-1]
    half = parts.shape[0] // 2
    got = lax.ppermute(parts[half:].astype(jnp.bfloat16), AXES, TO_CORE)
    chip = parts[:half] + got.astype(jnp.float32)
    quarter = half // 2
    got = lax.ppermute(chip[:quarter].astype(jnp.bfloat16), AXES, TO_Y)
    done = (chip[quarter:] + got.astype(jnp.float32)).astype(jnp.bfloat16)
    moved = lax.ppermute(done, AXES, flip)
    return over_z(moved.reshape(N_Z, SLOTS, width)).reshape(N_Z * SLOTS, width)


def mix(combine, values):
    hi = combine.astype(jnp.bfloat16)
    rest = combine - hi.astype(jnp.float32)
    mid = rest.astype(jnp.bfloat16)
    low = (rest - mid.astype(jnp.float32)).astype(jnp.bfloat16)
    lhs = jnp.concatenate([hi, mid, low], axis=1)
    rhs = jnp.concatenate([values, values, values], axis=0)
    return jnp.dot(lhs, rhs, preferred_element_type=jnp.float32).astype(jnp.bfloat16)


def shards(acts, cotan, routes, scores, w_gate, w_up, w_down):
    tok_rows, width = acts.shape
    gate_mat, up_mat, down_mat = w_gate[0], w_up[0], w_down[0]
    norm_w = scores / jnp.sum(scores, axis=1, keepdims=True) * ROUTE_SCALE
    match = routes[:, :, None] == jnp.arange(N_Z, dtype=jnp.int32)
    member = jnp.sum(match.astype(jnp.int32), axis=1)
    weight_te = jnp.sum(jnp.where(match, norm_w[:, :, None], 0.0), axis=1)
    slot_of = jnp.cumsum(member, axis=0) - member
    placed = (member[:, :, None] == 1) & (slot_of[:, :, None] == jnp.arange(SLOTS, dtype=jnp.int32))
    dispatch = placed.reshape(tok_rows, N_Z * SLOTS).T.astype(jnp.bfloat16)
    combine = (placed.astype(jnp.float32) * weight_te[:, :, None]).reshape(tok_rows, N_Z * SLOTS)

    def pack(values):
        rows = jnp.dot(dispatch, values, preferred_element_type=jnp.float32).astype(jnp.bfloat16)
        return rows.reshape(N_Z, SLOTS, width)

    x_own = over_z(pack(acts)).reshape(N_Z * SLOTS, width)
    g_own = over_z(pack(cotan)).reshape(N_Z * SLOTS, width)
    combine_next = lax.ppermute(combine, AXES, NEXT)
    combine_prev = lax.ppermute(combine, AXES, PREV)
    x = gather_quad(x_own)
    gate_val = jnp.dot(x, gate_mat, preferred_element_type=jnp.float32)
    up_val = jnp.dot(x, up_mat, preferred_element_type=jnp.float32)
    sig_val = jax.nn.sigmoid(gate_val)
    hidden = (gate_val * sig_val * up_val).astype(jnp.bfloat16)
    expert_out = jnp.dot(hidden, down_mat, preferred_element_type=jnp.float32)
    out_rows = scatter_quad(expert_out, NEXT_FLIP)
    g = gather_quad(g_own)
    contract = (((1,), (1,)), ((), ()))
    d_hidden = lax.dot_general(g, down_mat, contract, preferred_element_type=jnp.float32)
    d_gate = (d_hidden * up_val * sig_val * (1.0 + gate_val * (1.0 - sig_val))).astype(jnp.bfloat16)
    d_up = (d_hidden * gate_val * sig_val).astype(jnp.bfloat16)
    grad_in = lax.dot_general(d_gate, gate_mat, contract, preferred_element_type=jnp.float32)
    grad_in = grad_in + lax.dot_general(d_up, up_mat, contract, preferred_element_type=jnp.float32)
    grad_rows = scatter_quad(grad_in, PREV_FLIP)
    return mix(combine_next, out_rows), mix(combine_prev, grad_rows)


def solution(mesh):
    rows = P(AXES, None)
    in_specs = (rows, rows, rows, rows, P("pipe", None, "ep"), P("pipe", None, "ep"), P("pipe", "ep", None))
    return jax.shard_map(shards, mesh=mesh, in_specs=in_specs, out_specs=(rows, rows), check_vma=False)
```

time: 255 us -> 147 us (0.58)
  waiting for transfers between devices: 182 us -> 72 us
  starting transfers between devices: 33.9 us -> 45.3 us
  matrix products: 23.8 us -> 18.8 us
  local copies, waits for them, and re-layouts: 6.67 us -> 3.34 us
    all_to_all x4, waiting for transfers between devices: 159 us -> 27.3 us  [over_z(): lax.all_to_all(values, 'ep', 0, 0, axis_index_groups=Z_GROUPS, tiled=True)]
    ppermute x2 -> x12, waiting for transfers between devices: 22.3 us -> 44.7 us  [the longest x2 19.7 us: scatter_quad(): moved = lax.ppermute(done, AXES, flip)]
    ppermute x2 -> x12, starting transfers between devices: 8.1 us -> 17 us  [the longest x2 7.71 us: scatter_quad(): moved = lax.ppermute(done, AXES, flip)]
    dot_general x8, matrix products: 20.3 us -> 16.5 us  [the longest x2 4.59 us: pack(): jnp.dot(dispatch, values, preferred_element_type=jnp.float32)]
    reduce_sum x2 -> x0, other arithmetic: 3.77 us -> none  [unpack_rows(): returned.reshape(groups, SHARDS, capacity, width).astype(jnp.float32)]
    broadcast_in_dim x2 -> x0, local copies, waits for them, and re-layouts: 2.75 us -> none  [pack_rows(): return jnp.repeat(buffer.reshape(groups, capacity, width), SHARDS, axis=0)]
  transfers between devices with their start and end apart: 6 -> 16, of which waited for: 5 -> 10; matrix products, arithmetic and copies ran while one was open for 8% -> 11% of each run, Pallas kernels for 0% -> 0%
where the time goes in v1:
time: 147 us; the launch traced here: 146 us
  waiting for transfers between devices  72 us (49%)
  starting transfers between devices  45.3 us (31%)
  matrix products  18.8 us (13%)
  other arithmetic  5.76 us (4%)
  local copies, waits for them, and re-layouts  3.34 us (2%)
    all_to_all x4, starting transfers between devices, over_z(): lax.all_to_all(values, 'ep', 0, 0, axis_index_groups=Z_GROUPS, tiled=True)  28.3 us
    all_to_all x4, waiting for transfers between devices, over_z(): lax.all_to_all(values, 'ep', 0, 0, axis_index_groups=Z_GROUPS, tiled=True)  27.3 us
    ppermute x2, waiting for transfers between devices, scatter_quad(): moved = lax.ppermute(done, AXES, flip)  19.7 us
    ppermute x2, waiting for transfers between devices, scatter_quad(): got = lax.ppermute(chip[:quarter].astype(jnp.bfloat16), AXES, TO_Y)  9.8 us
    ppermute x2, waiting for transfers between devices, gather_quad(): both = jnp.concatenate([own, lax.ppermute(own, AXES, TO_Y)], axis=0)  8.34 us
    ppermute x2, starting transfers between devices, scatter_quad(): moved = lax.ppermute(done, AXES, flip)  7.71 us
    dot_general x2, matrix products, pack(): jnp.dot(dispatch, values, preferred_element_type=jnp.float32)  4.59 us
    dot_general x2, matrix products, mix(): jnp.dot(lhs, rhs, preferred_element_type=jnp.float32).astype(jnp.bfloat16)  4.01 us
  transfers between devices with their start and end apart: 16, of which 10 were waited for; matrix products, arithmetic and copies ran while one was open for 11% of the time, Pallas kernels for 0%

profile of v1, /device:TPU:32, one launch (start us, length us, event | category | flops | bytes accessed | tf_op | source)
XLA Modules:
  0.0 146.0 jit_solution(17723938613862864669)
XLA Ops:
  0.6 0.0 copy-start
  0.6 0.9 convert_reduce_fusion
  1.5 0.1 copy.15
  1.6 0.2 reduce_window_sum.11
  1.8 0.1 eq.53
  1.9 2.3 %fusion = bf16[8,8,3584]{2,1,0:T(8,128)(2,1)} fusion(bf16[128,3584]{1,0:T(8,128)(2,1)} %param.7, s32[64]{0:T(128)S(1)} %eq.53, s32[128,8]{0,1:T(8,128)S(1)} %copy.17, pred[128,8]{0,1:T(8,128)(4,1)S(1)} %broadcast_compare_fusion), kind=kOutput, calls=%fused_computation.5 | convolution fusion | flops 58966016 | bytes 1381632 | tf_op jit(solution)/shard_map/dot_general | solution.py:76
  4.2 8.6 %all-to-all-start = ((bf16[8,8,3584]{2,1,0:T(8,128)(2,1)}), bf16[8,8,3584]{2,1,0:T(8,128)(2,1)S(1)}, u32[]{:S(2)}, u32[]{:S(2)}) async-start(bf16[8,8,3584]{2,1,0:T(8,128)(2,1)} %fusion), calls=%async_computation | async-start | bytes 917504 | tf_op jit(solution)/shard_map/all_to_all | solution.py:33
  12.8 2.3 %fusion.1 = bf16[8,8,3584]{2,1,0:T(8,128)(2,1)} fusion(bf16[128,3584]{1,0:T(8,128)(2,1)} %param.8, s32[64]{0:T(128)S(1)} %eq.53, s32[128,8]{0,1:T(8,128)S(1)} %copy.17, pred[128,8]{0,1:T(8,128)(4,1)S(1)} %broadcast_compare_fusion), kind=kOutput, calls=%fused_computation.6 | convolution fusion | flops 58966016 | bytes 1381632 | tf_op jit(solution)/shard_map/dot_general | solution.py:76
  15.1 12.4 %all-to-all-done = bf16[8,8,3584]{2,1,0:T(8,128)(2,1)S(1)} async-done(((bf16[8,8,3584]{2,1,0:T(8,128)(2,1)}), bf16[8,8,3584]{2,1,0:T(8,128)(2,1)S(1)}, u32[]{:S(2)}, u32[]{:S(2)}) %all-to-all-start) | async-done | bytes 458784 | tf_op jit(solution)/shard_map/all_to_all | solution.py:33
  27.4 5.5 %all-to-all-start.2 = ((bf16[8,8,3584]{2,1,0:T(8,128)(2,1)}), bf16[8,8,3584]{2,1,0:T(8,128)(2,1)}, u32[]{:S(2)}, u32[]{:S(2)}) async-start(bf16[8,8,3584]{2,1,0:T(8,128)(2,1)} %fusion.1), calls=%async_computation.2 | async-start | bytes 917504 | tf_op jit(solution)/shard_map/all_to_all | solution.py:33
  32.9 1.6 %collective-permute-start.1 = (bf16[64,3584]{1,0:T(8,128)(2,1)S(1)}, bf16[64,3584]{1,0:T(8,128)(2,1)}, u32[]{:S(2)}, u32[]{:S(2)}) collective-permute-start(bf16[64,3584]{1,0:T(8,128)(2,1)S(1)} %bitcast.43), channel_id=1, source_target_pairs={{0,2},{1,3},{2,0},{3,1},{4,6},{5,7},{6,4},{7,5},{8,10},{9,11},{10,... | collective-permute-start | bytes 1376264 | tf_op jit(solution)/shard_map/ppermute | solution.py:37
  34.5 13.6 %all-to-all-done.2 = bf16[8,8,3584]{2,1,0:T(8,128)(2,1)} async-done(((bf16[8,8,3584]{2,1,0:T(8,128)(2,1)}), bf16[8,8,3584]{2,1,0:T(8,128)(2,1)}, u32[]{:S(2)}, u32[]{:S(2)}) %all-to-all-start.2) | async-done | bytes 458784 | tf_op jit(solution)/shard_map/all_to_all | solution.py:33
  48.0 1.6 %collective-permute-start.7 = (bf16[64,3584]{1,0:T(8,128)(2,1)}, bf16[64,3584]{1,0:T(8,128)(2,1)S(1)}, u32[]{:S(2)}, u32[]{:S(2)}) collective-permute-start(bf16[64,3584]{1,0:T(8,128)(2,1)} %bitcast.11), channel_id=1, source_target_pairs={{0,2},{1,3},{2,0},{3,1},{4,6},{5,7},{6,4},{7,5},{8,10},{9,11},{10,... | collective-permute-start | bytes 1376264 | tf_op jit(solution)/shard_map/ppermute | solution.py:37
  49.6 0.0 collective-permute-done.1
  49.6 1.1 pad_maximum_fusion.1
  50.7 0.1 collective-permute-start.2
  50.8 8.3 %collective-permute-done.7 = bf16[64,3584]{1,0:T(8,128)(2,1)S(1)} collective-permute-done((bf16[64,3584]{1,0:T(8,128)(2,1)}, bf16[64,3584]{1,0:T(8,128)(2,1)S(1)}, u32[]{:S(2)}, u32[]{:S(2)}) %collective-permute-start.7) | collective-permute-done | bytes 458784 | tf_op jit(solution)/shard_map/ppermute | solution.py:37
  59.1 1.1 pad_maximum_fusion.2
  60.2 0.0 copy-start.3
  60.2 0.1 collective-permute-start.8
  60.3 0.0 collective-permute-done.2
  60.3 0.0 copy-done
  60.3 2.3 %fusion.11 = f32[256,384]{1,0:T(8,128)S(1)} fusion(bf16[1,3584,384]{2,1,0:T(8,128)(2,1)S(1)} %copy-done, bf16[128,3584]{1,0:T(8,128)(2,1)S(1)} %collective-permute-done.2, bf16[64,3584]{1,0:T(8,128)(2,1)} %collective-permute-done.1, bf16[64,3584]{1,0:T(8,128)(2,1)S(1)} %bitcast.45), kind=kOutput, calls=%fused_computation.16 | convolution fusion | flops 710148096 | bytes 4980736 | tf_op jit(solution)/shard_map/dot_general | solution.py:84
  62.6 0.0 copy-done.3
  62.7 0.0 copy-start.2
  62.7 2.3 %fusion.7 = f32[256,384]{1,0:T(8,128)S(1)} fusion(bf16[1,3584,384]{2,1,0:T(8,128)(2,1)S(1)} %copy-done.3, bf16[128,3584]{1,0:T(8,128)(2,1)S(1)} %collective-permute-done.2, bf16[64,3584]{1,0:T(8,128)(2,1)} %collective-permute-done.1, bf16[64,3584]{1,0:T(8,128)(2,1)S(1)} %bitcast.46), kind=kOutput, calls=%fused_computation.12 | convolution fusion | flops 710148096 | bytes 4980736 | tf_op jit(solution)/shard_map/dot_general | solution.py:85
  65.0 0.0 collective-permute-done.8
  65.0 0.0 copy-done.2
  65.0 2.1 %fusion.2 = f32[256,384]{1,0:T(8,128)S(1)} fusion(bf16[1,384,3584]{2,1,0:T(8,128)(2,1)S(1)} %copy-done.2, bf16[128,3584]{1,0:T(8,128)(2,1)S(1)} %collective-permute-done.8, bf16[64,3584]{1,0:T(8,128)(2,1)S(1)} %collective-permute-done.7, bf16[64,3584]{1,0:T(8,128)(2,1)} %bitcast.11), kind=kOutput, calls=%fused_computation.7 | convolution fusion | flops 710148096 | bytes 4980736 | tf_op jit(solution)/shard_map/dot_general | solution.py:92
  67.1 1.2 fusion.9
  68.3 1.2 convolution_add_fusion
  69.5 0.1 slice.56
  69.6 0.4 collective-permute-start.9
  70.0 2.1 %collective-permute-done.9 = bf16[128,3584]{1,0:T(8,128)(2,1)S(1)} collective-permute-done((bf16[128,3584]{1,0:T(8,128)(2,1)S(1)}, bf16[128,3584]{1,0:T(8,128)(2,1)S(1)}, u32[]{:S(2)}, u32[]{:S(2)}) %collective-permute-start.9) | collective-permute-done | bytes 917536 | tf_op jit(solution)/shard_map/ppermute | solution.py:44
  72.2 0.2 slice_add_fusion
  72.4 1.7 %collective-permute-start.10 = (bf16[64,3584]{1,0:T(8,128)(2,1)S(1)}, bf16[64,3584]{1,0:T(8,128)(2,1)S(1)}, u32[]{:S(2)}, u32[]{:S(2)}) collective-permute-start(bf16[64,3584]{1,0:T(8,128)(2,1)S(1)} %slice.58), channel_id=1, source_target_pairs={{0,2},{1,3},{2,0},{3,1},{4,6},{5,7},{6,4},{7,5},{8,10},{9,11},{10,... | collective-permute-start | bytes 1376264 | tf_op jit(solution)/shard_map/ppermute | solution.py:47
  74.1 1.1 fusion.4
  75.2 0.1 slice.57
  75.3 0.1 collective-permute-start.3
  75.4 9.8 %collective-permute-done.10 = bf16[64,3584]{1,0:T(8,128)(2,1)S(1)} collective-permute-done((bf16[64,3584]{1,0:T(8,128)(2,1)S(1)}, bf16[64,3584]{1,0:T(8,128)(2,1)S(1)}, u32[]{:S(2)}, u32[]{:S(2)}) %collective-permute-start.10) | collective-permute-done | bytes 458784 | tf_op jit(solution)/shard_map/ppermute | solution.py:47
  85.2 0.1 fusion.28
  85.3 5.3 %collective-permute-start.11 = (bf16[64,3584]{1,0:T(8,128)(2,1)S(1)}, bf16[64,3584]{1,0:T(8,128)(2,1)S(1)}, u32[]{:S(2)}, u32[]{:S(2)}) collective-permute-start(bf16[64,3584]{1,0:T(8,128)(2,1)S(1)} %fusion.28), channel_id=1, source_target_pairs={{0,226},{1,227},{2,224},{3,225},{4,230},{5,231},{6,228},{7,229},{8... | collective-permute-start | bytes 1376264 | tf_op jit(solution)/shard_map/ppermute | solution.py:49
  90.6 0.0 collective-permute-done.3
  90.6 0.2 slice_add_fusion.1
  90.8 1.3 copy-done.1
  92.0 0.8 slice.59
  92.9 0.1 collective-permute-start.4
  93.0 7.1 %collective-permute-done.11 = bf16[64,3584]{1,0:T(8,128)(2,1)S(1)} collective-permute-done((bf16[64,3584]{1,0:T(8,128)(2,1)S(1)}, bf16[64,3584]{1,0:T(8,128)(2,1)S(1)}, u32[]{:S(2)}, u32[]{:S(2)}) %collective-permute-start.11) | collective-permute-done | bytes 458784 | tf_op jit(solution)/shard_map/ppermute | solution.py:49
  100.1 0.8 copy-done.4
  100.8 7.0 %all-to-all-start.3 = ((bf16[8,8,3584]{2,1,0:T(8,128)(2,1)}), bf16[8,8,3584]{2,1,0:T(8,128)(2,1)}, u32[]{:S(2)}, u32[]{:S(2)}) async-start(bf16[8,8,3584]{2,1,0:T(8,128)(2,1)} %bitcast.48), calls=%async_computation.3 | async-start | bytes 917504 | tf_op jit(solution)/shard_map/all_to_all | solution.py:33
  107.8 0.0 collective-permute-done.4
  107.8 2.0 %fusion.29 = bf16[64,3584]{1,0:T(8,128)(2,1)} fusion(f32[128,3584]{1,0:T(8,128)} %copy-done.1, bf16[64,3584]{1,0:T(8,128)(2,1)S(1)} %collective-permute-done.4), kind=kLoop, calls=%fused_computation.43 | loop fusion | flops 688128 | bytes 1835008 | tf_op jit(solution)/shard_map/convert_element_type | solution.py:48
  109.9 2.4 %collective-permute-start.5 = (bf16[64,3584]{1,0:T(8,128)(2,1)}, bf16[64,3584]{1,0:T(8,128)(2,1)}, u32[]{:S(2)}, u32[]{:S(2)}) collective-permute-start(bf16[64,3584]{1,0:T(8,128)(2,1)} %fusion.29), channel_id=1, source_target_pairs={{0,34},{1,35},{2,32},{3,33},{4,38},{5,39},{6,36},{7,37},{8,42},{9,... | collective-permute-start | bytes 1376264 | tf_op jit(solution)/shard_map/ppermute | solution.py:49
  112.3 12.6 %collective-permute-done.5 = bf16[64,3584]{1,0:T(8,128)(2,1)} collective-permute-done((bf16[64,3584]{1,0:T(8,128)(2,1)}, bf16[64,3584]{1,0:T(8,128)(2,1)}, u32[]{:S(2)}, u32[]{:S(2)}) %collective-permute-start.5) | collective-permute-done | bytes 458784 | tf_op jit(solution)/shard_map/ppermute | solution.py:49
  125.0 0.0 all-to-all-done.3
  125.0 7.2 %all-to-all-start.1 = ((bf16[8,8,3584]{2,1,0:T(8,128)(2,1)}), bf16[8,8,3584]{2,1,0:T(8,128)(2,1)S(1)}, u32[]{:S(2)}, u32[]{:S(2)}) async-start(bf16[8,8,3584]{2,1,0:T(8,128)(2,1)} %bitcast.8), calls=%async_computation.1 | async-start | bytes 917504 | tf_op jit(solution)/shard_map/all_to_all | solution.py:33
  132.2 0.1 bitcast_select_fusion
  132.3 0.8 collective-permute-start.6
  133.1 2.8 %collective-permute-start = (f32[128,64]{0,1:T(8,128)S(1)}, f32[128,64]{0,1:T(8,128)S(1)}, u32[]{:S(2)}, u32[]{:S(2)}) collective-permute-start(f32[128,64]{0,1:T(8,128)S(1)} %bitcast_select_fusion), channel_id=1, source_target_pairs={{0,32},{1,33},{2,34},{3,35},{4,36},{5,37},{6,38},{7,39},{8,40},{9,... | collective-permute-start | bytes 98312 | tf_op jit(solution)/shard_map/ppermute | solution.py:81
  135.9 1.9 %collective-permute-done.6 = f32[128,64]{0,1:T(8,128)S(1)} collective-permute-done((f32[128,64]{0,1:T(8,128)S(1)}, f32[128,64]{0,1:T(8,128)S(1)}, u32[]{:S(2)}, u32[]{:S(2)}) %collective-permute-start.6) | collective-permute-done | bytes 32800 | tf_op jit(solution)/shard_map/ppermute | solution.py:82
  137.8 2.8 %collective-permute-done = f32[128,64]{0,1:T(8,128)S(1)} collective-permute-done((f32[128,64]{0,1:T(8,128)S(1)}, f32[128,64]{0,1:T(8,128)S(1)}, u32[]{:S(2)}, u32[]{:S(2)}) %collective-permute-start) | collective-permute-done | bytes 32800 | tf_op jit(solution)/shard_map/ppermute | solution.py:81
  140.6 2.7 %convolution_convert_fusion = bf16[128,3584]{1,0:T(8,128)(2,1)} fusion(bf16[64,3584]{1,0:T(8,128)(2,1)} %bitcast.13, bf16[128,64]{0,1:T(8,128)(2,1)S(1)} %get-tuple-element.3, bf16[128,64]{0,1:T(8,128)(2,1)S(1)} %get-tuple-element.4, bf16[128,64]{0,1:T(8,128)(2,1)S(1)} %get-tuple-element.2), kind=kOutput, calls=%fused_computation.1 | convolution fusion | flops 180895744 | bytes 1425408 | tf_op jit(solution)/shard_map/dot_general | solution.py:60
  143.3 1.4 all-to-all-done.1
  144.7 1.3 convolution_convert_fusion.1
  (16 shorter events, 0.2 us)
Async XLA Ops:
  0.6 59.7 %copy-start = (bf16[1,3584,384]{2,1,0:T(8,128)(2,1)S(1)}, bf16[1,3584,384]{2,1,0:T(8,128)(2,1)}, u32[]{:S(2)}) copy-start(bf16[1,3584,384]{2,1,0:T(8,128)(2,1)} %param.11) | copy-start | bytes 8257540
  4.2 23.2 %all-to-all-start = ((bf16[8,8,3584]{2,1,0:T(8,128)(2,1)}), bf16[8,8,3584]{2,1,0:T(8,128)(2,1)S(1)}, u32[]{:S(2)}, u32[]{:S(2)}) async-start(bf16[8,8,3584]{2,1,0:T(8,128)(2,1)} %fusion), calls=%async_computation | async-start | bytes 917504 | tf_op jit(solution)/shard_map/all_to_all | solution.py:33
  27.4 20.6 %all-to-all-start.2 = ((bf16[8,8,3584]{2,1,0:T(8,128)(2,1)}), bf16[8,8,3584]{2,1,0:T(8,128)(2,1)}, u32[]{:S(2)}, u32[]{:S(2)}) async-start(bf16[8,8,3584]{2,1,0:T(8,128)(2,1)} %fusion.1), calls=%async_computation.2 | async-start | bytes 917504 | tf_op jit(solution)/shard_map/all_to_all | solution.py:33
  32.9 16.7 %collective-permute-start.1 = (bf16[64,3584]{1,0:T(8,128)(2,1)S(1)}, bf16[64,3584]{1,0:T(8,128)(2,1)}, u32[]{:S(2)}, u32[]{:S(2)}) collective-permute-start(bf16[64,3584]{1,0:T(8,128)(2,1)S(1)} %bitcast.43), channel_id=1, source_target_pairs={{0,2},{1,3},{2,0},{3,1},{4,6},{5,7},{6,4},{7,5},{8,10},{9,11},{10,... | collective-permute-start | bytes 1376264 | tf_op jit(solution)/shard_map/ppermute | solution.py:37
  48.0 11.1 %collective-permute-start.7 = (bf16[64,3584]{1,0:T(8,128)(2,1)}, bf16[64,3584]{1,0:T(8,128)(2,1)S(1)}, u32[]{:S(2)}, u32[]{:S(2)}) collective-permute-start(bf16[64,3584]{1,0:T(8,128)(2,1)} %bitcast.11), channel_id=1, source_target_pairs={{0,2},{1,3},{2,0},{3,1},{4,6},{5,7},{6,4},{7,5},{8,10},{9,11},{10,... | collective-permute-start | bytes 1376264 | tf_op jit(solution)/shard_map/ppermute | solution.py:37
  50.7 9.6 %collective-permute-start.2 = (bf16[128,3584]{1,0:T(8,128)(2,1)S(1)}, bf16[128,3584]{1,0:T(8,128)(2,1)S(1)}, u32[]{:S(2)}, u32[]{:S(2)}) collective-permute-start(bf16[128,3584]{1,0:T(8,128)(2,1)S(1)} %pad_maximum_fusion.1), channel_id=1, source_target_pairs={{0,1},{1,0},{2,3},{3,2},{4,5},{5,4},{6,7},{7,6},{8,9},{9,8},{10,11... | collective-permute-start | bytes 2752520 | tf_op jit(solution)/shard_map/ppermute | solution.py:38
  60.2 2.4 %copy-start.3 = (bf16[1,3584,384]{2,1,0:T(8,128)(2,1)S(1)}, bf16[1,3584,384]{2,1,0:T(8,128)(2,1)}, u32[]{:S(2)}) copy-start(bf16[1,3584,384]{2,1,0:T(8,128)(2,1)} %param.12) | copy-start | bytes 8257540
  60.2 4.8 %collective-permute-start.8 = (bf16[128,3584]{1,0:T(8,128)(2,1)S(1)}, bf16[128,3584]{1,0:T(8,128)(2,1)S(1)}, u32[]{:S(2)}, u32[]{:S(2)}) collective-permute-start(bf16[128,3584]{1,0:T(8,128)(2,1)S(1)} %pad_maximum_fusion.2), channel_id=1, source_target_pairs={{0,1},{1,0},{2,3},{3,2},{4,5},{5,4},{6,7},{7,6},{8,9},{9,8},{10,11... | collective-permute-start | bytes 2752520 | tf_op jit(solution)/shard_map/ppermute | solution.py:38
  62.7 2.3 %copy-start.2 = (bf16[1,384,3584]{2,1,0:T(8,128)(2,1)S(1)}, bf16[1,384,3584]{2,1,0:T(8,128)(2,1)}, u32[]{:S(2)}) copy-start(bf16[1,384,3584]{2,1,0:T(8,128)(2,1)} %param.13) | copy-start | bytes 8257540
  69.6 2.6 %collective-permute-start.9 = (bf16[128,3584]{1,0:T(8,128)(2,1)S(1)}, bf16[128,3584]{1,0:T(8,128)(2,1)S(1)}, u32[]{:S(2)}, u32[]{:S(2)}) collective-permute-start(bf16[128,3584]{1,0:T(8,128)(2,1)S(1)} %slice.56), channel_id=1, source_target_pairs={{0,1},{1,0},{2,3},{3,2},{4,5},{5,4},{6,7},{7,6},{8,9},{9,8},{10,11... | collective-permute-start | bytes 2752520 | tf_op jit(solution)/shard_map/ppermute | solution.py:44
  72.4 12.8 %collective-permute-start.10 = (bf16[64,3584]{1,0:T(8,128)(2,1)S(1)}, bf16[64,3584]{1,0:T(8,128)(2,1)S(1)}, u32[]{:S(2)}, u32[]{:S(2)}) collective-permute-start(bf16[64,3584]{1,0:T(8,128)(2,1)S(1)} %slice.58), channel_id=1, source_target_pairs={{0,2},{1,3},{2,0},{3,1},{4,6},{5,7},{6,4},{7,5},{8,10},{9,11},{10,... | collective-permute-start | bytes 1376264 | tf_op jit(solution)/shard_map/ppermute | solution.py:47
  75.3 15.3 %collective-permute-start.3 = (bf16[128,3584]{1,0:T(8,128)(2,1)S(1)}, bf16[128,3584]{1,0:T(8,128)(2,1)S(1)}, u32[]{:S(2)}, u32[]{:S(2)}) collective-permute-start(bf16[128,3584]{1,0:T(8,128)(2,1)S(1)} %slice.57), channel_id=1, source_target_pairs={{0,1},{1,0},{2,3},{3,2},{4,5},{5,4},{6,7},{7,6},{8,9},{9,8},{10,11... | collective-permute-start | bytes 2752520 | tf_op jit(solution)/shard_map/ppermute | solution.py:44
  85.3 14.8 %collective-permute-start.11 = (bf16[64,3584]{1,0:T(8,128)(2,1)S(1)}, bf16[64,3584]{1,0:T(8,128)(2,1)S(1)}, u32[]{:S(2)}, u32[]{:S(2)}) collective-permute-start(bf16[64,3584]{1,0:T(8,128)(2,1)S(1)} %fusion.28), channel_id=1, source_target_pairs={{0,226},{1,227},{2,224},{3,225},{4,230},{5,231},{6,228},{7,229},{8... | collective-permute-start | bytes 1376264 | tf_op jit(solution)/shard_map/ppermute | solution.py:49
  90.8 1.3 copy-start.1
  92.0 20.2 %copy-start.6 = (f32[128,8]{0,1:T(8,128)S(1)}, f32[128,8]{0,1:T(8,128)}, u32[]{:S(2)}) copy-start(f32[128,8]{0,1:T(8,128)} %param.10) | copy-start | bytes 12292
  92.0 20.3 %copy-start.5 = (s32[128,8]{0,1:T(8,128)S(1)}, s32[128,8]{0,1:T(8,128)}, u32[]{:S(2)}) copy-start(s32[128,8]{0,1:T(8,128)} %param.9) | copy-start | bytes 12292
  92.9 15.0 %collective-permute-start.4 = (bf16[64,3584]{1,0:T(8,128)(2,1)}, bf16[64,3584]{1,0:T(8,128)(2,1)S(1)}, u32[]{:S(2)}, u32[]{:S(2)}) collective-permute-start(bf16[64,3584]{1,0:T(8,128)(2,1)} %slice.59), channel_id=1, source_target_pairs={{0,2},{1,3},{2,0},{3,1},{4,6},{5,7},{6,4},{7,5},{8,10},{9,11},{10,... | collective-permute-start | bytes 1376264 | tf_op jit(solution)/shard_map/ppermute | solution.py:47
  100.1 0.8 copy-start.4
  100.8 24.1 %all-to-all-start.3 = ((bf16[8,8,3584]{2,1,0:T(8,128)(2,1)}), bf16[8,8,3584]{2,1,0:T(8,128)(2,1)}, u32[]{:S(2)}, u32[]{:S(2)}) async-start(bf16[8,8,3584]{2,1,0:T(8,128)(2,1)} %bitcast.48), calls=%async_computation.3 | async-start | bytes 917504 | tf_op jit(solution)/shard_map/all_to_all | solution.py:33
  109.9 15.1 %collective-permute-start.5 = (bf16[64,3584]{1,0:T(8,128)(2,1)}, bf16[64,3584]{1,0:T(8,128)(2,1)}, u32[]{:S(2)}, u32[]{:S(2)}) collective-permute-start(bf16[64,3584]{1,0:T(8,128)(2,1)} %fusion.29), channel_id=1, source_target_pairs={{0,34},{1,35},{2,32},{3,33},{4,38},{5,39},{6,36},{7,37},{8,42},{9,... | collective-permute-start | bytes 1376264 | tf_op jit(solution)/shard_map/ppermute | solution.py:49
  125.0 19.7 %all-to-all-start.1 = ((bf16[8,8,3584]{2,1,0:T(8,128)(2,1)}), bf16[8,8,3584]{2,1,0:T(8,128)(2,1)S(1)}, u32[]{:S(2)}, u32[]{:S(2)}) async-start(bf16[8,8,3584]{2,1,0:T(8,128)(2,1)} %bitcast.8), calls=%async_computation.1 | async-start | bytes 917504 | tf_op jit(solution)/shard_map/all_to_all | solution.py:33
  132.3 5.5 %collective-permute-start.6 = (f32[128,64]{0,1:T(8,128)S(1)}, f32[128,64]{0,1:T(8,128)S(1)}, u32[]{:S(2)}, u32[]{:S(2)}) collective-permute-start(f32[128,64]{0,1:T(8,128)S(1)} %bitcast_select_fusion), channel_id=1, source_target_pairs={{0,224},{1,225},{2,226},{3,227},{4,228},{5,229},{6,230},{7,231},{8... | collective-permute-start | bytes 98312 | tf_op jit(solution)/shard_map/ppermute | solution.py:82
  133.1 7.5 %collective-permute-start = (f32[128,64]{0,1:T(8,128)S(1)}, f32[128,64]{0,1:T(8,128)S(1)}, u32[]{:S(2)}, u32[]{:S(2)}) collective-permute-start(f32[128,64]{0,1:T(8,128)S(1)} %bitcast_select_fusion), channel_id=1, source_target_pairs={{0,32},{1,33},{2,34},{3,35},{4,36},{5,37},{6,38},{7,39},{8,40},{9,... | collective-permute-start | bytes 98312 | tf_op jit(solution)/shard_map/ppermute | solution.py:81

commit v2 on v1

v2 whole, which is shorter than its diff:
```python
import jax
import jax.numpy as jnp
from jax import lax
from jax.experimental import pallas as pl
from jax.experimental.pallas import tpu as pltpu
from jax.sharding import PartitionSpec as P

ROUTE_SCALE = 2.5
N_X, N_YH, N_Z, N_Y, N_C = 4, 2, 8, 2, 2
N_EP = N_Z * N_Y * N_C
AXES = ("pipe", "ep")
SLOTS = 8
ROWS = N_Z * SLOTS


def permutation(target):
    pairs = []
    for s in range(N_X * N_YH):
        for i in range(N_EP):
            z, y, c = i // 4, (i // 2) % 2, i % 2
            s2, z2, y2, c2 = target(s, z, y, c)
            pairs.append((s * N_EP + i, (s2 % 8) * N_EP + (z2 % N_Z) * 4 + y2 * 2 + c2))
    return pairs


TO_Y = permutation(lambda s, z, y, c: (s, z, 1 - y, c))
TO_CORE = permutation(lambda s, z, y, c: (s, z, y, 1 - c))
NEXT_FLIP = permutation(lambda s, z, y, c: (s + 1, z, 1 - y, c))
PREV_FLIP = permutation(lambda s, z, y, c: (s - 1, z, 1 - y, c))
NEXT = permutation(lambda s, z, y, c: (s + 1, z, y, c))
PREV = permutation(lambda s, z, y, c: (s - 1, z, y, c))
Z_GROUPS = [[z * 4 + q for z in range(N_Z)] for q in range(4)]
K_STEPS = 4
N_STEPS = 7


def over_z(values):
    return lax.all_to_all(values, "ep", 0, 0, axis_index_groups=Z_GROUPS, tiled=True)


def dot(a, b):
    return jnp.dot(a, b, preferred_element_type=jnp.float32)


def dot_t(a, b):
    return lax.dot_general(a, b, (((1,), (1,)), ((), ())), preferred_element_type=jnp.float32)


def fill(rows_scr, pieces):
    at = 0
    for piece in pieces:
        rows_scr[pl.ds(at, piece.shape[0]), :] = piece[...]
        at += piece.shape[0]


def emit_columns(tile, send_ref, keep_ref):
    half, width = keep_ref.shape
    step = width // N_STEPS
    for n in range(N_STEPS):
        cols = pl.ds(n * step, step)
        value = tile(cols)
        keep_ref[:, cols] = value[:half]
        send_ref[:, cols] = value[half:].astype(jnp.bfloat16)


def over_width(rows_scr, mat, product):
    step = rows_scr.shape[1] // K_STEPS
    total = None
    for k in range(K_STEPS):
        part = pl.ds(k * step, step)
        add = product(rows_scr[:, part], mat(part))
        total = add if total is None else total + add
    return total


def forward_kernel(own_ref, y_ref, c_ref, gate_ref, up_ref, down_ref, send_ref, keep_ref, slope_ref, gated_ref, x_scr):
    fill(x_scr, (own_ref, y_ref, c_ref))
    gate_val = over_width(x_scr, lambda part: gate_ref[part, :], dot)
    up_val = over_width(x_scr, lambda part: up_ref[part, :], dot)
    sig_val = jax.nn.sigmoid(gate_val)
    gated = gate_val * sig_val
    gated_ref[...] = gated
    slope_ref[...] = up_val * sig_val * (1.0 + gate_val * (1.0 - sig_val))
    hidden = (gated * up_val).astype(jnp.bfloat16)
    emit_columns(lambda cols: dot(hidden, down_ref[:, cols]), send_ref, keep_ref)


def backward_kernel(own_ref, y_ref, c_ref, gate_ref, up_ref, down_ref, slope_ref, gated_ref, send_ref, keep_ref, g_scr):
    fill(g_scr, (own_ref, y_ref, c_ref))
    d_hidden = over_width(g_scr, lambda part: down_ref[:, part], dot_t)
    d_gate = (d_hidden * slope_ref[...]).astype(jnp.bfloat16)
    d_up = (d_hidden * gated_ref[...]).astype(jnp.bfloat16)
    emit_columns(lambda cols: dot_t(d_gate, gate_ref[cols, :]) + dot_t(d_up, up_ref[cols, :]), send_ref, keep_ref)


VMEM = pl.BlockSpec(memory_space=pltpu.VMEM)


def expert_call(kernel, pieces, gate_mat, up_mat, down_mat, saved, cost):
    width, hid = gate_mat.shape
    rows = sum(p.shape[0] for p in pieces)
    half = rows // 2
    out_shape = [jax.ShapeDtypeStruct((half, width), jnp.bfloat16), jax.ShapeDtypeStruct((half, width), jnp.float32)]
    if not saved:
        out_shape += [jax.ShapeDtypeStruct((rows, hid), jnp.float32)] * 2
    operands = (*pieces, *((m) for m in (gate_mat, up_mat, down_mat)), *saved)
    return pl.pallas_call(
        kernel,
        out_shape=out_shape,
        in_specs=[VMEM] * len(operands),
        out_specs=[VMEM] * len(out_shape),
        scratch_shapes=[pltpu.VMEM((rows, width), jnp.bfloat16)],
        compiler_params=pltpu.CompilerParams(vmem_limit_bytes=40 * 2**20),
        cost_estimate=pl.CostEstimate(flops=cost, bytes_accessed=12_000_000, transcendentals=0),
    )(*operands)


def mix(combine, values):
    hi = combine.astype(jnp.bfloat16)
    rest = combine - hi.astype(jnp.float32)
    mid = rest.astype(jnp.bfloat16)
    low = (rest - mid.astype(jnp.float32)).astype(jnp.bfloat16)
    lhs = jnp.concatenate([hi, mid, low], axis=1)
    rhs = jnp.concatenate([values, values, values], axis=0)
    return dot(lhs, rhs).astype(jnp.bfloat16)


def shards(acts, cotan, routes, scores, w_gate, w_up, w_down):
    tok_rows, width = acts.shape
    gate_mat, up_mat, down_mat = w_gate[0], w_up[0], w_down[0]
    norm_w = scores / jnp.sum(scores, axis=1, keepdims=True) * ROUTE_SCALE
    match = routes[:, :, None] == jnp.arange(N_Z, dtype=jnp.int32)
    member = jnp.sum(match.astype(jnp.int32), axis=1)
    weight_te = jnp.sum(jnp.where(match, norm_w[:, :, None], 0.0), axis=1)
    slot_of = jnp.cumsum(member, axis=0) - member
    placed = (member[:, :, None] == 1) & (slot_of[:, :, None] == jnp.arange(SLOTS, dtype=jnp.int32))
    dispatch = placed.reshape(tok_rows, ROWS).T.astype(jnp.bfloat16)
    combine = (placed.astype(jnp.float32) * weight_te[:, :, None]).reshape(tok_rows, ROWS)

    together = lax.optimization_barrier

    def to(values, table):
        return lax.ppermute(values, AXES, table)

    def back(values):
        return over_z(values.reshape(N_Z, SLOTS, width)).reshape(ROWS, width)

    def halves(keep, got):
        a = (keep[:ROWS] + got[:ROWS].astype(jnp.float32)).astype(jnp.bfloat16)
        return a, keep[ROWS:] + got[ROWS:].astype(jnp.float32)

    def finish(kept, got):
        return (kept + got.astype(jnp.float32)).astype(jnp.bfloat16)

    empty = jnp.zeros_like(placed)
    first = jnp.concatenate([placed, empty], axis=2).reshape(tok_rows, 2 * ROWS).T.astype(jnp.bfloat16)
    second = jnp.concatenate([empty, placed], axis=2).reshape(tok_rows, 2 * ROWS).T.astype(jnp.bfloat16)
    pair = (dot(first, acts) + dot(second, cotan)).astype(jnp.bfloat16)
    pair = over_z(pair.reshape(N_Z, 2 * SLOTS, width))
    x_own, g_own = pair[:, :SLOTS].reshape(ROWS, width), pair[:, SLOTS:].reshape(ROWS, width)
    combine_next = to(combine, NEXT)
    combine_prev = to(combine, PREV)
    x_own, g_own, combine_next, combine_prev = together((x_own, g_own, combine_next, combine_prev))
    x_y = to(x_own, TO_Y)
    x_y, x_own, g_own = together((x_y, x_own, g_own))
    x_c = to(jnp.concatenate([x_own, x_y], axis=0), TO_CORE)
    send, keep, slope, gated = expert_call(forward_kernel, (x_own, x_y, x_c), gate_mat, up_mat, down_mat, (), 20_000_000_000)
    g_y = to(g_own, TO_Y)
    send, keep, slope, gated, g_own, g_y = together((send, keep, slope, gated, g_own, g_y))
    got = to(send, TO_CORE)
    g_c = to(jnp.concatenate([g_own, g_y], axis=0), TO_CORE)
    out_a, out_b = halves(keep, got)
    out_a, out_b, g_c = together((out_a, out_b, g_c))
    out_y = to(out_a, TO_Y)
    send, keep = expert_call(backward_kernel, (g_own, g_y, g_c), gate_mat, up_mat, down_mat, (slope, gated), 20_000_000_000)
    grad_a, grad_b = halves(keep, to(send, TO_CORE))
    out_rows = back(finish(out_b, out_y))
    grad_rows = to(finish(grad_b, to(grad_a, TO_Y)), PREV_FLIP)
    out_rows, grad_rows = together((out_rows, grad_rows))
    out_rows = to(out_rows, NEXT_FLIP)
    grad_rows = back(grad_rows)
    return mix(combine_next, out_rows), mix(combine_prev, grad_rows)


def solution(mesh):
    rows = P(AXES, None)
    in_specs = (rows, rows, rows, rows, P("pipe", None, "ep"), P("pipe", None, "ep"), P("pipe", "ep", None))
    return jax.shard_map(shards, mesh=mesh, in_specs=in_specs, out_specs=(rows, rows), check_vma=False)
```

time: 147 us -> 131 us (0.89)
  matrix products: 18.8 us -> 4.41 us
  waiting for transfers between devices: 72 us -> 65.3 us
  Pallas kernels: 0 us -> 6.57 us
  other arithmetic: 5.76 us -> 3.71 us
    dot_general x10 -> x4, matrix products: 18.8 us -> 4.41 us  [dot(): return jnp.dot(a, b, preferred_element_type=jnp.float32)]
    pallas_call x0 -> x2, Pallas kernels: none -> 6.57 us  [expert_call(): pl.pallas_call(kernel, out_shape=out_shape, in_specs=[VMEM] * len(operand...]
    ppermute x12, waiting for transfers between devices: 44.7 us -> 39.8 us  [to(): return lax.ppermute(values, AXES, table)]
    ppermute x12, starting transfers between devices: 17 us -> 21.1 us  [to(): return lax.ppermute(values, AXES, table)]
    all_to_all x4 -> x3, starting transfers between devices: 28.3 us -> 24.2 us  [over_z(): lax.all_to_all(values, 'ep', 0, 0, axis_index_groups=Z_GROUPS, tiled=True)]
    unnamed x14 -> x16, local copies, waits for them, and re-layouts: 2.05 us -> 4.5 us
    concatenate x2, other arithmetic: 2.16 us -> 0.12 us  [the longest x1 0.06 us: shards(): x_c = to(jnp.concatenate([x_own, x_y], axis=0), TO_CORE)]
    all_to_all x4 -> x3, waiting for transfers between devices: 27.3 us -> 25.5 us  [over_z(): lax.all_to_all(values, 'ep', 0, 0, axis_index_groups=Z_GROUPS, tiled=True)]
  transfers between devices with their start and end apart: 16 -> 15, of which waited for: 10 -> 12; matrix products, arithmetic and copies ran while one was open for 11% -> 3% of each run, Pallas kernels for 0% -> 3%
where the time goes in v2:
time: 131 us
  waiting for transfers between devices  65.3 us (50%)
  starting transfers between devices  45.3 us (35%)
  Pallas kernels  6.57 us (5%)
  local copies, waits for them, and re-layouts  4.81 us (4%)
  matrix products  4.41 us (3%)
  other arithmetic  3.71 us (3%)
    ppermute x12, waiting for transfers between devices, to(): return lax.ppermute(values, AXES, table)  39.8 us
    all_to_all x3, waiting for transfers between devices, over_z(): lax.all_to_all(values, 'ep', 0, 0, axis_index_groups=Z_GROUPS, tiled=True)  25.5 us
    all_to_all x3, starting transfers between devices, over_z(): lax.all_to_all(values, 'ep', 0, 0, axis_index_groups=Z_GROUPS, tiled=True)  24.2 us
    ppermute x12, starting transfers between devices, to(): return lax.ppermute(values, AXES, table)  21.1 us
    pallas_call x2, Pallas kernels, expert_call(): pl.pallas_call(kernel, out_shape=out_shape, in_specs=[VMEM] * len(operand...  6.57 us
    unnamed x16, local copies, waits for them, and re-layouts  4.5 us
    dot_general x4, matrix products, dot(): return jnp.dot(a, b, preferred_element_type=jnp.float32)  4.41 us
  transfers between devices with their start and end apart: 15, of which 12 were waited for; matrix products, arithmetic and copies ran while one was open for 3% of the time, Pallas kernels for 3%

profile of v2, /device:TPU:32, one launch (start us, length us, event | category | flops | bytes accessed | tf_op | source)
XLA Modules:
  0.0 131.0 jit_solution(10402019685226285370)
XLA Ops:
  0.6 0.0 copy-start
  0.6 0.0 copy-start.4
  0.7 0.8 convert_reduce_fusion
  1.5 0.1 copy.15
  1.6 0.2 reduce_window_sum.11
  1.9 0.0 copy-done
  1.9 0.4 fusion.31
  2.3 0.0 copy-done.4
  2.3 1.3 %fusion = bf16[128,3584]{1,0:T(8,128)(2,1)} fusion(f32[128,3584]{1,0:T(8,128)S(1)} %fusion.31, pred[128,128]{0,1:T(8,128)(4,1)S(1)} %bitcast.36, bf16[128,3584]{1,0:T(8,128)(2,1)S(1)} %copy-done.4), kind=kOutput, calls=%fused_computation.1 | convolution fusion | flops 118358016 | bytes 3686400 | tf_op jit(solution)/shard_map/dot_general | solution.py:42
  3.6 0.0 copy-start.7
  3.6 0.0 copy-start.6
  3.6 8.7 %all-to-all-start = ((bf16[8,16,3584]{2,1,0:T(8,128)(2,1)}), bf16[8,16,3584]{2,1,0:T(8,128)(2,1)S(1)}, u32[]{:S(2)}, u32[]{:S(2)}) async-start(bf16[8,16,3584]{2,1,0:T(8,128)(2,1)} %bitcast.2), calls=%async_computation | async-start | bytes 1835008 | tf_op jit(solution)/shard_map/all_to_all | solution.py:38
  12.3 0.1 eq.58
  12.4 0.0 copy-done.7
  12.4 0.0 copy-done.6
  12.5 0.1 bitcast_select_fusion
  12.6 3.3 %collective-permute-start = (f32[128,64]{0,1:T(8,128)S(1)}, f32[128,64]{0,1:T(8,128)S(1)}, u32[]{:S(2)}, u32[]{:S(2)}) collective-permute-start(f32[128,64]{0,1:T(8,128)S(1)} %bitcast_select_fusion), channel_id=1, source_target_pairs={{0,32},{1,33},{2,34},{3,35},{4,36},{5,37},{6,38},{7,39},{8,40},{9,... | collective-permute-start | bytes 98312 | tf_op jit(solution)/shard_map/ppermute | solution.py:143
  15.8 2.4 %collective-permute-start.1 = (f32[128,64]{0,1:T(8,128)S(1)}, f32[128,64]{0,1:T(8,128)S(1)}, u32[]{:S(2)}, u32[]{:S(2)}) collective-permute-start(f32[128,64]{0,1:T(8,128)S(1)} %bitcast_select_fusion), channel_id=1, source_target_pairs={{0,224},{1,225},{2,226},{3,227},{4,228},{5,229},{6,230},{7,231},{8... | collective-permute-start | bytes 98312 | tf_op jit(solution)/shard_map/ppermute | solution.py:143
  18.3 18.5 %all-to-all-done = bf16[8,16,3584]{2,1,0:T(8,128)(2,1)S(1)} async-done(((bf16[8,16,3584]{2,1,0:T(8,128)(2,1)}), bf16[8,16,3584]{2,1,0:T(8,128)(2,1)S(1)}, u32[]{:S(2)}, u32[]{:S(2)}) %all-to-all-start) | async-done | bytes 917536 | tf_op jit(solution)/shard_map/all_to_all | solution.py:38
  36.8 0.0 copy-start.1
  36.8 0.1 slice_bitcast_fusion
  36.9 0.0 collective-permute-done
  36.9 0.0 collective-permute-done.1
  36.9 1.7 %collective-permute-start.2 = (bf16[64,3584]{1,0:T(8,128)(2,1)S(1)}, bf16[64,3584]{1,0:T(8,128)(2,1)S(1)}, u32[]{:S(2)}, u32[]{:S(2)}) collective-permute-start(bf16[64,3584]{1,0:T(8,128)(2,1)S(1)} %get-tuple-element.29.own_ref), channel_id=1, source_target_pairs={{0,2},{1,3},{2,0},{3,1},{4,6},{5,7},{6,4},{7,5},{8,10},{9,11},{10,... | collective-permute-start | bytes 1376264 | tf_op jit(solution)/shard_map/ppermute | solution.py:143
  38.5 8.3 %collective-permute-done.2.y_ref = bf16[64,3584]{1,0:T(8,128)(2,1)S(1)} collective-permute-done((bf16[64,3584]{1,0:T(8,128)(2,1)S(1)}, bf16[64,3584]{1,0:T(8,128)(2,1)S(1)}, u32[]{:S(2)}, u32[]{:S(2)}) %collective-permute-start.2) | collective-permute-done | bytes 458784 | tf_op jit(solution)/shard_map/ppermute | solution.py:143
  46.8 0.1 pad_maximum_fusion
  46.9 0.1 collective-permute-start.3
  47.0 1.7 %collective-permute-start.4 = (bf16[64,3584]{1,0:T(8,128)(2,1)S(1)}, bf16[64,3584]{1,0:T(8,128)(2,1)S(1)}, u32[]{:S(2)}, u32[]{:S(2)}) collective-permute-start(bf16[64,3584]{1,0:T(8,128)(2,1)S(1)} %get-tuple-element.38.own_ref), channel_id=1, source_target_pairs={{0,2},{1,3},{2,0},{3,1},{4,6},{5,7},{6,4},{7,5},{8,10},{9,11},{10,... | collective-permute-start | bytes 1376264 | tf_op jit(solution)/shard_map/ppermute | solution.py:143
  48.6 0.8 collective-permute-done.3.c_ref
  49.4 0.0 copy-done.1
  49.4 0.0 copy-start.2
  49.4 1.8 %copy-done.2 = bf16[1,3584,384]{2,1,0:T(8,128)(2,1)S(1)} copy-done((bf16[1,3584,384]{2,1,0:T(8,128)(2,1)S(1)}, bf16[1,3584,384]{2,1,0:T(8,128)(2,1)}, u32[]{:S(2)}) %copy-start.2) | copy-done | bytes 2752536
  51.2 0.0 copy-start.3
  51.2 1.8 %copy-done.3 = bf16[1,384,3584]{2,1,0:T(8,128)(2,1)S(1)} copy-done((bf16[1,384,3584]{2,1,0:T(8,128)(2,1)S(1)}, bf16[1,384,3584]{2,1,0:T(8,128)(2,1)}, u32[]{:S(2)}) %copy-start.3) | copy-done | bytes 2752536
  53.0 3.4 %shard_map.86 = (bf16[128,3584]{1,0:T(8,128)(2,1)S(1)}, f32[128,3584]{1,0:T(8,128)S(1)}, f32[256,384]{1,0:T(8,128)S(1)}, f32[256,384]{1,0:T(8,128)S(1)}) custom-call(bf16[64,3584]{1,0:T(8,128)(2,1)S(1)} %get-tuple-element.29.own_ref, bf16[64,3584]{1,0:T(8,128)(2,1)S(1)} %collective-permute-done.2.y_ref, bf16[128,3584]{1,0:T(8,128)(2,1)S(1)} %collective-permute-done.3.c_ref, ...), custom_call_target="tpu_custom_call" | custom-call | flops 20000000000 | bytes 12000000 | tf_op jit(solution)/shard_map/pallas_call | solution.py:107
  56.4 3.6 %collective-permute-done.4.y_ref = bf16[64,3584]{1,0:T(8,128)(2,1)S(1)} collective-permute-done((bf16[64,3584]{1,0:T(8,128)(2,1)S(1)}, bf16[64,3584]{1,0:T(8,128)(2,1)S(1)}, u32[]{:S(2)}, u32[]{:S(2)}) %collective-permute-start.4) | collective-permute-done | bytes 458784 | tf_op jit(solution)/shard_map/ppermute | solution.py:143
  59.9 0.0 collective-permute-start.5
  59.9 0.1 pad_maximum_fusion.1
  60.0 0.6 collective-permute-start.6
  60.6 1.8 %collective-permute-done.5 = bf16[128,3584]{1,0:T(8,128)(2,1)S(1)} collective-permute-done((bf16[128,3584]{1,0:T(8,128)(2,1)S(1)}, bf16[128,3584]{1,0:T(8,128)(2,1)S(1)}, u32[]{:S(2)}, u32[]{:S(2)}) %collective-permute-start.5) | collective-permute-done | bytes 917536 | tf_op jit(solution)/shard_map/ppermute | solution.py:143
  62.4 0.2 convert_add_fusion
  62.6 1.1 collective-permute-done.6.c_ref
  63.7 3.2 %shard_map.87 = (bf16[128,3584]{1,0:T(8,128)(2,1)S(1)}, f32[128,3584]{1,0:T(8,128)S(1)}) custom-call(bf16[64,3584]{1,0:T(8,128)(2,1)S(1)} %get-tuple-element.38.own_ref, bf16[64,3584]{1,0:T(8,128)(2,1)S(1)} %collective-permute-done.4.y_ref, bf16[128,3584]{1,0:T(8,128)(2,1)S(1)} %collective-permute-done.6.c_ref, bf16[3584,384]{1,0:T(8,128)(2,1)S(1)} %bitcast.30, ...), custom_call_target="tpu_custom_call" | custom-call | flops 20000000000 | bytes 12000000 | tf_op jit(solution)/shard_map/pallas_call | solution.py:107
  66.9 0.2 collective-permute-start.8
  67.1 1.7 %collective-permute-start.7 = (bf16[64,3584]{1,0:T(8,128)(2,1)S(1)}, bf16[64,3584]{1,0:T(8,128)(2,1)S(1)}, u32[]{:S(2)}, u32[]{:S(2)}) collective-permute-start(bf16[64,3584]{1,0:T(8,128)(2,1)S(1)} %get-tuple-element.41), channel_id=1, source_target_pairs={{0,2},{1,3},{2,0},{3,1},{4,6},{5,7},{6,4},{7,5},{8,10},{9,11},{10,... | collective-permute-start | bytes 1376264 | tf_op jit(solution)/shard_map/ppermute | solution.py:143
  68.9 0.6 collective-permute-done.8
  69.5 0.0 copy-start.5
  69.5 0.9 copy-done.5
  70.4 0.1 add_convert_fusion.1
  70.5 1.7 %collective-permute-start.9 = (bf16[64,3584]{1,0:T(8,128)(2,1)S(1)}, bf16[64,3584]{1,0:T(8,128)(2,1)}, u32[]{:S(2)}, u32[]{:S(2)}) collective-permute-start(bf16[64,3584]{1,0:T(8,128)(2,1)S(1)} %add_convert_fusion.1), channel_id=1, source_target_pairs={{0,2},{1,3},{2,0},{3,1},{4,6},{5,7},{6,4},{7,5},{8,10},{9,11},{10,... | collective-permute-start | bytes 1376264 | tf_op jit(solution)/shard_map/ppermute | solution.py:143
  72.1 8.5 %collective-permute-done.7 = bf16[64,3584]{1,0:T(8,128)(2,1)S(1)} collective-permute-done((bf16[64,3584]{1,0:T(8,128)(2,1)S(1)}, bf16[64,3584]{1,0:T(8,128)(2,1)S(1)}, u32[]{:S(2)}, u32[]{:S(2)}) %collective-permute-start.7) | collective-permute-done | bytes 458784 | tf_op jit(solution)/shard_map/ppermute | solution.py:143
  80.6 0.8 fusion.11
  81.5 8.0 %all-to-all-start.1 = ((bf16[8,8,3584]{2,1,0:T(8,128)(2,1)}), bf16[8,8,3584]{2,1,0:T(8,128)(2,1)}, u32[]{:S(2)}, u32[]{:S(2)}) async-start(bf16[8,8,3584]{2,1,0:T(8,128)(2,1)} %fusion.11), calls=%async_computation.1 | async-start | bytes 917504 | tf_op jit(solution)/shard_map/all_to_all | solution.py:38
  89.5 0.3 collective-permute-done.9
  89.9 1.3 add_convert_fusion
  91.2 5.3 %collective-permute-start.10 = (bf16[64,3584]{1,0:T(8,128)(2,1)S(1)}, bf16[64,3584]{1,0:T(8,128)(2,1)}, u32[]{:S(2)}, u32[]{:S(2)}) collective-permute-start(bf16[64,3584]{1,0:T(8,128)(2,1)S(1)} %add_convert_fusion), channel_id=1, source_target_pairs={{0,226},{1,227},{2,224},{3,225},{4,230},{5,231},{6,228},{7,229},{8... | collective-permute-start | bytes 1376264 | tf_op jit(solution)/shard_map/ppermute | solution.py:143
  96.5 7.0 %all-to-all-done.1 = bf16[8,8,3584]{2,1,0:T(8,128)(2,1)} async-done(((bf16[8,8,3584]{2,1,0:T(8,128)(2,1)}), bf16[8,8,3584]{2,1,0:T(8,128)(2,1)}, u32[]{:S(2)}, u32[]{:S(2)}) %all-to-all-start.1) | async-done | bytes 458784 | tf_op jit(solution)/shard_map/all_to_all | solution.py:38
  103.4 2.4 %collective-permute-done.10 = bf16[64,3584]{1,0:T(8,128)(2,1)} collective-permute-done((bf16[64,3584]{1,0:T(8,128)(2,1)S(1)}, bf16[64,3584]{1,0:T(8,128)(2,1)}, u32[]{:S(2)}, u32[]{:S(2)}) %collective-permute-start.10) | collective-permute-done | bytes 458784 | tf_op jit(solution)/shard_map/ppermute | solution.py:143
  105.8 7.4 %all-to-all-start.2 = ((bf16[8,8,3584]{2,1,0:T(8,128)(2,1)}), bf16[8,8,3584]{2,1,0:T(8,128)(2,1)S(1)}, u32[]{:S(2)}, u32[]{:S(2)}) async-start(bf16[8,8,3584]{2,1,0:T(8,128)(2,1)} %bitcast.13), calls=%async_computation.2 | async-start | bytes 917504 | tf_op jit(solution)/shard_map/all_to_all | solution.py:38
  113.2 2.5 %collective-permute-start.11 = (bf16[64,3584]{1,0:T(8,128)(2,1)}, bf16[64,3584]{1,0:T(8,128)(2,1)S(1)}, u32[]{:S(2)}, u32[]{:S(2)}) collective-permute-start(bf16[64,3584]{1,0:T(8,128)(2,1)} %bitcast.12), channel_id=1, source_target_pairs={{0,34},{1,35},{2,32},{3,33},{4,38},{5,39},{6,36},{7,37},{8,42},{9,... | collective-permute-start | bytes 1376264 | tf_op jit(solution)/shard_map/ppermute | solution.py:143
  115.8 12.5 %collective-permute-done.11 = bf16[64,3584]{1,0:T(8,128)(2,1)S(1)} collective-permute-done((bf16[64,3584]{1,0:T(8,128)(2,1)}, bf16[64,3584]{1,0:T(8,128)(2,1)S(1)}, u32[]{:S(2)}, u32[]{:S(2)}) %collective-permute-start.11) | collective-permute-done | bytes 458784 | tf_op jit(solution)/shard_map/ppermute | solution.py:143
  128.3 1.3 %convolution_convert_fusion.1 = bf16[128,3584]{1,0:T(8,128)(2,1)} fusion(bf16[64,3584]{1,0:T(8,128)(2,1)S(1)} %collective-permute-done.11, bf16[128,64]{0,1:T(8,128)(2,1)S(1)} %get-tuple-element.58, bf16[128,64]{0,1:T(8,128)(2,1)S(1)} %get-tuple-element.59, bf16[128,64]{0,1:T(8,128)(2,1)S(1)} %get-tuple-element.57), kind=kOutput, calls=%fused_computation.3 | convolution fusion | flops 180895744 | bytes 1425408 | tf_op jit(solution)/shard_map/dot_general | solution.py:42
  129.6 0.0 all-to-all-done.2
  129.6 1.3 %convolution_convert_fusion = bf16[128,3584]{1,0:T(8,128)(2,1)} fusion(bf16[64,3584]{1,0:T(8,128)(2,1)S(1)} %bitcast.35, bf16[128,64]{0,1:T(8,128)(2,1)S(1)} %get-tuple-element.55, bf16[128,64]{0,1:T(8,128)(2,1)S(1)} %get-tuple-element.56, bf16[128,64]{0,1:T(8,128)(2,1)S(1)} %get-tuple-element.54), kind=kOutput, calls=%fused_computation.2 | convolution fusion | flops 180895744 | bytes 1425408 | tf_op jit(solution)/shard_map/dot_general | solution.py:42
  (11 shorter events, 0.2 us)
Async XLA Ops:
  0.6 1.3 copy-start
  0.6 1.7 %copy-start.4 = (bf16[128,3584]{1,0:T(8,128)(2,1)S(1)}, bf16[128,3584]{1,0:T(8,128)(2,1)}, u32[]{:S(2)}) copy-start(bf16[128,3584]{1,0:T(8,128)(2,1)} %param.8) | copy-start | bytes 2752516
  3.6 8.8 %copy-start.7 = (f32[128,8]{0,1:T(8,128)S(1)}, f32[128,8]{0,1:T(8,128)}, u32[]{:S(2)}) copy-start(f32[128,8]{0,1:T(8,128)} %param.10) | copy-start | bytes 12292
  3.6 8.8 %copy-start.6 = (s32[128,8]{0,1:T(8,128)S(1)}, s32[128,8]{0,1:T(8,128)}, u32[]{:S(2)}) copy-start(s32[128,8]{0,1:T(8,128)} %param.9) | copy-start | bytes 12292
  3.6 33.2 %all-to-all-start = ((bf16[8,16,3584]{2,1,0:T(8,128)(2,1)}), bf16[8,16,3584]{2,1,0:T(8,128)(2,1)S(1)}, u32[]{:S(2)}, u32[]{:S(2)}) async-start(bf16[8,16,3584]{2,1,0:T(8,128)(2,1)} %bitcast.2), calls=%async_computation | async-start | bytes 1835008 | tf_op jit(solution)/shard_map/all_to_all | solution.py:38
  12.6 24.3 %collective-permute-start = (f32[128,64]{0,1:T(8,128)S(1)}, f32[128,64]{0,1:T(8,128)S(1)}, u32[]{:S(2)}, u32[]{:S(2)}) collective-permute-start(f32[128,64]{0,1:T(8,128)S(1)} %bitcast_select_fusion), channel_id=1, source_target_pairs={{0,32},{1,33},{2,34},{3,35},{4,36},{5,37},{6,38},{7,39},{8,40},{9,... | collective-permute-start | bytes 98312 | tf_op jit(solution)/shard_map/ppermute | solution.py:143
  15.8 21.0 %collective-permute-start.1 = (f32[128,64]{0,1:T(8,128)S(1)}, f32[128,64]{0,1:T(8,128)S(1)}, u32[]{:S(2)}, u32[]{:S(2)}) collective-permute-start(f32[128,64]{0,1:T(8,128)S(1)} %bitcast_select_fusion), channel_id=1, source_target_pairs={{0,224},{1,225},{2,226},{3,227},{4,228},{5,229},{6,230},{7,231},{8... | collective-permute-start | bytes 98312 | tf_op jit(solution)/shard_map/ppermute | solution.py:143
  36.8 12.6 %copy-start.1 = (bf16[1,3584,384]{2,1,0:T(8,128)(2,1)S(1)}, bf16[1,3584,384]{2,1,0:T(8,128)(2,1)}, u32[]{:S(2)}) copy-start(bf16[1,3584,384]{2,1,0:T(8,128)(2,1)} %param.11) | copy-start | bytes 8257540
  36.9 9.9 %collective-permute-start.2 = (bf16[64,3584]{1,0:T(8,128)(2,1)S(1)}, bf16[64,3584]{1,0:T(8,128)(2,1)S(1)}, u32[]{:S(2)}, u32[]{:S(2)}) collective-permute-start(bf16[64,3584]{1,0:T(8,128)(2,1)S(1)} %get-tuple-element.29.own_ref), channel_id=1, source_target_pairs={{0,2},{1,3},{2,0},{3,1},{4,6},{5,7},{6,4},{7,5},{8,10},{9,11},{10,... | collective-permute-start | bytes 1376264 | tf_op jit(solution)/shard_map/ppermute | solution.py:143
  46.9 2.6 %collective-permute-start.3 = (bf16[128,3584]{1,0:T(8,128)(2,1)S(1)}, bf16[128,3584]{1,0:T(8,128)(2,1)S(1)}, u32[]{:S(2)}, u32[]{:S(2)}) collective-permute-start(bf16[128,3584]{1,0:T(8,128)(2,1)S(1)} %pad_maximum_fusion), channel_id=1, source_target_pairs={{0,1},{1,0},{2,3},{3,2},{4,5},{5,4},{6,7},{7,6},{8,9},{9,8},{10,11... | collective-permute-start | bytes 2752520 | tf_op jit(solution)/shard_map/ppermute | solution.py:143
  47.0 12.9 %collective-permute-start.4 = (bf16[64,3584]{1,0:T(8,128)(2,1)S(1)}, bf16[64,3584]{1,0:T(8,128)(2,1)S(1)}, u32[]{:S(2)}, u32[]{:S(2)}) collective-permute-start(bf16[64,3584]{1,0:T(8,128)(2,1)S(1)} %get-tuple-element.38.own_ref), channel_id=1, source_target_pairs={{0,2},{1,3},{2,0},{3,1},{4,6},{5,7},{6,4},{7,5},{8,10},{9,11},{10,... | collective-permute-start | bytes 1376264 | tf_op jit(solution)/shard_map/ppermute | solution.py:143
  49.4 1.8 %copy-start.2 = (bf16[1,3584,384]{2,1,0:T(8,128)(2,1)S(1)}, bf16[1,3584,384]{2,1,0:T(8,128)(2,1)}, u32[]{:S(2)}) copy-start(bf16[1,3584,384]{2,1,0:T(8,128)(2,1)} %param.12) | copy-start | bytes 8257540
  51.2 1.8 %copy-start.3 = (bf16[1,384,3584]{2,1,0:T(8,128)(2,1)S(1)}, bf16[1,384,3584]{2,1,0:T(8,128)(2,1)}, u32[]{:S(2)}) copy-start(bf16[1,384,3584]{2,1,0:T(8,128)(2,1)} %param.13) | copy-start | bytes 8257540
  59.9 2.5 %collective-permute-start.5 = (bf16[128,3584]{1,0:T(8,128)(2,1)S(1)}, bf16[128,3584]{1,0:T(8,128)(2,1)S(1)}, u32[]{:S(2)}, u32[]{:S(2)}) collective-permute-start(bf16[128,3584]{1,0:T(8,128)(2,1)S(1)} %get-tuple-element.37), channel_id=1, source_target_pairs={{0,1},{1,0},{2,3},{3,2},{4,5},{5,4},{6,7},{7,6},{8,9},{9,8},{10,11... | collective-permute-start | bytes 2752520 | tf_op jit(solution)/shard_map/ppermute | solution.py:143
  60.0 3.7 %collective-permute-start.6 = (bf16[128,3584]{1,0:T(8,128)(2,1)S(1)}, bf16[128,3584]{1,0:T(8,128)(2,1)S(1)}, u32[]{:S(2)}, u32[]{:S(2)}) collective-permute-start(bf16[128,3584]{1,0:T(8,128)(2,1)S(1)} %pad_maximum_fusion.1), channel_id=1, source_target_pairs={{0,1},{1,0},{2,3},{3,2},{4,5},{5,4},{6,7},{7,6},{8,9},{9,8},{10,11... | collective-permute-start | bytes 2752520 | tf_op jit(solution)/shard_map/ppermute | solution.py:143
  66.9 2.6 %collective-permute-start.8 = (bf16[128,3584]{1,0:T(8,128)(2,1)S(1)}, bf16[128,3584]{1,0:T(8,128)(2,1)S(1)}, u32[]{:S(2)}, u32[]{:S(2)}) collective-permute-start(bf16[128,3584]{1,0:T(8,128)(2,1)S(1)} %get-tuple-element.46), channel_id=1, source_target_pairs={{0,1},{1,0},{2,3},{3,2},{4,5},{5,4},{6,7},{7,6},{8,9},{9,8},{10,11... | collective-permute-start | bytes 2752520 | tf_op jit(solution)/shard_map/ppermute | solution.py:143
  67.1 13.5 %collective-permute-start.7 = (bf16[64,3584]{1,0:T(8,128)(2,1)S(1)}, bf16[64,3584]{1,0:T(8,128)(2,1)S(1)}, u32[]{:S(2)}, u32[]{:S(2)}) collective-permute-start(bf16[64,3584]{1,0:T(8,128)(2,1)S(1)} %get-tuple-element.41), channel_id=1, source_target_pairs={{0,2},{1,3},{2,0},{3,1},{4,6},{5,7},{6,4},{7,5},{8,10},{9,11},{10,... | collective-permute-start | bytes 1376264 | tf_op jit(solution)/shard_map/ppermute | solution.py:143
  69.5 0.9 copy-start.5
  70.5 19.4 %collective-permute-start.9 = (bf16[64,3584]{1,0:T(8,128)(2,1)S(1)}, bf16[64,3584]{1,0:T(8,128)(2,1)}, u32[]{:S(2)}, u32[]{:S(2)}) collective-permute-start(bf16[64,3584]{1,0:T(8,128)(2,1)S(1)} %add_convert_fusion.1), channel_id=1, source_target_pairs={{0,2},{1,3},{2,0},{3,1},{4,6},{5,7},{6,4},{7,5},{8,10},{9,11},{10,... | collective-permute-start | bytes 1376264 | tf_op jit(solution)/shard_map/ppermute | solution.py:143
  81.5 22.0 %all-to-all-start.1 = ((bf16[8,8,3584]{2,1,0:T(8,128)(2,1)}), bf16[8,8,3584]{2,1,0:T(8,128)(2,1)}, u32[]{:S(2)}, u32[]{:S(2)}) async-start(bf16[8,8,3584]{2,1,0:T(8,128)(2,1)} %fusion.11), calls=%async_computation.1 | async-start | bytes 917504 | tf_op jit(solution)/shard_map/all_to_all | solution.py:38
  91.2 14.6 %collective-permute-start.10 = (bf16[64,3584]{1,0:T(8,128)(2,1)S(1)}, bf16[64,3584]{1,0:T(8,128)(2,1)}, u32[]{:S(2)}, u32[]{:S(2)}) collective-permute-start(bf16[64,3584]{1,0:T(8,128)(2,1)S(1)} %add_convert_fusion), channel_id=1, source_target_pairs={{0,226},{1,227},{2,224},{3,225},{4,230},{5,231},{6,228},{7,229},{8... | collective-permute-start | bytes 1376264 | tf_op jit(solution)/shard_map/ppermute | solution.py:143
  105.8 23.8 %all-to-all-start.2 = ((bf16[8,8,3584]{2,1,0:T(8,128)(2,1)}), bf16[8,8,3584]{2,1,0:T(8,128)(2,1)S(1)}, u32[]{:S(2)}, u32[]{:S(2)}) async-start(bf16[8,8,3584]{2,1,0:T(8,128)(2,1)} %bitcast.13), calls=%async_computation.2 | async-start | bytes 917504 | tf_op jit(solution)/shard_map/all_to_all | solution.py:38
  113.2 15.0 %collective-permute-start.11 = (bf16[64,3584]{1,0:T(8,128)(2,1)}, bf16[64,3584]{1,0:T(8,128)(2,1)S(1)}, u32[]{:S(2)}, u32[]{:S(2)}) collective-permute-start(bf16[64,3584]{1,0:T(8,128)(2,1)} %bitcast.12), channel_id=1, source_target_pairs={{0,34},{1,35},{2,32},{3,33},{4,38},{5,39},{6,36},{7,37},{8,42},{9,... | collective-permute-start | bytes 1376264 | tf_op jit(solution)/shard_map/ppermute | solution.py:143

commit v3 on v2

--- a/solution.py
+++ b/solution.py
@@ -53,14 +53,14 @@
         at += piece.shape[0]
 
 
-def emit_columns(tile, send_ref, keep_ref):
-    half, width = keep_ref.shape
+def emit_columns(tile, outs):
+    part, width = outs[0].shape
     step = width // N_STEPS
     for n in range(N_STEPS):
         cols = pl.ds(n * step, step)
         value = tile(cols)
-        keep_ref[:, cols] = value[:half]
-        send_ref[:, cols] = value[half:].astype(jnp.bfloat16)
+        for i, out in enumerate(outs):
+            out[:, cols] = value[i * part:(i + 1) * part].astype(out.dtype)
 
 
 def over_width(rows_scr, mat, product):
@@ -73,8 +73,8 @@
     return total
 
 
-def forward_kernel(own_ref, y_ref, c_ref, gate_ref, up_ref, down_ref, send_ref, keep_ref, slope_ref, gated_ref, x_scr):
-    fill(x_scr, (own_ref, y_ref, c_ref))
+def forward_kernel(p0, p1, p2, p3, gate_ref, up_ref, down_ref, k0, k1, s0, s1, slope_ref, gated_ref, x_scr):
+    fill(x_scr, (p0, p1, p2, p3))
     gate_val = over_width(x_scr, lambda part: gate_ref[part, :], dot)
     up_val = over_width(x_scr, lambda part: up_ref[part, :], dot)
     sig_val = jax.nn.sigmoid(gate_val)
@@ -82,15 +82,15 @@
     gated_ref[...] = gated
     slope_ref[...] = up_val * sig_val * (1.0 + gate_val * (1.0 - sig_val))
     hidden = (gated * up_val).astype(jnp.bfloat16)
-    emit_columns(lambda cols: dot(hidden, down_ref[:, cols]), send_ref, keep_ref)
-
-
-def backward_kernel(own_ref, y_ref, c_ref, gate_ref, up_ref, down_ref, slope_ref, gated_ref, send_ref, keep_ref, g_scr):
-    fill(g_scr, (own_ref, y_ref, c_ref))
+    emit_columns(lambda cols: dot(hidden, down_ref[:, cols]), (k0, k1, s0, s1))
+
+
+def backward_kernel(p0, p1, p2, p3, gate_ref, up_ref, down_ref, slope_ref, gated_ref, k0, k1, s0, s1, g_scr):
+    fill(g_scr, (p0, p1, p2, p3))
     d_hidden = over_width(g_scr, lambda part: down_ref[:, part], dot_t)
     d_gate = (d_hidden * slope_ref[...]).astype(jnp.bfloat16)
     d_up = (d_hidden * gated_ref[...]).astype(jnp.bfloat16)
-    emit_columns(lambda cols: dot_t(d_gate, gate_ref[cols, :]) + dot_t(d_up, up_ref[cols, :]), send_ref, keep_ref)
+    emit_columns(lambda cols: dot_t(d_gate, gate_ref[cols, :]) + dot_t(d_up, up_ref[cols, :]), (k0, k1, s0, s1))
 
 
 VMEM = pl.BlockSpec(memory_space=pltpu.VMEM)
@@ -99,30 +99,45 @@
 def expert_call(kernel, pieces, gate_mat, up_mat, down_mat, saved, cost):
     width, hid = gate_mat.shape
     rows = sum(p.shape[0] for p in pieces)
-    half = rows // 2
-    out_shape = [jax.ShapeDtypeStruct((half, width), jnp.bfloat16), jax.ShapeDtypeStruct((half, width), jnp.float32)]
+    part = rows // 4
+    out_shape = [jax.ShapeDtypeStruct((part, width), t) for t in (jnp.float32, jnp.float32, jnp.bfloat16, jnp.bfloat16)]
     if not saved:
         out_shape += [jax.ShapeDtypeStruct((rows, hid), jnp.float32)] * 2
-    operands = (*pieces, *((m) for m in (gate_mat, up_mat, down_mat)), *saved)
+    operands = (*pieces, *(m for m in (gate_mat, up_mat, down_mat)), *saved)
     return pl.pallas_call(
         kernel,
         out_shape=out_shape,
         in_specs=[VMEM] * len(operands),
         out_specs=[VMEM] * len(out_shape),
         scratch_shapes=[pltpu.VMEM((rows, width), jnp.bfloat16)],
-        compiler_params=pltpu.CompilerParams(vmem_limit_bytes=40 * 2**20),
+        compiler_params=pltpu.CompilerParams(vmem_limit_bytes=20 * 2**20),
         cost_estimate=pl.CostEstimate(flops=cost, bytes_accessed=12_000_000, transcendentals=0),
     )(*operands)
 
 
-def mix(combine, values):
+def mix_kernel(combine_ref, value_ref, out_ref):
+    combine = combine_ref[...]
     hi = combine.astype(jnp.bfloat16)
     rest = combine - hi.astype(jnp.float32)
     mid = rest.astype(jnp.bfloat16)
     low = (rest - mid.astype(jnp.float32)).astype(jnp.bfloat16)
-    lhs = jnp.concatenate([hi, mid, low], axis=1)
-    rhs = jnp.concatenate([values, values, values], axis=0)
-    return dot(lhs, rhs).astype(jnp.bfloat16)
+    weights = jnp.concatenate([hi, mid, low], axis=1)
+    step = out_ref.shape[1] // N_STEPS
+    for n in range(N_STEPS):
+        cols = pl.ds(n * step, step)
+        value = value_ref[:, cols]
+        out_ref[:, cols] = dot(weights, jnp.concatenate([value, value, value], axis=0)).astype(jnp.bfloat16)
+
+
+def mix(combine, values, cost):
+    return pl.pallas_call(
+        mix_kernel,
+        out_shape=jax.ShapeDtypeStruct((combine.shape[0], values.shape[1]), jnp.bfloat16),
+        in_specs=[VMEM, VMEM],
+        out_specs=VMEM,
+        compiler_params=pltpu.CompilerParams(vmem_limit_bytes=20 * 2**20),
+        cost_estimate=pl.CostEstimate(flops=cost, bytes_accessed=2_000_000, transcendentals=0),
+    )(combine, values)
 
 
 def shards(acts, cotan, routes, scores, w_gate, w_up, w_down):
@@ -145,12 +160,8 @@
     def back(values):
         return over_z(values.reshape(N_Z, SLOTS, width)).reshape(ROWS, width)
 
-    def halves(keep, got):
-        a = (keep[:ROWS] + got[:ROWS].astype(jnp.float32)).astype(jnp.bfloat16)
-        return a, keep[ROWS:] + got[ROWS:].astype(jnp.float32)
-
-    def finish(kept, got):
-        return (kept + got.astype(jnp.float32)).astype(jnp.bfloat16)
+    def finish(*terms):
+        return sum(t.astype(jnp.float32) for t in terms).astype(jnp.bfloat16)
 
     empty = jnp.zeros_like(placed)
     first = jnp.concatenate([placed, empty], axis=2).reshape(tok_rows, 2 * ROWS).T.astype(jnp.bfloat16)
@@ -162,24 +173,31 @@
     combine_prev = to(combine, PREV)
     x_own, g_own, combine_next, combine_prev = together((x_own, g_own, combine_next, combine_prev))
     x_y = to(x_own, TO_Y)
-    x_y, x_own, g_own = together((x_y, x_own, g_own))
-    x_c = to(jnp.concatenate([x_own, x_y], axis=0), TO_CORE)
-    send, keep, slope, gated = expert_call(forward_kernel, (x_own, x_y, x_c), gate_mat, up_mat, down_mat, (), 20_000_000_000)
+    x_c = to(x_own, TO_CORE)
+    g_c = to(g_own, TO_CORE)
+    x_y, x_c, g_c, x_own, g_own = together((x_y, x_c, g_c, x_own, g_own))
+    x_cy = to(x_y, TO_CORE)
+    keep_a, keep_b, send_a, send_b, slope, gated = expert_call(
+        forward_kernel, (x_own, x_y, x_c, x_cy), gate_mat, up_mat, down_mat, (), 20_000_000_000
+    )
     g_y = to(g_own, TO_Y)
-    send, keep, slope, gated, g_own, g_y = together((send, keep, slope, gated, g_own, g_y))
-    got = to(send, TO_CORE)
-    g_c = to(jnp.concatenate([g_own, g_y], axis=0), TO_CORE)
-    out_a, out_b = halves(keep, got)
-    out_a, out_b, g_c = together((out_a, out_b, g_c))
+    send_a, send_b, slope, gated, g_y = together((send_a, send_b, slope, gated, g_y))
+    got_a, out_b = to(send_a, TO_CORE), to(send_b, TO_CORE)
+    g_cy = to(g_y, TO_CORE)
+    out_a = finish(keep_a, got_a)
+    out_a, g_cy = together((out_a, g_cy))
     out_y = to(out_a, TO_Y)
-    send, keep = expert_call(backward_kernel, (g_own, g_y, g_c), gate_mat, up_mat, down_mat, (slope, gated), 20_000_000_000)
-    grad_a, grad_b = halves(keep, to(send, TO_CORE))
-    out_rows = back(finish(out_b, out_y))
-    grad_rows = to(finish(grad_b, to(grad_a, TO_Y)), PREV_FLIP)
+    grad_keep_a, grad_keep_b, send_a, send_b = expert_call(
+        backward_kernel, (g_own, g_y, g_c, g_cy), gate_mat, up_mat, down_mat, (slope, gated), 20_000_000_000
+    )
+    got_a, grad_b = to(send_a, TO_CORE), to(send_b, TO_CORE)
+    grad_y = to(finish(grad_keep_a, got_a), TO_Y)
+    out_rows = back(finish(keep_b, out_b, out_y))
+    grad_rows = to(finish(grad_keep_b, grad_b, grad_y), PREV_FLIP)
     out_rows, grad_rows = together((out_rows, grad_rows))
     out_rows = to(out_rows, NEXT_FLIP)
     grad_rows = back(grad_rows)
-    return mix(combine_next, out_rows), mix(combine_prev, grad_rows)
+    return mix(combine_next, out_rows, 500_000_000), mix(combine_prev, grad_rows, 500_000_000)
 
 
 def solution(mesh):

time: 131 us -> 130 us (level)
  Pallas kernels: 6.57 us -> 9.31 us
  matrix products: 4.41 us -> 1.71 us
  waiting for transfers between devices: 65.3 us -> 63 us
    pallas_call x0 -> x2, Pallas kernels: none -> 2.73 us  [mix(): pl.pallas_call(mix_kernel, out_shape=jax.ShapeDtypeStruct((combine.shape[...]
    dot_general x4 -> x2, matrix products: 4.41 us -> 1.71 us  [dot(): return jnp.dot(a, b, preferred_element_type=jnp.float32)]
    ppermute x12 -> x16, waiting for transfers between devices: 39.8 us -> 38.5 us  [to(): return lax.ppermute(values, AXES, table)]
    unnamed x16 -> x20, local copies, waits for them, and re-layouts: 4.5 us -> 5.36 us
    ppermute x12 -> x16, starting transfers between devices: 21.1 us -> 21.4 us  [to(): return lax.ppermute(values, AXES, table)]
  transfers between devices with their start and end apart: 15 -> 19, of which waited for: 12 -> 11; matrix products, arithmetic and copies ran while one was open for 3% -> 2% of each run, Pallas kernels for 3% -> 4%
where the time goes in v3:
time: 130 us; the launch traced here: 129 us
  waiting for transfers between devices  63 us (48%)
  starting transfers between devices  45 us (35%)
  Pallas kernels  9.31 us (7%)
  local copies, waits for them, and re-layouts  5.98 us (5%)
  other arithmetic  3.46 us (3%)
  matrix products  1.71 us (1%)
    ppermute x16, waiting for transfers between devices, to(): return lax.ppermute(values, AXES, table)  38.5 us
    all_to_all x3, waiting for transfers between devices, over_z(): lax.all_to_all(values, 'ep', 0, 0, axis_index_groups=Z_GROUPS, tiled=True)  24.5 us
    all_to_all x3, starting transfers between devices, over_z(): lax.all_to_all(values, 'ep', 0, 0, axis_index_groups=Z_GROUPS, tiled=True)  23.6 us
    ppermute x16, starting transfers between devices, to(): return lax.ppermute(values, AXES, table)  21.4 us
    pallas_call x2, Pallas kernels, expert_call(): pl.pallas_call(kernel, out_shape=out_shape, in_specs=[VMEM] * len(operand...  6.58 us
    unnamed x20, local copies, waits for them, and re-layouts  5.36 us
    pallas_call x2, Pallas kernels, mix(): pl.pallas_call(mix_kernel, out_shape=jax.ShapeDtypeStruct((combine.shape[...  2.73 us
  transfers between devices with their start and end apart: 19, of which 11 were waited for; matrix products, arithmetic and copies ran while one was open for 2% of the time, Pallas kernels for 4%

profile of v3, /device:TPU:32, one launch (start us, length us, event | category | flops | bytes accessed | tf_op | source)
XLA Modules:
  0.0 129.2 jit_solution(16818995007401772675)
XLA Ops:
  0.6 0.0 copy-start
  0.6 0.0 copy-start.7
  0.7 0.8 convert_reduce_fusion
  1.5 0.1 copy.18
  1.6 0.2 reduce_window_sum.11
  1.9 0.0 copy-done
  1.9 0.4 fusion.4
  2.3 0.0 copy-done.7
  2.3 1.3 %fusion = bf16[128,3584]{1,0:T(8,128)(2,1)} fusion(f32[128,3584]{1,0:T(8,128)S(1)} %fusion.4, pred[128,128]{0,1:T(8,128)(4,1)S(1)} %bitcast.33, bf16[128,3584]{1,0:T(8,128)(2,1)S(1)} %copy-done.7), kind=kOutput, calls=%fused_computation.1 | convolution fusion | flops 118358016 | bytes 3686400 | tf_op jit(solution)/shard_map/dot_general | solution.py:42
  3.6 8.7 %all-to-all-start = ((bf16[8,16,3584]{2,1,0:T(8,128)(2,1)}), bf16[8,16,3584]{2,1,0:T(8,128)(2,1)S(1)}, u32[]{:S(2)}, u32[]{:S(2)}) async-start(bf16[8,16,3584]{2,1,0:T(8,128)(2,1)} %bitcast.2), calls=%async_computation | async-start | bytes 1835008 | tf_op jit(solution)/shard_map/all_to_all | solution.py:38
  12.4 0.1 copy.23
  12.5 0.1 copy.22
  12.6 0.1 copy.21
  12.7 0.1 eq.58
  12.8 3.3 %collective-permute-start = (f32[128,64]{1,0:T(8,128)S(1)}, f32[128,64]{1,0:T(8,128)S(1)}, u32[]{:S(2)}, u32[]{:S(2)}) collective-permute-start(f32[128,64]{1,0:T(8,128)S(1)} %and_select_fusion), channel_id=1, source_target_pairs={{0,32},{1,33},{2,34},{3,35},{4,36},{5,37},{6,38},{7,39},{8,40},{9,... | collective-permute-start | bytes 98312 | tf_op jit(solution)/shard_map/ppermute | solution.py:158
  16.1 2.4 %collective-permute-start.1 = (f32[128,64]{1,0:T(8,128)S(1)}, f32[128,64]{1,0:T(8,128)S(1)}, u32[]{:S(2)}, u32[]{:S(2)}) collective-permute-start(f32[128,64]{1,0:T(8,128)S(1)} %and_select_fusion), channel_id=1, source_target_pairs={{0,224},{1,225},{2,226},{3,227},{4,228},{5,229},{6,230},{7,231},{8... | collective-permute-start | bytes 98312 | tf_op jit(solution)/shard_map/ppermute | solution.py:158
  18.6 18.2 %all-to-all-done = bf16[8,16,3584]{2,1,0:T(8,128)(2,1)S(1)} async-done(((bf16[8,16,3584]{2,1,0:T(8,128)(2,1)}), bf16[8,16,3584]{2,1,0:T(8,128)(2,1)S(1)}, u32[]{:S(2)}, u32[]{:S(2)}) %all-to-all-start) | async-done | bytes 917536 | tf_op jit(solution)/shard_map/all_to_all | solution.py:38
  36.8 0.1 slice_bitcast_fusion
  36.9 0.0 collective-permute-done.combine_ref
  36.9 0.0 collective-permute-done.1.combine_ref
  36.9 1.7 %collective-permute-start.2 = (bf16[64,3584]{1,0:T(8,128)(2,1)S(1)}, bf16[64,3584]{1,0:T(8,128)(2,1)S(1)}, u32[]{:S(2)}, u32[]{:S(2)}) collective-permute-start(bf16[64,3584]{1,0:T(8,128)(2,1)S(1)} %get-tuple-element.33.p0), channel_id=1, source_target_pairs={{0,2},{1,3},{2,0},{3,1},{4,6},{5,7},{6,4},{7,5},{8,10},{9,11},{10,... | collective-permute-start | bytes 1376264 | tf_op jit(solution)/shard_map/ppermute | solution.py:158
  38.5 0.0 collective-permute-start.3
  38.5 0.5 collective-permute-start.4
  39.1 7.8 %collective-permute-done.2.p1 = bf16[64,3584]{1,0:T(8,128)(2,1)S(1)} collective-permute-done((bf16[64,3584]{1,0:T(8,128)(2,1)S(1)}, bf16[64,3584]{1,0:T(8,128)(2,1)S(1)}, u32[]{:S(2)}, u32[]{:S(2)}) %collective-permute-start.2) | collective-permute-done | bytes 458784 | tf_op jit(solution)/shard_map/ppermute | solution.py:158
  46.8 0.0 collective-permute-done.3.p2
  46.8 0.0 collective-permute-done.4.p2
  46.8 0.0 collective-permute-start.5
  46.8 1.7 %collective-permute-start.6 = (bf16[64,3584]{1,0:T(8,128)(2,1)S(1)}, bf16[64,3584]{1,0:T(8,128)(2,1)S(1)}, u32[]{:S(2)}, u32[]{:S(2)}) collective-permute-start(bf16[64,3584]{1,0:T(8,128)(2,1)S(1)} %get-tuple-element.41.p0), channel_id=1, source_target_pairs={{0,2},{1,3},{2,0},{3,1},{4,6},{5,7},{6,4},{7,5},{8,10},{9,11},{10,... | collective-permute-start | bytes 1376264 | tf_op jit(solution)/shard_map/ppermute | solution.py:158
  48.5 0.1 collective-permute-done.5.p3
  48.6 1.8 %copy-done.1 = bf16[1,3584,384]{2,1,0:T(8,128)(2,1)S(1)} copy-done((bf16[1,3584,384]{2,1,0:T(8,128)(2,1)S(1)}, bf16[1,3584,384]{2,1,0:T(8,128)(2,1)}, u32[]{:S(2)}) %copy-start.1) | copy-done | bytes 2752536
  50.4 1.8 %copy-done.3 = bf16[1,3584,384]{2,1,0:T(8,128)(2,1)S(1)} copy-done((bf16[1,3584,384]{2,1,0:T(8,128)(2,1)S(1)}, bf16[1,3584,384]{2,1,0:T(8,128)(2,1)}, u32[]{:S(2)}) %copy-start.3) | copy-done | bytes 2752536
  52.2 1.8 %copy-done.5 = bf16[1,384,3584]{2,1,0:T(8,128)(2,1)S(1)} copy-done((bf16[1,384,3584]{2,1,0:T(8,128)(2,1)S(1)}, bf16[1,384,3584]{2,1,0:T(8,128)(2,1)}, u32[]{:S(2)}) %copy-start.5) | copy-done | bytes 2752536
  54.0 3.4 %shard_map.86 = (f32[64,3584]{1,0:T(8,128)S(1)}, f32[64,3584]{1,0:T(8,128)S(1)}, bf16[64,3584]{1,0:T(8,128)(2,1)S(1)}, bf16[64,3584]{1,0:T(8,128)(2,1)S(1)}, f32...) custom-call(bf16[64,3584]{1,0:T(8,128)(2,1)S(1)} %get-tuple-element.33.p0, bf16[64,3584]{1,0:T(8,128)(2,1)S(1)} %collective-permute-done.2.p1, ...), custom_call_target="tpu_custom_call" | custom-call | flops 20000000000 | bytes 12000000 | tf_op jit(solution)/shard_map/pallas_call | solution.py:107
  57.4 2.4 %collective-permute-done.6.p1 = bf16[64,3584]{1,0:T(8,128)(2,1)S(1)} collective-permute-done((bf16[64,3584]{1,0:T(8,128)(2,1)S(1)}, bf16[64,3584]{1,0:T(8,128)(2,1)S(1)}, u32[]{:S(2)}, u32[]{:S(2)}) %collective-permute-start.6) | collective-permute-done | bytes 458784 | tf_op jit(solution)/shard_map/ppermute | solution.py:158
  59.8 0.0 collective-permute-start.8
  59.8 0.5 collective-permute-start.9
  60.3 1.3 %collective-permute-done.8 = bf16[64,3584]{1,0:T(8,128)(2,1)S(1)} collective-permute-done((bf16[64,3584]{1,0:T(8,128)(2,1)S(1)}, bf16[64,3584]{1,0:T(8,128)(2,1)S(1)}, u32[]{:S(2)}, u32[]{:S(2)}) %collective-permute-start.8) | collective-permute-done | bytes 458784 | tf_op jit(solution)/shard_map/ppermute | solution.py:158
  61.6 0.1 add_convert_fusion.3
  61.7 0.6 collective-permute-done.9.p3
  62.2 0.0 copy-done.2
  62.3 3.2 %shard_map.87 = (f32[64,3584]{1,0:T(8,128)S(1)}, f32[64,3584]{1,0:T(8,128)S(1)}, bf16[64,3584]{1,0:T(8,128)(2,1)S(1)}, bf16[64,3584]{1,0:T(8,128)(2,1)S(1)}) custom-call(bf16[64,3584]{1,0:T(8,128)(2,1)S(1)} %get-tuple-element.41.p0, bf16[64,3584]{1,0:T(8,128)(2,1)S(1)} %collective-permute-done.6.p1, bf16[64,3584]{1,0:T(8,128)(2,1)S(1)} %collective-permute-done.4.p2, ...), custom_call_target="tpu_custom_call" | custom-call | flops 20000000000 | bytes 12000000 | tf_op jit(solution)/shard_map/pallas_call | solution.py:107
  65.5 0.2 collective-permute-start.12
  65.7 0.4 collective-permute-start.7
  66.1 1.6 %collective-permute-start.10 = (bf16[64,3584]{1,0:T(8,128)(2,1)S(1)}, bf16[64,3584]{1,0:T(8,128)(2,1)S(1)}, u32[]{:S(2)}, u32[]{:S(2)}) collective-permute-start(bf16[64,3584]{1,0:T(8,128)(2,1)S(1)} %add_convert_fusion.3), channel_id=1, source_target_pairs={{0,2},{1,3},{2,0},{3,1},{4,6},{5,7},{6,4},{7,5},{8,10},{9,11},{10,... | collective-permute-start | bytes 1376264 | tf_op jit(solution)/shard_map/ppermute | solution.py:158
  67.6 0.0 collective-permute-start.11
  67.6 0.0 collective-permute-done.12
  67.6 0.1 add_convert_fusion.1
  67.7 1.4 %collective-permute-start.13 = (bf16[64,3584]{1,0:T(8,128)(2,1)S(1)}, bf16[64,3584]{1,0:T(8,128)(2,1)}, u32[]{:S(2)}, u32[]{:S(2)}) collective-permute-start(bf16[64,3584]{1,0:T(8,128)(2,1)S(1)} %add_convert_fusion.1), channel_id=1, source_target_pairs={{0,2},{1,3},{2,0},{3,1},{4,6},{5,7},{6,4},{7,5},{8,10},{9,11},{10,... | collective-permute-start | bytes 1376264 | tf_op jit(solution)/shard_map/ppermute | solution.py:158
  69.1 0.0 collective-permute-done.7
  69.1 10.3 %collective-permute-done.10 = bf16[64,3584]{1,0:T(8,128)(2,1)S(1)} collective-permute-done((bf16[64,3584]{1,0:T(8,128)(2,1)S(1)}, bf16[64,3584]{1,0:T(8,128)(2,1)S(1)}, u32[]{:S(2)}, u32[]{:S(2)}) %collective-permute-start.10) | collective-permute-done | bytes 458784 | tf_op jit(solution)/shard_map/ppermute | solution.py:158
  79.4 0.9 fusion.1
  80.3 7.4 %all-to-all-start.1 = ((bf16[8,8,3584]{2,1,0:T(8,128)(2,1)}), bf16[8,8,3584]{2,1,0:T(8,128)(2,1)S(1)}, u32[]{:S(2)}, u32[]{:S(2)}) async-start(bf16[8,8,3584]{2,1,0:T(8,128)(2,1)} %fusion.1), calls=%async_computation.1 | async-start | bytes 917504 | tf_op jit(solution)/shard_map/all_to_all | solution.py:38
  87.8 0.0 collective-permute-done.11
  87.8 0.8 collective-permute-done.13
  88.6 1.3 %add_convert_fusion = bf16[64,3584]{1,0:T(8,128)(2,1)S(1)} fusion(bf16[64,3584]{1,0:T(8,128)(2,1)} %collective-permute-done.13, f32[64,3584]{1,0:T(8,128)S(1)} %get-tuple-element.51, bf16[64,3584]{1,0:T(8,128)(2,1)} %collective-permute-done.11), kind=kLoop, calls=%fused_computation.2 | loop fusion | flops 1146880 | bytes 2293760 | tf_op jit(solution)/shard_map/convert_element_type | solution.py:164
  89.9 5.3 %collective-permute-start.14 = (bf16[64,3584]{1,0:T(8,128)(2,1)S(1)}, bf16[64,3584]{1,0:T(8,128)(2,1)}, u32[]{:S(2)}, u32[]{:S(2)}) collective-permute-start(bf16[64,3584]{1,0:T(8,128)(2,1)S(1)} %add_convert_fusion), channel_id=1, source_target_pairs={{0,226},{1,227},{2,224},{3,225},{4,230},{5,231},{6,228},{7,229},{8... | collective-permute-start | bytes 1376264 | tf_op jit(solution)/shard_map/ppermute | solution.py:158
  95.1 6.2 %all-to-all-done.1 = bf16[8,8,3584]{2,1,0:T(8,128)(2,1)S(1)} async-done(((bf16[8,8,3584]{2,1,0:T(8,128)(2,1)}), bf16[8,8,3584]{2,1,0:T(8,128)(2,1)S(1)}, u32[]{:S(2)}, u32[]{:S(2)}) %all-to-all-start.1) | async-done | bytes 458784 | tf_op jit(solution)/shard_map/all_to_all | solution.py:38
  101.4 3.0 %collective-permute-done.14 = bf16[64,3584]{1,0:T(8,128)(2,1)} collective-permute-done((bf16[64,3584]{1,0:T(8,128)(2,1)S(1)}, bf16[64,3584]{1,0:T(8,128)(2,1)}, u32[]{:S(2)}, u32[]{:S(2)}) %collective-permute-start.14) | collective-permute-done | bytes 458784 | tf_op jit(solution)/shard_map/ppermute | solution.py:158
  104.4 7.4 %all-to-all-start.2 = ((bf16[8,8,3584]{2,1,0:T(8,128)(2,1)}), bf16[8,8,3584]{2,1,0:T(8,128)(2,1)S(1)}, u32[]{:S(2)}, u32[]{:S(2)}) async-start(bf16[8,8,3584]{2,1,0:T(8,128)(2,1)} %bitcast.13), calls=%async_computation.2 | async-start | bytes 917504 | tf_op jit(solution)/shard_map/all_to_all | solution.py:38
  111.8 2.5 %collective-permute-start.15 = (bf16[64,3584]{1,0:T(8,128)(2,1)S(1)}, bf16[64,3584]{1,0:T(8,128)(2,1)S(1)}, u32[]{:S(2)}, u32[]{:S(2)}) collective-permute-start(bf16[64,3584]{1,0:T(8,128)(2,1)S(1)} %bitcast.32), channel_id=1, source_target_pairs={{0,34},{1,35},{2,32},{3,33},{4,38},{5,39},{6,36},{7,37},{8,42},{9,... | collective-permute-start | bytes 1376264 | tf_op jit(solution)/shard_map/ppermute | solution.py:158
  114.3 12.2 %collective-permute-done.15.value_ref = bf16[64,3584]{1,0:T(8,128)(2,1)S(1)} collective-permute-done((bf16[64,3584]{1,0:T(8,128)(2,1)S(1)}, bf16[64,3584]{1,0:T(8,128)(2,1)S(1)}, u32[]{:S(2)}, u32[]{:S(2)}) %collective-permute-start.15) | collective-permute-done | bytes 458784 | tf_op jit(solution)/shard_map/ppermute | solution.py:158
  126.5 1.4 %shard_map.88 = bf16[128,3584]{1,0:T(8,128)(2,1)} custom-call(f32[128,64]{1,0:T(8,128)S(1)} %collective-permute-done.combine_ref, bf16[64,3584]{1,0:T(8,128)(2,1)S(1)} %collective-permute-done.15.value_ref), custom_call_target="tpu_custom_call" | custom-call | flops 500000000 | bytes 2000000 | tf_op jit(solution)/shard_map/pallas_call | solution.py:133
  127.9 0.0 all-to-all-done.2
  127.9 1.4 %shard_map.89 = bf16[128,3584]{1,0:T(8,128)(2,1)} custom-call(f32[128,64]{1,0:T(8,128)S(1)} %collective-permute-done.1.combine_ref, bf16[64,3584]{1,0:T(8,128)(2,1)S(1)} %bitcast.25), custom_call_target="tpu_custom_call" | custom-call | flops 500000000 | bytes 2000000 | tf_op jit(solution)/shard_map/pallas_call | solution.py:133
  (24 shorter events, 0.2 us)
Async XLA Ops:
  0.6 1.3 copy-start
  0.6 1.7 %copy-start.7 = (bf16[128,3584]{1,0:T(8,128)(2,1)S(1)}, bf16[128,3584]{1,0:T(8,128)(2,1)}, u32[]{:S(2)}) copy-start(bf16[128,3584]{1,0:T(8,128)(2,1)} %param.8) | copy-start | bytes 2752516
  3.6 8.7 %copy-start.9 = (f32[128,8]{0,1:T(8,128)S(1)}, f32[128,8]{0,1:T(8,128)}, u32[]{:S(2)}) copy-start(f32[128,8]{0,1:T(8,128)} %param.10) | copy-start | bytes 12292
  3.6 8.7 %copy-start.8 = (s32[128,8]{0,1:T(8,128)S(1)}, s32[128,8]{0,1:T(8,128)}, u32[]{:S(2)}) copy-start(s32[128,8]{0,1:T(8,128)} %param.9) | copy-start | bytes 12292
  3.6 33.2 %all-to-all-start = ((bf16[8,16,3584]{2,1,0:T(8,128)(2,1)}), bf16[8,16,3584]{2,1,0:T(8,128)(2,1)S(1)}, u32[]{:S(2)}, u32[]{:S(2)}) async-start(bf16[8,16,3584]{2,1,0:T(8,128)(2,1)} %bitcast.2), calls=%async_computation | async-start | bytes 1835008 | tf_op jit(solution)/shard_map/all_to_all | solution.py:38
  12.8 24.0 %collective-permute-start = (f32[128,64]{1,0:T(8,128)S(1)}, f32[128,64]{1,0:T(8,128)S(1)}, u32[]{:S(2)}, u32[]{:S(2)}) collective-permute-start(f32[128,64]{1,0:T(8,128)S(1)} %and_select_fusion), channel_id=1, source_target_pairs={{0,32},{1,33},{2,34},{3,35},{4,36},{5,37},{6,38},{7,39},{8,40},{9,... | collective-permute-start | bytes 98312 | tf_op jit(solution)/shard_map/ppermute | solution.py:158
  16.1 20.8 %collective-permute-start.1 = (f32[128,64]{1,0:T(8,128)S(1)}, f32[128,64]{1,0:T(8,128)S(1)}, u32[]{:S(2)}, u32[]{:S(2)}) collective-permute-start(f32[128,64]{1,0:T(8,128)S(1)} %and_select_fusion), channel_id=1, source_target_pairs={{0,224},{1,225},{2,226},{3,227},{4,228},{5,229},{6,230},{7,231},{8... | collective-permute-start | bytes 98312 | tf_op jit(solution)/shard_map/ppermute | solution.py:158
  36.9 9.9 %collective-permute-start.2 = (bf16[64,3584]{1,0:T(8,128)(2,1)S(1)}, bf16[64,3584]{1,0:T(8,128)(2,1)S(1)}, u32[]{:S(2)}, u32[]{:S(2)}) collective-permute-start(bf16[64,3584]{1,0:T(8,128)(2,1)S(1)} %get-tuple-element.33.p0), channel_id=1, source_target_pairs={{0,2},{1,3},{2,0},{3,1},{4,6},{5,7},{6,4},{7,5},{8,10},{9,11},{10,... | collective-permute-start | bytes 1376264 | tf_op jit(solution)/shard_map/ppermute | solution.py:158
  38.5 8.3 %collective-permute-start.3 = (bf16[64,3584]{1,0:T(8,128)(2,1)S(1)}, bf16[64,3584]{1,0:T(8,128)(2,1)S(1)}, u32[]{:S(2)}, u32[]{:S(2)}) collective-permute-start(bf16[64,3584]{1,0:T(8,128)(2,1)S(1)} %get-tuple-element.33.p0), channel_id=1, source_target_pairs={{0,1},{1,0},{2,3},{3,2},{4,5},{5,4},{6,7},{7,6},{8,9},{9,8},{10,11... | collective-permute-start | bytes 1376264 | tf_op jit(solution)/shard_map/ppermute | solution.py:158
  38.5 8.3 %collective-permute-start.4 = (bf16[64,3584]{1,0:T(8,128)(2,1)S(1)}, bf16[64,3584]{1,0:T(8,128)(2,1)S(1)}, u32[]{:S(2)}, u32[]{:S(2)}) collective-permute-start(bf16[64,3584]{1,0:T(8,128)(2,1)S(1)} %get-tuple-element.41.p0), channel_id=1, source_target_pairs={{0,1},{1,0},{2,3},{3,2},{4,5},{5,4},{6,7},{7,6},{8,9},{9,8},{10,11... | collective-permute-start | bytes 1376264 | tf_op jit(solution)/shard_map/ppermute | solution.py:158
  46.8 1.8 %collective-permute-start.5 = (bf16[64,3584]{1,0:T(8,128)(2,1)S(1)}, bf16[64,3584]{1,0:T(8,128)(2,1)S(1)}, u32[]{:S(2)}, u32[]{:S(2)}) collective-permute-start(bf16[64,3584]{1,0:T(8,128)(2,1)S(1)} %collective-permute-done.2.p1), channel_id=1, source_target_pairs={{0,1},{1,0},{2,3},{3,2},{4,5},{5,4},{6,7},{7,6},{8,9},{9,8},{10,11... | collective-permute-start | bytes 1376264 | tf_op jit(solution)/shard_map/ppermute | solution.py:158
  46.8 12.9 %collective-permute-start.6 = (bf16[64,3584]{1,0:T(8,128)(2,1)S(1)}, bf16[64,3584]{1,0:T(8,128)(2,1)S(1)}, u32[]{:S(2)}, u32[]{:S(2)}) collective-permute-start(bf16[64,3584]{1,0:T(8,128)(2,1)S(1)} %get-tuple-element.41.p0), channel_id=1, source_target_pairs={{0,2},{1,3},{2,0},{3,1},{4,6},{5,7},{6,4},{7,5},{8,10},{9,11},{10,... | collective-permute-start | bytes 1376264 | tf_op jit(solution)/shard_map/ppermute | solution.py:158
  48.6 1.8 %copy-start.1 = (bf16[1,3584,384]{2,1,0:T(8,128)(2,1)S(1)}, bf16[1,3584,384]{2,1,0:T(8,128)(2,1)}, u32[]{:S(2)}) copy-start(bf16[1,3584,384]{2,1,0:T(8,128)(2,1)} %param.11) | copy-start | bytes 8257540
  50.4 1.8 %copy-start.3 = (bf16[1,3584,384]{2,1,0:T(8,128)(2,1)S(1)}, bf16[1,3584,384]{2,1,0:T(8,128)(2,1)}, u32[]{:S(2)}) copy-start(bf16[1,3584,384]{2,1,0:T(8,128)(2,1)} %param.12) | copy-start | bytes 8257540
  52.2 1.8 %copy-start.5 = (bf16[1,384,3584]{2,1,0:T(8,128)(2,1)S(1)}, bf16[1,384,3584]{2,1,0:T(8,128)(2,1)}, u32[]{:S(2)}) copy-start(bf16[1,384,3584]{2,1,0:T(8,128)(2,1)} %param.13) | copy-start | bytes 8257540
  54.0 8.3 %copy-start.2 = (bf16[1,3584,384]{2,1,0:T(8,128)(2,1)S(1)}, bf16[1,3584,384]{2,1,0:T(8,128)(2,1)}, u32[]{:S(2)}) copy-start(bf16[1,3584,384]{2,1,0:T(8,128)(2,1)} %param.11) | copy-start | bytes 8257540
  54.0 8.3 %copy-start.4 = (bf16[1,3584,384]{2,1,0:T(8,128)(2,1)S(1)}, bf16[1,3584,384]{2,1,0:T(8,128)(2,1)}, u32[]{:S(2)}) copy-start(bf16[1,3584,384]{2,1,0:T(8,128)(2,1)} %param.12) | copy-start | bytes 8257540
  54.0 8.3 %copy-start.6 = (bf16[1,384,3584]{2,1,0:T(8,128)(2,1)S(1)}, bf16[1,384,3584]{2,1,0:T(8,128)(2,1)}, u32[]{:S(2)}) copy-start(bf16[1,384,3584]{2,1,0:T(8,128)(2,1)} %param.13) | copy-start | bytes 8257540
  59.8 1.8 %collective-permute-start.8 = (bf16[64,3584]{1,0:T(8,128)(2,1)S(1)}, bf16[64,3584]{1,0:T(8,128)(2,1)S(1)}, u32[]{:S(2)}, u32[]{:S(2)}) collective-permute-start(bf16[64,3584]{1,0:T(8,128)(2,1)S(1)} %get-tuple-element.44), channel_id=1, source_target_pairs={{0,1},{1,0},{2,3},{3,2},{4,5},{5,4},{6,7},{7,6},{8,9},{9,8},{10,11... | collective-permute-start | bytes 1376264 | tf_op jit(solution)/shard_map/ppermute | solution.py:158
  59.8 2.5 %collective-permute-start.9 = (bf16[64,3584]{1,0:T(8,128)(2,1)S(1)}, bf16[64,3584]{1,0:T(8,128)(2,1)S(1)}, u32[]{:S(2)}, u32[]{:S(2)}) collective-permute-start(bf16[64,3584]{1,0:T(8,128)(2,1)S(1)} %collective-permute-done.6.p1), channel_id=1, source_target_pairs={{0,1},{1,0},{2,3},{3,2},{4,5},{5,4},{6,7},{7,6},{8,9},{9,8},{10,11... | collective-permute-start | bytes 1376264 | tf_op jit(solution)/shard_map/ppermute | solution.py:158
  65.5 2.2 %collective-permute-start.12 = (bf16[64,3584]{1,0:T(8,128)(2,1)S(1)}, bf16[64,3584]{1,0:T(8,128)(2,1)S(1)}, u32[]{:S(2)}, u32[]{:S(2)}) collective-permute-start(bf16[64,3584]{1,0:T(8,128)(2,1)S(1)} %get-tuple-element.54), channel_id=1, source_target_pairs={{0,1},{1,0},{2,3},{3,2},{4,5},{5,4},{6,7},{7,6},{8,9},{9,8},{10,11... | collective-permute-start | bytes 1376264 | tf_op jit(solution)/shard_map/ppermute | solution.py:158
  65.7 3.4 %collective-permute-start.7 = (bf16[64,3584]{1,0:T(8,128)(2,1)S(1)}, bf16[64,3584]{1,0:T(8,128)(2,1)S(1)}, u32[]{:S(2)}, u32[]{:S(2)}) collective-permute-start(bf16[64,3584]{1,0:T(8,128)(2,1)S(1)} %get-tuple-element.42), channel_id=1, source_target_pairs={{0,1},{1,0},{2,3},{3,2},{4,5},{5,4},{6,7},{7,6},{8,9},{9,8},{10,11... | collective-permute-start | bytes 1376264 | tf_op jit(solution)/shard_map/ppermute | solution.py:158
  66.1 13.4 %collective-permute-start.10 = (bf16[64,3584]{1,0:T(8,128)(2,1)S(1)}, bf16[64,3584]{1,0:T(8,128)(2,1)S(1)}, u32[]{:S(2)}, u32[]{:S(2)}) collective-permute-start(bf16[64,3584]{1,0:T(8,128)(2,1)S(1)} %add_convert_fusion.3), channel_id=1, source_target_pairs={{0,2},{1,3},{2,0},{3,1},{4,6},{5,7},{6,4},{7,5},{8,10},{9,11},{10,... | collective-permute-start | bytes 1376264 | tf_op jit(solution)/shard_map/ppermute | solution.py:158
  67.6 20.1 %collective-permute-start.11 = (bf16[64,3584]{1,0:T(8,128)(2,1)S(1)}, bf16[64,3584]{1,0:T(8,128)(2,1)}, u32[]{:S(2)}, u32[]{:S(2)}) collective-permute-start(bf16[64,3584]{1,0:T(8,128)(2,1)S(1)} %get-tuple-element.52), channel_id=1, source_target_pairs={{0,1},{1,0},{2,3},{3,2},{4,5},{5,4},{6,7},{7,6},{8,9},{9,8},{10,11... | collective-permute-start | bytes 1376264 | tf_op jit(solution)/shard_map/ppermute | solution.py:158
  67.7 20.8 %collective-permute-start.13 = (bf16[64,3584]{1,0:T(8,128)(2,1)S(1)}, bf16[64,3584]{1,0:T(8,128)(2,1)}, u32[]{:S(2)}, u32[]{:S(2)}) collective-permute-start(bf16[64,3584]{1,0:T(8,128)(2,1)S(1)} %add_convert_fusion.1), channel_id=1, source_target_pairs={{0,2},{1,3},{2,0},{3,1},{4,6},{5,7},{6,4},{7,5},{8,10},{9,11},{10,... | collective-permute-start | bytes 1376264 | tf_op jit(solution)/shard_map/ppermute | solution.py:158
  80.3 21.0 %all-to-all-start.1 = ((bf16[8,8,3584]{2,1,0:T(8,128)(2,1)}), bf16[8,8,3584]{2,1,0:T(8,128)(2,1)S(1)}, u32[]{:S(2)}, u32[]{:S(2)}) async-start(bf16[8,8,3584]{2,1,0:T(8,128)(2,1)} %fusion.1), calls=%async_computation.1 | async-start | bytes 917504 | tf_op jit(solution)/shard_map/all_to_all | solution.py:38
  89.9 14.5 %collective-permute-start.14 = (bf16[64,3584]{1,0:T(8,128)(2,1)S(1)}, bf16[64,3584]{1,0:T(8,128)(2,1)}, u32[]{:S(2)}, u32[]{:S(2)}) collective-permute-start(bf16[64,3584]{1,0:T(8,128)(2,1)S(1)} %add_convert_fusion), channel_id=1, source_target_pairs={{0,226},{1,227},{2,224},{3,225},{4,230},{5,231},{6,228},{7,229},{8... | collective-permute-start | bytes 1376264 | tf_op jit(solution)/shard_map/ppermute | solution.py:158
  104.4 23.5 %all-to-all-start.2 = ((bf16[8,8,3584]{2,1,0:T(8,128)(2,1)}), bf16[8,8,3584]{2,1,0:T(8,128)(2,1)S(1)}, u32[]{:S(2)}, u32[]{:S(2)}) async-start(bf16[8,8,3584]{2,1,0:T(8,128)(2,1)} %bitcast.13), calls=%async_computation.2 | async-start | bytes 917504 | tf_op jit(solution)/shard_map/all_to_all | solution.py:38
  111.8 14.7 %collective-permute-start.15 = (bf16[64,3584]{1,0:T(8,128)(2,1)S(1)}, bf16[64,3584]{1,0:T(8,128)(2,1)S(1)}, u32[]{:S(2)}, u32[]{:S(2)}) collective-permute-start(bf16[64,3584]{1,0:T(8,128)(2,1)S(1)} %bitcast.32), channel_id=1, source_target_pairs={{0,34},{1,35},{2,32},{3,33},{4,38},{5,39},{6,36},{7,37},{8,42},{9,... | collective-permute-start | bytes 1376264 | tf_op jit(solution)/shard_map/ppermute | solution.py:158

commit v4 on v3

--- a/solution.py
+++ b/solution.py
@@ -100,7 +100,7 @@
     width, hid = gate_mat.shape
     rows = sum(p.shape[0] for p in pieces)
     part = rows // 4
-    out_shape = [jax.ShapeDtypeStruct((part, width), t) for t in (jnp.float32, jnp.float32, jnp.bfloat16, jnp.bfloat16)]
+    out_shape = [jax.ShapeDtypeStruct((part, width), jnp.bfloat16)] * 4
     if not saved:
         out_shape += [jax.ShapeDtypeStruct((rows, hid), jnp.float32)] * 2
     operands = (*pieces, *(m for m in (gate_mat, up_mat, down_mat)), *saved)
@@ -181,7 +181,7 @@
         forward_kernel, (x_own, x_y, x_c, x_cy), gate_mat, up_mat, down_mat, (), 20_000_000_000
     )
     g_y = to(g_own, TO_Y)
-    send_a, send_b, slope, gated, g_y = together((send_a, send_b, slope, gated, g_y))
+    slope, gated, g_y = together((slope, gated, g_y))
     got_a, out_b = to(send_a, TO_CORE), to(send_b, TO_CORE)
     g_cy = to(g_y, TO_CORE)
     out_a = finish(keep_a, got_a)

time: 130 us -> 128 us (0.985)
    ppermute x16, waiting for transfers between devices: 38.5 us -> 36 us  [to(): return lax.ppermute(values, AXES, table)]
  transfers between devices with their start and end apart: 19 -> 19, of which waited for: 11 -> 10; matrix products, arithmetic and copies ran while one was open for 2% -> 2% of each run, Pallas kernels for 4% -> 4%
where the time goes in v4:
time: 128 us; the launch traced here: 127 us
  waiting for transfers between devices  61.7 us (48%)
  starting transfers between devices  44.6 us (35%)
  Pallas kernels  9.31 us (7%)
  local copies, waits for them, and re-layouts  5.98 us (5%)
  other arithmetic  3.19 us (2%)
  matrix products  1.71 us (1%)
    ppermute x16, waiting for transfers between devices, to(): return lax.ppermute(values, AXES, table)  36 us
    all_to_all x3, waiting for transfers between devices, over_z(): lax.all_to_all(values, 'ep', 0, 0, axis_index_groups=Z_GROUPS, tiled=True)  25.7 us
    all_to_all x3, starting transfers between devices, over_z(): lax.all_to_all(values, 'ep', 0, 0, axis_index_groups=Z_GROUPS, tiled=True)  23.6 us
    ppermute x16, starting transfers between devices, to(): return lax.ppermute(values, AXES, table)  21 us
    pallas_call x2, Pallas kernels, expert_call(): pl.pallas_call(kernel, out_shape=out_shape, in_specs=[VMEM] * len(operand...  6.58 us
    unnamed x20, local copies, waits for them, and re-layouts  5.36 us
    pallas_call x2, Pallas kernels, mix(): pl.pallas_call(mix_kernel, out_shape=jax.ShapeDtypeStruct((combine.shape[...  2.73 us
  transfers between devices with their start and end apart: 19, of which 10 were waited for; matrix products, arithmetic and copies ran while one was open for 2% of the time, Pallas kernels for 4%

profile of v4, /device:TPU:32, one launch (start us, length us, event | category | flops | bytes accessed | tf_op | source)
XLA Modules:
  0.0 127.4 jit_solution(13586384144783284195)
XLA Ops:
  0.6 0.0 copy-start
  0.6 0.0 copy-start.7
  0.7 0.8 convert_reduce_fusion
  1.5 0.1 copy.18
  1.6 0.2 reduce_window_sum.11
  1.9 0.0 copy-done
  1.9 0.4 fusion.4
  2.3 0.0 copy-done.7
  2.3 1.3 %fusion = bf16[128,3584]{1,0:T(8,128)(2,1)} fusion(f32[128,3584]{1,0:T(8,128)S(1)} %fusion.4, pred[128,128]{0,1:T(8,128)(4,1)S(1)} %bitcast.33, bf16[128,3584]{1,0:T(8,128)(2,1)S(1)} %copy-done.7), kind=kOutput, calls=%fused_computation.1 | convolution fusion | flops 118358016 | bytes 3686400 | tf_op jit(solution)/shard_map/dot_general | solution.py:42
  3.6 8.7 %all-to-all-start = ((bf16[8,16,3584]{2,1,0:T(8,128)(2,1)}), bf16[8,16,3584]{2,1,0:T(8,128)(2,1)S(1)}, u32[]{:S(2)}, u32[]{:S(2)}) async-start(bf16[8,16,3584]{2,1,0:T(8,128)(2,1)} %bitcast.2), calls=%async_computation | async-start | bytes 1835008 | tf_op jit(solution)/shard_map/all_to_all | solution.py:38
  12.3 0.0 copy-done.9
  12.4 0.1 copy.23
  12.5 0.1 copy.22
  12.6 0.1 copy.21
  12.7 0.1 eq.58
  12.8 3.3 %collective-permute-start = (f32[128,64]{1,0:T(8,128)S(1)}, f32[128,64]{1,0:T(8,128)S(1)}, u32[]{:S(2)}, u32[]{:S(2)}) collective-permute-start(f32[128,64]{1,0:T(8,128)S(1)} %and_select_fusion), channel_id=1, source_target_pairs={{0,32},{1,33},{2,34},{3,35},{4,36},{5,37},{6,38},{7,39},{8,40},{9,... | collective-permute-start | bytes 98312 | tf_op jit(solution)/shard_map/ppermute | solution.py:158
  16.1 2.4 %collective-permute-start.1 = (f32[128,64]{1,0:T(8,128)S(1)}, f32[128,64]{1,0:T(8,128)S(1)}, u32[]{:S(2)}, u32[]{:S(2)}) collective-permute-start(f32[128,64]{1,0:T(8,128)S(1)} %and_select_fusion), channel_id=1, source_target_pairs={{0,224},{1,225},{2,226},{3,227},{4,228},{5,229},{6,230},{7,231},{8... | collective-permute-start | bytes 98312 | tf_op jit(solution)/shard_map/ppermute | solution.py:158
  18.6 18.2 %all-to-all-done = bf16[8,16,3584]{2,1,0:T(8,128)(2,1)S(1)} async-done(((bf16[8,16,3584]{2,1,0:T(8,128)(2,1)}), bf16[8,16,3584]{2,1,0:T(8,128)(2,1)S(1)}, u32[]{:S(2)}, u32[]{:S(2)}) %all-to-all-start) | async-done | bytes 917536 | tf_op jit(solution)/shard_map/all_to_all | solution.py:38
  36.8 0.1 slice_bitcast_fusion
  36.9 0.0 collective-permute-done.combine_ref
  36.9 0.0 collective-permute-done.1.combine_ref
  36.9 1.7 %collective-permute-start.2 = (bf16[64,3584]{1,0:T(8,128)(2,1)S(1)}, bf16[64,3584]{1,0:T(8,128)(2,1)S(1)}, u32[]{:S(2)}, u32[]{:S(2)}) collective-permute-start(bf16[64,3584]{1,0:T(8,128)(2,1)S(1)} %get-tuple-element.31.p0), channel_id=1, source_target_pairs={{0,2},{1,3},{2,0},{3,1},{4,6},{5,7},{6,4},{7,5},{8,10},{9,11},{10,... | collective-permute-start | bytes 1376264 | tf_op jit(solution)/shard_map/ppermute | solution.py:158
  38.5 0.0 collective-permute-start.3
  38.5 0.5 collective-permute-start.4
  39.1 7.8 %collective-permute-done.2.p1 = bf16[64,3584]{1,0:T(8,128)(2,1)S(1)} collective-permute-done((bf16[64,3584]{1,0:T(8,128)(2,1)S(1)}, bf16[64,3584]{1,0:T(8,128)(2,1)S(1)}, u32[]{:S(2)}, u32[]{:S(2)}) %collective-permute-start.2) | collective-permute-done | bytes 458784 | tf_op jit(solution)/shard_map/ppermute | solution.py:158
  46.8 0.0 collective-permute-done.3.p2
  46.8 0.0 collective-permute-done.4.p2
  46.8 0.0 collective-permute-start.5
  46.8 1.7 %collective-permute-start.8 = (bf16[64,3584]{1,0:T(8,128)(2,1)S(1)}, bf16[64,3584]{1,0:T(8,128)(2,1)S(1)}, u32[]{:S(2)}, u32[]{:S(2)}) collective-permute-start(bf16[64,3584]{1,0:T(8,128)(2,1)S(1)} %get-tuple-element.40.p0), channel_id=1, source_target_pairs={{0,2},{1,3},{2,0},{3,1},{4,6},{5,7},{6,4},{7,5},{8,10},{9,11},{10,... | collective-permute-start | bytes 1376264 | tf_op jit(solution)/shard_map/ppermute | solution.py:158
  48.5 0.1 collective-permute-done.5.p3
  48.6 1.8 %copy-done.1 = bf16[1,3584,384]{2,1,0:T(8,128)(2,1)S(1)} copy-done((bf16[1,3584,384]{2,1,0:T(8,128)(2,1)S(1)}, bf16[1,3584,384]{2,1,0:T(8,128)(2,1)}, u32[]{:S(2)}) %copy-start.1) | copy-done | bytes 2752536
  50.4 1.8 %copy-done.3 = bf16[1,3584,384]{2,1,0:T(8,128)(2,1)S(1)} copy-done((bf16[1,3584,384]{2,1,0:T(8,128)(2,1)S(1)}, bf16[1,3584,384]{2,1,0:T(8,128)(2,1)}, u32[]{:S(2)}) %copy-start.3) | copy-done | bytes 2752536
  52.2 1.8 %copy-done.5 = bf16[1,384,3584]{2,1,0:T(8,128)(2,1)S(1)} copy-done((bf16[1,384,3584]{2,1,0:T(8,128)(2,1)S(1)}, bf16[1,384,3584]{2,1,0:T(8,128)(2,1)}, u32[]{:S(2)}) %copy-start.5) | copy-done | bytes 2752536
  54.0 3.4 %shard_map.86 = (bf16[64,3584]{1,0:T(8,128)(2,1)S(1)}, bf16[64,3584]{1,0:T(8,128)(2,1)S(1)}, bf16[64,3584]{1,0:T(8,128)(2,1)S(1)}, bf16[64,3584]{1,0:T(8,128)(2,...) custom-call(bf16[64,3584]{1,0:T(8,128)(2,1)S(1)} %get-tuple-element.31.p0, ...), custom_call_target="tpu_custom_call" | custom-call | flops 20000000000 | bytes 12000000 | tf_op jit(solution)/shard_map/pallas_call | solution.py:107
  57.4 0.2 collective-permute-start.7
  57.6 2.2 %collective-permute-done.8.p1 = bf16[64,3584]{1,0:T(8,128)(2,1)S(1)} collective-permute-done((bf16[64,3584]{1,0:T(8,128)(2,1)S(1)}, bf16[64,3584]{1,0:T(8,128)(2,1)S(1)}, u32[]{:S(2)}, u32[]{:S(2)}) %collective-permute-start.8) | collective-permute-done | bytes 458784 | tf_op jit(solution)/shard_map/ppermute | solution.py:158
  59.8 0.0 collective-permute-start.9
  59.8 0.0 collective-permute-done.7
  59.8 0.1 add_convert_fusion.3
  59.9 1.7 %collective-permute-done.9.p3 = bf16[64,3584]{1,0:T(8,128)(2,1)S(1)} collective-permute-done((bf16[64,3584]{1,0:T(8,128)(2,1)S(1)}, bf16[64,3584]{1,0:T(8,128)(2,1)S(1)}, u32[]{:S(2)}, u32[]{:S(2)}) %collective-permute-start.9) | collective-permute-done | bytes 458784 | tf_op jit(solution)/shard_map/ppermute | solution.py:158
  61.6 3.2 %shard_map.87 = (bf16[64,3584]{1,0:T(8,128)(2,1)S(1)}, bf16[64,3584]{1,0:T(8,128)(2,1)S(1)}, bf16[64,3584]{1,0:T(8,128)(2,1)S(1)}, bf16[64,3584]{1,0:T(8,128)(2,1)S(1)}) custom-call(bf16[64,3584]{1,0:T(8,128)(2,1)S(1)} %get-tuple-element.40.p0, bf16[64,3584]{1,0:T(8,128)(2,1)S(1)} %collective-permute-done.8.p1, ...), custom_call_target="tpu_custom_call" | custom-call | flops 20000000000 | bytes 12000000 | tf_op jit(solution)/shard_map/pallas_call | solution.py:107
  64.8 0.2 collective-permute-start.12
  65.0 0.4 collective-permute-start.6
  65.4 1.6 %collective-permute-start.10 = (bf16[64,3584]{1,0:T(8,128)(2,1)S(1)}, bf16[64,3584]{1,0:T(8,128)(2,1)S(1)}, u32[]{:S(2)}, u32[]{:S(2)}) collective-permute-start(bf16[64,3584]{1,0:T(8,128)(2,1)S(1)} %add_convert_fusion.3), channel_id=1, source_target_pairs={{0,2},{1,3},{2,0},{3,1},{4,6},{5,7},{6,4},{7,5},{8,10},{9,11},{10,... | collective-permute-start | bytes 1376264 | tf_op jit(solution)/shard_map/ppermute | solution.py:158
  67.0 0.0 collective-permute-start.11
  67.0 0.0 collective-permute-done.12
  67.0 0.9 add_convert_fusion.1
  67.9 1.3 %collective-permute-start.13 = (bf16[64,3584]{1,0:T(8,128)(2,1)}, bf16[64,3584]{1,0:T(8,128)(2,1)S(1)}, u32[]{:S(2)}, u32[]{:S(2)}) collective-permute-start(bf16[64,3584]{1,0:T(8,128)(2,1)} %add_convert_fusion.1), channel_id=1, source_target_pairs={{0,2},{1,3},{2,0},{3,1},{4,6},{5,7},{6,4},{7,5},{8,10},{9,11},{10,... | collective-permute-start | bytes 1376264 | tf_op jit(solution)/shard_map/ppermute | solution.py:158
  69.2 0.0 collective-permute-done.6
  69.2 9.6 %collective-permute-done.10 = bf16[64,3584]{1,0:T(8,128)(2,1)S(1)} collective-permute-done((bf16[64,3584]{1,0:T(8,128)(2,1)S(1)}, bf16[64,3584]{1,0:T(8,128)(2,1)S(1)}, u32[]{:S(2)}, u32[]{:S(2)}) %collective-permute-start.10) | collective-permute-done | bytes 458784 | tf_op jit(solution)/shard_map/ppermute | solution.py:158
  78.8 0.9 fusion.1
  79.7 7.4 %all-to-all-start.1 = ((bf16[8,8,3584]{2,1,0:T(8,128)(2,1)}), bf16[8,8,3584]{2,1,0:T(8,128)(2,1)S(1)}, u32[]{:S(2)}, u32[]{:S(2)}) async-start(bf16[8,8,3584]{2,1,0:T(8,128)(2,1)} %fusion.1), calls=%async_computation.1 | async-start | bytes 917504 | tf_op jit(solution)/shard_map/all_to_all | solution.py:38
  87.1 0.0 collective-permute-done.11
  87.1 0.7 collective-permute-done.13
  87.8 0.2 add_convert_fusion
  88.0 5.3 %collective-permute-start.14 = (bf16[64,3584]{1,0:T(8,128)(2,1)S(1)}, bf16[64,3584]{1,0:T(8,128)(2,1)}, u32[]{:S(2)}, u32[]{:S(2)}) collective-permute-start(bf16[64,3584]{1,0:T(8,128)(2,1)S(1)} %add_convert_fusion), channel_id=1, source_target_pairs={{0,226},{1,227},{2,224},{3,225},{4,230},{5,231},{6,228},{7,229},{8... | collective-permute-start | bytes 1376264 | tf_op jit(solution)/shard_map/ppermute | solution.py:158
  93.3 7.5 %all-to-all-done.1 = bf16[8,8,3584]{2,1,0:T(8,128)(2,1)S(1)} async-done(((bf16[8,8,3584]{2,1,0:T(8,128)(2,1)}), bf16[8,8,3584]{2,1,0:T(8,128)(2,1)S(1)}, u32[]{:S(2)}, u32[]{:S(2)}) %all-to-all-start.1) | async-done | bytes 458784 | tf_op jit(solution)/shard_map/all_to_all | solution.py:38
  100.7 1.8 %collective-permute-done.14 = bf16[64,3584]{1,0:T(8,128)(2,1)} collective-permute-done((bf16[64,3584]{1,0:T(8,128)(2,1)S(1)}, bf16[64,3584]{1,0:T(8,128)(2,1)}, u32[]{:S(2)}, u32[]{:S(2)}) %collective-permute-start.14) | collective-permute-done | bytes 458784 | tf_op jit(solution)/shard_map/ppermute | solution.py:158
  102.5 7.4 %all-to-all-start.2 = ((bf16[8,8,3584]{2,1,0:T(8,128)(2,1)}), bf16[8,8,3584]{2,1,0:T(8,128)(2,1)S(1)}, u32[]{:S(2)}, u32[]{:S(2)}) async-start(bf16[8,8,3584]{2,1,0:T(8,128)(2,1)} %bitcast.13), calls=%async_computation.2 | async-start | bytes 917504 | tf_op jit(solution)/shard_map/all_to_all | solution.py:38
  109.9 2.5 %collective-permute-start.15 = (bf16[64,3584]{1,0:T(8,128)(2,1)S(1)}, bf16[64,3584]{1,0:T(8,128)(2,1)S(1)}, u32[]{:S(2)}, u32[]{:S(2)}) collective-permute-start(bf16[64,3584]{1,0:T(8,128)(2,1)S(1)} %bitcast.32), channel_id=1, source_target_pairs={{0,34},{1,35},{2,32},{3,33},{4,38},{5,39},{6,36},{7,37},{8,42},{9,... | collective-permute-start | bytes 1376264 | tf_op jit(solution)/shard_map/ppermute | solution.py:158
  112.4 12.2 %collective-permute-done.15.value_ref = bf16[64,3584]{1,0:T(8,128)(2,1)S(1)} collective-permute-done((bf16[64,3584]{1,0:T(8,128)(2,1)S(1)}, bf16[64,3584]{1,0:T(8,128)(2,1)S(1)}, u32[]{:S(2)}, u32[]{:S(2)}) %collective-permute-start.15) | collective-permute-done | bytes 458784 | tf_op jit(solution)/shard_map/ppermute | solution.py:158
  124.6 1.4 %shard_map.88 = bf16[128,3584]{1,0:T(8,128)(2,1)} custom-call(f32[128,64]{1,0:T(8,128)S(1)} %collective-permute-done.combine_ref, bf16[64,3584]{1,0:T(8,128)(2,1)S(1)} %collective-permute-done.15.value_ref), custom_call_target="tpu_custom_call" | custom-call | flops 500000000 | bytes 2000000 | tf_op jit(solution)/shard_map/pallas_call | solution.py:133
  126.0 0.0 all-to-all-done.2
  126.0 1.4 %shard_map.89 = bf16[128,3584]{1,0:T(8,128)(2,1)} custom-call(f32[128,64]{1,0:T(8,128)S(1)} %collective-permute-done.1.combine_ref, bf16[64,3584]{1,0:T(8,128)(2,1)S(1)} %bitcast.25), custom_call_target="tpu_custom_call" | custom-call | flops 500000000 | bytes 2000000 | tf_op jit(solution)/shard_map/pallas_call | solution.py:133
  (24 shorter events, 0.2 us)
Async XLA Ops:
  0.6 1.3 copy-start
  0.6 1.7 %copy-start.7 = (bf16[128,3584]{1,0:T(8,128)(2,1)S(1)}, bf16[128,3584]{1,0:T(8,128)(2,1)}, u32[]{:S(2)}) copy-start(bf16[128,3584]{1,0:T(8,128)(2,1)} %param.8) | copy-start | bytes 2752516
  3.6 8.7 %copy-start.9 = (f32[128,8]{0,1:T(8,128)S(1)}, f32[128,8]{0,1:T(8,128)}, u32[]{:S(2)}) copy-start(f32[128,8]{0,1:T(8,128)} %param.10) | copy-start | bytes 12292
  3.6 8.7 %copy-start.8 = (s32[128,8]{0,1:T(8,128)S(1)}, s32[128,8]{0,1:T(8,128)}, u32[]{:S(2)}) copy-start(s32[128,8]{0,1:T(8,128)} %param.9) | copy-start | bytes 12292
  3.6 33.2 %all-to-all-start = ((bf16[8,16,3584]{2,1,0:T(8,128)(2,1)}), bf16[8,16,3584]{2,1,0:T(8,128)(2,1)S(1)}, u32[]{:S(2)}, u32[]{:S(2)}) async-start(bf16[8,16,3584]{2,1,0:T(8,128)(2,1)} %bitcast.2), calls=%async_computation | async-start | bytes 1835008 | tf_op jit(solution)/shard_map/all_to_all | solution.py:38
  12.8 24.0 %collective-permute-start = (f32[128,64]{1,0:T(8,128)S(1)}, f32[128,64]{1,0:T(8,128)S(1)}, u32[]{:S(2)}, u32[]{:S(2)}) collective-permute-start(f32[128,64]{1,0:T(8,128)S(1)} %and_select_fusion), channel_id=1, source_target_pairs={{0,32},{1,33},{2,34},{3,35},{4,36},{5,37},{6,38},{7,39},{8,40},{9,... | collective-permute-start | bytes 98312 | tf_op jit(solution)/shard_map/ppermute | solution.py:158
  16.1 20.8 %collective-permute-start.1 = (f32[128,64]{1,0:T(8,128)S(1)}, f32[128,64]{1,0:T(8,128)S(1)}, u32[]{:S(2)}, u32[]{:S(2)}) collective-permute-start(f32[128,64]{1,0:T(8,128)S(1)} %and_select_fusion), channel_id=1, source_target_pairs={{0,224},{1,225},{2,226},{3,227},{4,228},{5,229},{6,230},{7,231},{8... | collective-permute-start | bytes 98312 | tf_op jit(solution)/shard_map/ppermute | solution.py:158
  36.9 9.9 %collective-permute-start.2 = (bf16[64,3584]{1,0:T(8,128)(2,1)S(1)}, bf16[64,3584]{1,0:T(8,128)(2,1)S(1)}, u32[]{:S(2)}, u32[]{:S(2)}) collective-permute-start(bf16[64,3584]{1,0:T(8,128)(2,1)S(1)} %get-tuple-element.31.p0), channel_id=1, source_target_pairs={{0,2},{1,3},{2,0},{3,1},{4,6},{5,7},{6,4},{7,5},{8,10},{9,11},{10,... | collective-permute-start | bytes 1376264 | tf_op jit(solution)/shard_map/ppermute | solution.py:158
  38.5 8.3 %collective-permute-start.3 = (bf16[64,3584]{1,0:T(8,128)(2,1)S(1)}, bf16[64,3584]{1,0:T(8,128)(2,1)S(1)}, u32[]{:S(2)}, u32[]{:S(2)}) collective-permute-start(bf16[64,3584]{1,0:T(8,128)(2,1)S(1)} %get-tuple-element.31.p0), channel_id=1, source_target_pairs={{0,1},{1,0},{2,3},{3,2},{4,5},{5,4},{6,7},{7,6},{8,9},{9,8},{10,11... | collective-permute-start | bytes 1376264 | tf_op jit(solution)/shard_map/ppermute | solution.py:158
  38.5 8.3 %collective-permute-start.4 = (bf16[64,3584]{1,0:T(8,128)(2,1)S(1)}, bf16[64,3584]{1,0:T(8,128)(2,1)S(1)}, u32[]{:S(2)}, u32[]{:S(2)}) collective-permute-start(bf16[64,3584]{1,0:T(8,128)(2,1)S(1)} %get-tuple-element.40.p0), channel_id=1, source_target_pairs={{0,1},{1,0},{2,3},{3,2},{4,5},{5,4},{6,7},{7,6},{8,9},{9,8},{10,11... | collective-permute-start | bytes 1376264 | tf_op jit(solution)/shard_map/ppermute | solution.py:158
  46.8 1.8 %collective-permute-start.5 = (bf16[64,3584]{1,0:T(8,128)(2,1)S(1)}, bf16[64,3584]{1,0:T(8,128)(2,1)S(1)}, u32[]{:S(2)}, u32[]{:S(2)}) collective-permute-start(bf16[64,3584]{1,0:T(8,128)(2,1)S(1)} %collective-permute-done.2.p1), channel_id=1, source_target_pairs={{0,1},{1,0},{2,3},{3,2},{4,5},{5,4},{6,7},{7,6},{8,9},{9,8},{10,11... | collective-permute-start | bytes 1376264 | tf_op jit(solution)/shard_map/ppermute | solution.py:158
  46.8 12.9 %collective-permute-start.8 = (bf16[64,3584]{1,0:T(8,128)(2,1)S(1)}, bf16[64,3584]{1,0:T(8,128)(2,1)S(1)}, u32[]{:S(2)}, u32[]{:S(2)}) collective-permute-start(bf16[64,3584]{1,0:T(8,128)(2,1)S(1)} %get-tuple-element.40.p0), channel_id=1, source_target_pairs={{0,2},{1,3},{2,0},{3,1},{4,6},{5,7},{6,4},{7,5},{8,10},{9,11},{10,... | collective-permute-start | bytes 1376264 | tf_op jit(solution)/shard_map/ppermute | solution.py:158
  48.6 1.8 %copy-start.1 = (bf16[1,3584,384]{2,1,0:T(8,128)(2,1)S(1)}, bf16[1,3584,384]{2,1,0:T(8,128)(2,1)}, u32[]{:S(2)}) copy-start(bf16[1,3584,384]{2,1,0:T(8,128)(2,1)} %param.11) | copy-start | bytes 8257540
  50.4 1.8 %copy-start.3 = (bf16[1,3584,384]{2,1,0:T(8,128)(2,1)S(1)}, bf16[1,3584,384]{2,1,0:T(8,128)(2,1)}, u32[]{:S(2)}) copy-start(bf16[1,3584,384]{2,1,0:T(8,128)(2,1)} %param.12) | copy-start | bytes 8257540
  52.2 1.8 %copy-start.5 = (bf16[1,384,3584]{2,1,0:T(8,128)(2,1)S(1)}, bf16[1,384,3584]{2,1,0:T(8,128)(2,1)}, u32[]{:S(2)}) copy-start(bf16[1,384,3584]{2,1,0:T(8,128)(2,1)} %param.13) | copy-start | bytes 8257540
  54.0 7.6 %copy-start.2 = (bf16[1,3584,384]{2,1,0:T(8,128)(2,1)S(1)}, bf16[1,3584,384]{2,1,0:T(8,128)(2,1)}, u32[]{:S(2)}) copy-start(bf16[1,3584,384]{2,1,0:T(8,128)(2,1)} %param.11) | copy-start | bytes 8257540
  54.0 7.6 %copy-start.4 = (bf16[1,3584,384]{2,1,0:T(8,128)(2,1)S(1)}, bf16[1,3584,384]{2,1,0:T(8,128)(2,1)}, u32[]{:S(2)}) copy-start(bf16[1,3584,384]{2,1,0:T(8,128)(2,1)} %param.12) | copy-start | bytes 8257540
  54.0 7.6 %copy-start.6 = (bf16[1,384,3584]{2,1,0:T(8,128)(2,1)S(1)}, bf16[1,384,3584]{2,1,0:T(8,128)(2,1)}, u32[]{:S(2)}) copy-start(bf16[1,384,3584]{2,1,0:T(8,128)(2,1)} %param.13) | copy-start | bytes 8257540
  57.4 2.4 %collective-permute-start.7 = (bf16[64,3584]{1,0:T(8,128)(2,1)S(1)}, bf16[64,3584]{1,0:T(8,128)(2,1)S(1)}, u32[]{:S(2)}, u32[]{:S(2)}) collective-permute-start(bf16[64,3584]{1,0:T(8,128)(2,1)S(1)} %get-tuple-element.37), channel_id=1, source_target_pairs={{0,1},{1,0},{2,3},{3,2},{4,5},{5,4},{6,7},{7,6},{8,9},{9,8},{10,11... | collective-permute-start | bytes 1376264 | tf_op jit(solution)/shard_map/ppermute | solution.py:158
  59.8 1.8 %collective-permute-start.9 = (bf16[64,3584]{1,0:T(8,128)(2,1)S(1)}, bf16[64,3584]{1,0:T(8,128)(2,1)S(1)}, u32[]{:S(2)}, u32[]{:S(2)}) collective-permute-start(bf16[64,3584]{1,0:T(8,128)(2,1)S(1)} %collective-permute-done.8.p1), channel_id=1, source_target_pairs={{0,1},{1,0},{2,3},{3,2},{4,5},{5,4},{6,7},{7,6},{8,9},{9,8},{10,11... | collective-permute-start | bytes 1376264 | tf_op jit(solution)/shard_map/ppermute | solution.py:158
  64.8 2.2 %collective-permute-start.12 = (bf16[64,3584]{1,0:T(8,128)(2,1)S(1)}, bf16[64,3584]{1,0:T(8,128)(2,1)S(1)}, u32[]{:S(2)}, u32[]{:S(2)}) collective-permute-start(bf16[64,3584]{1,0:T(8,128)(2,1)S(1)} %get-tuple-element.50), channel_id=1, source_target_pairs={{0,1},{1,0},{2,3},{3,2},{4,5},{5,4},{6,7},{7,6},{8,9},{9,8},{10,11... | collective-permute-start | bytes 1376264 | tf_op jit(solution)/shard_map/ppermute | solution.py:158
  65.0 4.1 %collective-permute-start.6 = (bf16[64,3584]{1,0:T(8,128)(2,1)S(1)}, bf16[64,3584]{1,0:T(8,128)(2,1)S(1)}, u32[]{:S(2)}, u32[]{:S(2)}) collective-permute-start(bf16[64,3584]{1,0:T(8,128)(2,1)S(1)} %get-tuple-element.35), channel_id=1, source_target_pairs={{0,1},{1,0},{2,3},{3,2},{4,5},{5,4},{6,7},{7,6},{8,9},{9,8},{10,11... | collective-permute-start | bytes 1376264 | tf_op jit(solution)/shard_map/ppermute | solution.py:158
  65.4 13.4 %collective-permute-start.10 = (bf16[64,3584]{1,0:T(8,128)(2,1)S(1)}, bf16[64,3584]{1,0:T(8,128)(2,1)S(1)}, u32[]{:S(2)}, u32[]{:S(2)}) collective-permute-start(bf16[64,3584]{1,0:T(8,128)(2,1)S(1)} %add_convert_fusion.3), channel_id=1, source_target_pairs={{0,2},{1,3},{2,0},{3,1},{4,6},{5,7},{6,4},{7,5},{8,10},{9,11},{10,... | collective-permute-start | bytes 1376264 | tf_op jit(solution)/shard_map/ppermute | solution.py:158
  67.0 20.2 %collective-permute-start.11 = (bf16[64,3584]{1,0:T(8,128)(2,1)S(1)}, bf16[64,3584]{1,0:T(8,128)(2,1)S(1)}, u32[]{:S(2)}, u32[]{:S(2)}) collective-permute-start(bf16[64,3584]{1,0:T(8,128)(2,1)S(1)} %get-tuple-element.48), channel_id=1, source_target_pairs={{0,1},{1,0},{2,3},{3,2},{4,5},{5,4},{6,7},{7,6},{8,9},{9,8},{10,11... | collective-permute-start | bytes 1376264 | tf_op jit(solution)/shard_map/ppermute | solution.py:158
  67.9 19.9 %collective-permute-start.13 = (bf16[64,3584]{1,0:T(8,128)(2,1)}, bf16[64,3584]{1,0:T(8,128)(2,1)S(1)}, u32[]{:S(2)}, u32[]{:S(2)}) collective-permute-start(bf16[64,3584]{1,0:T(8,128)(2,1)} %add_convert_fusion.1), channel_id=1, source_target_pairs={{0,2},{1,3},{2,0},{3,1},{4,6},{5,7},{6,4},{7,5},{8,10},{9,11},{10,... | collective-permute-start | bytes 1376264 | tf_op jit(solution)/shard_map/ppermute | solution.py:158
  79.7 21.0 %all-to-all-start.1 = ((bf16[8,8,3584]{2,1,0:T(8,128)(2,1)}), bf16[8,8,3584]{2,1,0:T(8,128)(2,1)S(1)}, u32[]{:S(2)}, u32[]{:S(2)}) async-start(bf16[8,8,3584]{2,1,0:T(8,128)(2,1)} %fusion.1), calls=%async_computation.1 | async-start | bytes 917504 | tf_op jit(solution)/shard_map/all_to_all | solution.py:38
  88.0 14.5 %collective-permute-start.14 = (bf16[64,3584]{1,0:T(8,128)(2,1)S(1)}, bf16[64,3584]{1,0:T(8,128)(2,1)}, u32[]{:S(2)}, u32[]{:S(2)}) collective-permute-start(bf16[64,3584]{1,0:T(8,128)(2,1)S(1)} %add_convert_fusion), channel_id=1, source_target_pairs={{0,226},{1,227},{2,224},{3,225},{4,230},{5,231},{6,228},{7,229},{8... | collective-permute-start | bytes 1376264 | tf_op jit(solution)/shard_map/ppermute | solution.py:158
  102.5 23.5 %all-to-all-start.2 = ((bf16[8,8,3584]{2,1,0:T(8,128)(2,1)}), bf16[8,8,3584]{2,1,0:T(8,128)(2,1)S(1)}, u32[]{:S(2)}, u32[]{:S(2)}) async-start(bf16[8,8,3584]{2,1,0:T(8,128)(2,1)} %bitcast.13), calls=%async_computation.2 | async-start | bytes 917504 | tf_op jit(solution)/shard_map/all_to_all | solution.py:38
  109.9 14.7 %collective-permute-start.15 = (bf16[64,3584]{1,0:T(8,128)(2,1)S(1)}, bf16[64,3584]{1,0:T(8,128)(2,1)S(1)}, u32[]{:S(2)}, u32[]{:S(2)}) collective-permute-start(bf16[64,3584]{1,0:T(8,128)(2,1)S(1)} %bitcast.32), channel_id=1, source_target_pairs={{0,34},{1,35},{2,32},{3,33},{4,38},{5,39},{6,36},{7,37},{8,42},{9,... | collective-permute-start | bytes 1376264 | tf_op jit(solution)/shard_map/ppermute | solution.py:158

commit v5 on v4

--- a/solution.py
+++ b/solution.py
@@ -115,18 +115,23 @@
     )(*operands)
 
 
-def mix_kernel(combine_ref, value_ref, out_ref):
+def mix_kernel(combine_ref, value_ref, out_ref, out_scr, sems):
     combine = combine_ref[...]
     hi = combine.astype(jnp.bfloat16)
     rest = combine - hi.astype(jnp.float32)
     mid = rest.astype(jnp.bfloat16)
     low = (rest - mid.astype(jnp.float32)).astype(jnp.bfloat16)
     weights = jnp.concatenate([hi, mid, low], axis=1)
+    copies = []
     step = out_ref.shape[1] // N_STEPS
     for n in range(N_STEPS):
         cols = pl.ds(n * step, step)
         value = value_ref[:, cols]
-        out_ref[:, cols] = dot(weights, jnp.concatenate([value, value, value], axis=0)).astype(jnp.bfloat16)
+        out_scr[:, cols] = dot(weights, jnp.concatenate([value, value, value], axis=0)).astype(jnp.bfloat16)
+        copies.append(pltpu.make_async_copy(out_scr.at[:, cols], out_ref.at[:, cols], sems.at[n]))
+        copies[-1].start()
+    for copy in copies:
+        copy.wait()
 
 
 def mix(combine, values, cost):
@@ -134,7 +139,11 @@
         mix_kernel,
         out_shape=jax.ShapeDtypeStruct((combine.shape[0], values.shape[1]), jnp.bfloat16),
         in_specs=[VMEM, VMEM],
-        out_specs=VMEM,
+        out_specs=pl.BlockSpec(memory_space=pl.ANY),
+        scratch_shapes=[
+            pltpu.VMEM((combine.shape[0], values.shape[1]), jnp.bfloat16),
+            pltpu.SemaphoreType.DMA((N_STEPS,)),
+        ],
         compiler_params=pltpu.CompilerParams(vmem_limit_bytes=20 * 2**20),
         cost_estimate=pl.CostEstimate(flops=cost, bytes_accessed=2_000_000, transcendentals=0),
     )(combine, values)

time: 128 us -> 128 us (level)
  no operation moved by 1% of the time
where the time goes in v5:
time: 128 us; the launch traced here: 127 us
  waiting for transfers between devices  61.7 us (48%)
  starting transfers between devices  44.6 us (35%)
  Pallas kernels  9 us (7%)
  local copies, waits for them, and re-layouts  5.98 us (5%)
  other arithmetic  3.19 us (2%)
  matrix products  1.71 us (1%)
    ppermute x16, waiting for transfers between devices, to(): return lax.ppermute(values, AXES, table)  36 us
    all_to_all x3, waiting for transfers between devices, over_z(): lax.all_to_all(values, 'ep', 0, 0, axis_index_groups=Z_GROUPS, tiled=True)  25.7 us
    all_to_all x3, starting transfers between devices, over_z(): lax.all_to_all(values, 'ep', 0, 0, axis_index_groups=Z_GROUPS, tiled=True)  23.6 us
    ppermute x16, starting transfers between devices, to(): return lax.ppermute(values, AXES, table)  21 us
    pallas_call x2, Pallas kernels, expert_call(): pl.pallas_call(kernel, out_shape=out_shape, in_specs=[VMEM] * len(operand...  6.58 us
    unnamed x20, local copies, waits for them, and re-layouts  5.36 us
  transfers between devices with their start and end apart: 19, of which 10 were waited for; matrix products, arithmetic and copies ran while one was open for 2% of the time, Pallas kernels for 4%

profile of v5, /device:TPU:32, one launch (start us, length us, event | category | flops | bytes accessed | tf_op | source)
XLA Modules:
  0.0 127.2 jit_solution(8614028982974330762)
XLA Ops:
  0.6 0.0 copy-start
  0.6 0.0 copy-start.7
  0.7 0.8 convert_reduce_fusion
  1.5 0.1 copy.18
  1.6 0.2 reduce_window_sum.11
  1.9 0.0 copy-done
  1.9 0.4 fusion.4
  2.3 1.3 %fusion = bf16[128,3584]{1,0:T(8,128)(2,1)} fusion(f32[128,3584]{1,0:T(8,128)S(1)} %fusion.4, pred[128,128]{0,1:T(8,128)(4,1)S(1)} %bitcast.33, bf16[128,3584]{1,0:T(8,128)(2,1)S(1)} %copy-done.7), kind=kOutput, calls=%fused_computation.1 | convolution fusion | flops 118358016 | bytes 3686400 | tf_op jit(solution)/shard_map/dot_general | solution.py:42
  3.6 8.7 %all-to-all-start = ((bf16[8,16,3584]{2,1,0:T(8,128)(2,1)}), bf16[8,16,3584]{2,1,0:T(8,128)(2,1)S(1)}, u32[]{:S(2)}, u32[]{:S(2)}) async-start(bf16[8,16,3584]{2,1,0:T(8,128)(2,1)} %bitcast.2), calls=%async_computation | async-start | bytes 1835008 | tf_op jit(solution)/shard_map/all_to_all | solution.py:38
  12.3 0.0 copy-done.9
  12.4 0.0 copy-done.8
  12.4 0.1 copy.23
  12.5 0.1 copy.22
  12.6 0.1 copy.21
  12.7 0.1 eq.58
  12.8 3.3 %collective-permute-start = (f32[128,64]{1,0:T(8,128)S(1)}, f32[128,64]{1,0:T(8,128)S(1)}, u32[]{:S(2)}, u32[]{:S(2)}) collective-permute-start(f32[128,64]{1,0:T(8,128)S(1)} %and_select_fusion), channel_id=1, source_target_pairs={{0,32},{1,33},{2,34},{3,35},{4,36},{5,37},{6,38},{7,39},{8,40},{9,... | collective-permute-start | bytes 98312 | tf_op jit(solution)/shard_map/ppermute | solution.py:167
  16.1 2.4 %collective-permute-start.1 = (f32[128,64]{1,0:T(8,128)S(1)}, f32[128,64]{1,0:T(8,128)S(1)}, u32[]{:S(2)}, u32[]{:S(2)}) collective-permute-start(f32[128,64]{1,0:T(8,128)S(1)} %and_select_fusion), channel_id=1, source_target_pairs={{0,224},{1,225},{2,226},{3,227},{4,228},{5,229},{6,230},{7,231},{8... | collective-permute-start | bytes 98312 | tf_op jit(solution)/shard_map/ppermute | solution.py:167
  18.6 18.2 %all-to-all-done = bf16[8,16,3584]{2,1,0:T(8,128)(2,1)S(1)} async-done(((bf16[8,16,3584]{2,1,0:T(8,128)(2,1)}), bf16[8,16,3584]{2,1,0:T(8,128)(2,1)S(1)}, u32[]{:S(2)}, u32[]{:S(2)}) %all-to-all-start) | async-done | bytes 917536 | tf_op jit(solution)/shard_map/all_to_all | solution.py:38
  36.8 0.1 slice_bitcast_fusion
  36.9 0.0 collective-permute-done.combine_ref
  36.9 0.0 collective-permute-done.1.combine_ref
  36.9 1.7 %collective-permute-start.2 = (bf16[64,3584]{1,0:T(8,128)(2,1)S(1)}, bf16[64,3584]{1,0:T(8,128)(2,1)S(1)}, u32[]{:S(2)}, u32[]{:S(2)}) collective-permute-start(bf16[64,3584]{1,0:T(8,128)(2,1)S(1)} %get-tuple-element.31.p0), channel_id=1, source_target_pairs={{0,2},{1,3},{2,0},{3,1},{4,6},{5,7},{6,4},{7,5},{8,10},{9,11},{10,... | collective-permute-start | bytes 1376264 | tf_op jit(solution)/shard_map/ppermute | solution.py:167
  38.5 0.0 collective-permute-start.3
  38.5 0.5 collective-permute-start.4
  39.1 7.8 %collective-permute-done.2.p1 = bf16[64,3584]{1,0:T(8,128)(2,1)S(1)} collective-permute-done((bf16[64,3584]{1,0:T(8,128)(2,1)S(1)}, bf16[64,3584]{1,0:T(8,128)(2,1)S(1)}, u32[]{:S(2)}, u32[]{:S(2)}) %collective-permute-start.2) | collective-permute-done | bytes 458784 | tf_op jit(solution)/shard_map/ppermute | solution.py:167
  46.8 0.0 collective-permute-done.3.p2
  46.8 0.0 collective-permute-done.4.p2
  46.8 0.0 collective-permute-start.5
  46.8 1.7 %collective-permute-start.8 = (bf16[64,3584]{1,0:T(8,128)(2,1)S(1)}, bf16[64,3584]{1,0:T(8,128)(2,1)S(1)}, u32[]{:S(2)}, u32[]{:S(2)}) collective-permute-start(bf16[64,3584]{1,0:T(8,128)(2,1)S(1)} %get-tuple-element.40.p0), channel_id=1, source_target_pairs={{0,2},{1,3},{2,0},{3,1},{4,6},{5,7},{6,4},{7,5},{8,10},{9,11},{10,... | collective-permute-start | bytes 1376264 | tf_op jit(solution)/shard_map/ppermute | solution.py:167
  48.5 0.1 collective-permute-done.5.p3
  48.6 1.8 %copy-done.1 = bf16[1,3584,384]{2,1,0:T(8,128)(2,1)S(1)} copy-done((bf16[1,3584,384]{2,1,0:T(8,128)(2,1)S(1)}, bf16[1,3584,384]{2,1,0:T(8,128)(2,1)}, u32[]{:S(2)}) %copy-start.1) | copy-done | bytes 2752536
  50.4 1.8 %copy-done.3 = bf16[1,3584,384]{2,1,0:T(8,128)(2,1)S(1)} copy-done((bf16[1,3584,384]{2,1,0:T(8,128)(2,1)S(1)}, bf16[1,3584,384]{2,1,0:T(8,128)(2,1)}, u32[]{:S(2)}) %copy-start.3) | copy-done | bytes 2752536
  52.2 1.8 %copy-done.5 = bf16[1,384,3584]{2,1,0:T(8,128)(2,1)S(1)} copy-done((bf16[1,384,3584]{2,1,0:T(8,128)(2,1)S(1)}, bf16[1,384,3584]{2,1,0:T(8,128)(2,1)}, u32[]{:S(2)}) %copy-start.5) | copy-done | bytes 2752536
  54.0 3.4 %shard_map.86 = (bf16[64,3584]{1,0:T(8,128)(2,1)S(1)}, bf16[64,3584]{1,0:T(8,128)(2,1)S(1)}, bf16[64,3584]{1,0:T(8,128)(2,1)S(1)}, bf16[64,3584]{1,0:T(8,128)(2,...) custom-call(bf16[64,3584]{1,0:T(8,128)(2,1)S(1)} %get-tuple-element.31.p0, ...), custom_call_target="tpu_custom_call" | custom-call | flops 20000000000 | bytes 12000000 | tf_op jit(solution)/shard_map/pallas_call | solution.py:107
  57.4 0.2 collective-permute-start.7
  57.6 2.2 %collective-permute-done.8.p1 = bf16[64,3584]{1,0:T(8,128)(2,1)S(1)} collective-permute-done((bf16[64,3584]{1,0:T(8,128)(2,1)S(1)}, bf16[64,3584]{1,0:T(8,128)(2,1)S(1)}, u32[]{:S(2)}, u32[]{:S(2)}) %collective-permute-start.8) | collective-permute-done | bytes 458784 | tf_op jit(solution)/shard_map/ppermute | solution.py:167
  59.8 0.0 collective-permute-start.9
  59.8 0.0 collective-permute-done.7
  59.8 0.1 add_convert_fusion.3
  59.9 1.7 %collective-permute-done.9.p3 = bf16[64,3584]{1,0:T(8,128)(2,1)S(1)} collective-permute-done((bf16[64,3584]{1,0:T(8,128)(2,1)S(1)}, bf16[64,3584]{1,0:T(8,128)(2,1)S(1)}, u32[]{:S(2)}, u32[]{:S(2)}) %collective-permute-start.9) | collective-permute-done | bytes 458784 | tf_op jit(solution)/shard_map/ppermute | solution.py:167
  61.6 3.2 %shard_map.87 = (bf16[64,3584]{1,0:T(8,128)(2,1)S(1)}, bf16[64,3584]{1,0:T(8,128)(2,1)S(1)}, bf16[64,3584]{1,0:T(8,128)(2,1)S(1)}, bf16[64,3584]{1,0:T(8,128)(2,1)S(1)}) custom-call(bf16[64,3584]{1,0:T(8,128)(2,1)S(1)} %get-tuple-element.40.p0, bf16[64,3584]{1,0:T(8,128)(2,1)S(1)} %collective-permute-done.8.p1, ...), custom_call_target="tpu_custom_call" | custom-call | flops 20000000000 | bytes 12000000 | tf_op jit(solution)/shard_map/pallas_call | solution.py:107
  64.8 0.2 collective-permute-start.12
  65.0 0.4 collective-permute-start.6
  65.4 1.6 %collective-permute-start.10 = (bf16[64,3584]{1,0:T(8,128)(2,1)S(1)}, bf16[64,3584]{1,0:T(8,128)(2,1)S(1)}, u32[]{:S(2)}, u32[]{:S(2)}) collective-permute-start(bf16[64,3584]{1,0:T(8,128)(2,1)S(1)} %add_convert_fusion.3), channel_id=1, source_target_pairs={{0,2},{1,3},{2,0},{3,1},{4,6},{5,7},{6,4},{7,5},{8,10},{9,11},{10,... | collective-permute-start | bytes 1376264 | tf_op jit(solution)/shard_map/ppermute | solution.py:167
  67.0 0.0 collective-permute-start.11
  67.0 0.0 collective-permute-done.12
  67.0 0.9 add_convert_fusion.1
  67.9 1.3 %collective-permute-start.13 = (bf16[64,3584]{1,0:T(8,128)(2,1)}, bf16[64,3584]{1,0:T(8,128)(2,1)S(1)}, u32[]{:S(2)}, u32[]{:S(2)}) collective-permute-start(bf16[64,3584]{1,0:T(8,128)(2,1)} %add_convert_fusion.1), channel_id=1, source_target_pairs={{0,2},{1,3},{2,0},{3,1},{4,6},{5,7},{6,4},{7,5},{8,10},{9,11},{10,... | collective-permute-start | bytes 1376264 | tf_op jit(solution)/shard_map/ppermute | solution.py:167
  69.2 0.0 collective-permute-done.6
  69.2 9.6 %collective-permute-done.10 = bf16[64,3584]{1,0:T(8,128)(2,1)S(1)} collective-permute-done((bf16[64,3584]{1,0:T(8,128)(2,1)S(1)}, bf16[64,3584]{1,0:T(8,128)(2,1)S(1)}, u32[]{:S(2)}, u32[]{:S(2)}) %collective-permute-start.10) | collective-permute-done | bytes 458784 | tf_op jit(solution)/shard_map/ppermute | solution.py:167
  78.8 0.9 fusion.1
  79.7 7.4 %all-to-all-start.1 = ((bf16[8,8,3584]{2,1,0:T(8,128)(2,1)}), bf16[8,8,3584]{2,1,0:T(8,128)(2,1)S(1)}, u32[]{:S(2)}, u32[]{:S(2)}) async-start(bf16[8,8,3584]{2,1,0:T(8,128)(2,1)} %fusion.1), calls=%async_computation.1 | async-start | bytes 917504 | tf_op jit(solution)/shard_map/all_to_all | solution.py:38
  87.1 0.0 collective-permute-done.11
  87.1 0.7 collective-permute-done.13
  87.8 0.2 add_convert_fusion
  88.0 5.3 %collective-permute-start.14 = (bf16[64,3584]{1,0:T(8,128)(2,1)S(1)}, bf16[64,3584]{1,0:T(8,128)(2,1)}, u32[]{:S(2)}, u32[]{:S(2)}) collective-permute-start(bf16[64,3584]{1,0:T(8,128)(2,1)S(1)} %add_convert_fusion), channel_id=1, source_target_pairs={{0,226},{1,227},{2,224},{3,225},{4,230},{5,231},{6,228},{7,229},{8... | collective-permute-start | bytes 1376264 | tf_op jit(solution)/shard_map/ppermute | solution.py:167
  93.3 7.5 %all-to-all-done.1 = bf16[8,8,3584]{2,1,0:T(8,128)(2,1)S(1)} async-done(((bf16[8,8,3584]{2,1,0:T(8,128)(2,1)}), bf16[8,8,3584]{2,1,0:T(8,128)(2,1)S(1)}, u32[]{:S(2)}, u32[]{:S(2)}) %all-to-all-start.1) | async-done | bytes 458784 | tf_op jit(solution)/shard_map/all_to_all | solution.py:38
  100.7 1.8 %collective-permute-done.14 = bf16[64,3584]{1,0:T(8,128)(2,1)} collective-permute-done((bf16[64,3584]{1,0:T(8,128)(2,1)S(1)}, bf16[64,3584]{1,0:T(8,128)(2,1)}, u32[]{:S(2)}, u32[]{:S(2)}) %collective-permute-start.14) | collective-permute-done | bytes 458784 | tf_op jit(solution)/shard_map/ppermute | solution.py:167
  102.5 7.4 %all-to-all-start.2 = ((bf16[8,8,3584]{2,1,0:T(8,128)(2,1)}), bf16[8,8,3584]{2,1,0:T(8,128)(2,1)S(1)}, u32[]{:S(2)}, u32[]{:S(2)}) async-start(bf16[8,8,3584]{2,1,0:T(8,128)(2,1)} %bitcast.13), calls=%async_computation.2 | async-start | bytes 917504 | tf_op jit(solution)/shard_map/all_to_all | solution.py:38
  109.9 2.5 %collective-permute-start.15 = (bf16[64,3584]{1,0:T(8,128)(2,1)S(1)}, bf16[64,3584]{1,0:T(8,128)(2,1)S(1)}, u32[]{:S(2)}, u32[]{:S(2)}) collective-permute-start(bf16[64,3584]{1,0:T(8,128)(2,1)S(1)} %bitcast.32), channel_id=1, source_target_pairs={{0,34},{1,35},{2,32},{3,33},{4,38},{5,39},{6,36},{7,37},{8,42},{9,... | collective-permute-start | bytes 1376264 | tf_op jit(solution)/shard_map/ppermute | solution.py:167
  112.4 12.2 %collective-permute-done.15.value_ref = bf16[64,3584]{1,0:T(8,128)(2,1)S(1)} collective-permute-done((bf16[64,3584]{1,0:T(8,128)(2,1)S(1)}, bf16[64,3584]{1,0:T(8,128)(2,1)S(1)}, u32[]{:S(2)}, u32[]{:S(2)}) %collective-permute-start.15) | collective-permute-done | bytes 458784 | tf_op jit(solution)/shard_map/ppermute | solution.py:167
  124.6 1.2 shard_map.88
  125.8 0.0 all-to-all-done.2
  125.9 1.2 shard_map.89
  (24 shorter events, 0.2 us)
Async XLA Ops:
  0.6 1.3 copy-start
  0.6 1.7 %copy-start.7 = (bf16[128,3584]{1,0:T(8,128)(2,1)S(1)}, bf16[128,3584]{1,0:T(8,128)(2,1)}, u32[]{:S(2)}) copy-start(bf16[128,3584]{1,0:T(8,128)(2,1)} %param.8) | copy-start | bytes 2752516
  3.6 8.7 %copy-start.9 = (f32[128,8]{0,1:T(8,128)S(1)}, f32[128,8]{0,1:T(8,128)}, u32[]{:S(2)}) copy-start(f32[128,8]{0,1:T(8,128)} %param.10) | copy-start | bytes 12292
  3.6 8.7 %copy-start.8 = (s32[128,8]{0,1:T(8,128)S(1)}, s32[128,8]{0,1:T(8,128)}, u32[]{:S(2)}) copy-start(s32[128,8]{0,1:T(8,128)} %param.9) | copy-start | bytes 12292
  3.6 33.2 %all-to-all-start = ((bf16[8,16,3584]{2,1,0:T(8,128)(2,1)}), bf16[8,16,3584]{2,1,0:T(8,128)(2,1)S(1)}, u32[]{:S(2)}, u32[]{:S(2)}) async-start(bf16[8,16,3584]{2,1,0:T(8,128)(2,1)} %bitcast.2), calls=%async_computation | async-start | bytes 1835008 | tf_op jit(solution)/shard_map/all_to_all | solution.py:38
  12.8 24.0 %collective-permute-start = (f32[128,64]{1,0:T(8,128)S(1)}, f32[128,64]{1,0:T(8,128)S(1)}, u32[]{:S(2)}, u32[]{:S(2)}) collective-permute-start(f32[128,64]{1,0:T(8,128)S(1)} %and_select_fusion), channel_id=1, source_target_pairs={{0,32},{1,33},{2,34},{3,35},{4,36},{5,37},{6,38},{7,39},{8,40},{9,... | collective-permute-start | bytes 98312 | tf_op jit(solution)/shard_map/ppermute | solution.py:167
  16.1 20.8 %collective-permute-start.1 = (f32[128,64]{1,0:T(8,128)S(1)}, f32[128,64]{1,0:T(8,128)S(1)}, u32[]{:S(2)}, u32[]{:S(2)}) collective-permute-start(f32[128,64]{1,0:T(8,128)S(1)} %and_select_fusion), channel_id=1, source_target_pairs={{0,224},{1,225},{2,226},{3,227},{4,228},{5,229},{6,230},{7,231},{8... | collective-permute-start | bytes 98312 | tf_op jit(solution)/shard_map/ppermute | solution.py:167
  36.9 9.9 %collective-permute-start.2 = (bf16[64,3584]{1,0:T(8,128)(2,1)S(1)}, bf16[64,3584]{1,0:T(8,128)(2,1)S(1)}, u32[]{:S(2)}, u32[]{:S(2)}) collective-permute-start(bf16[64,3584]{1,0:T(8,128)(2,1)S(1)} %get-tuple-element.31.p0), channel_id=1, source_target_pairs={{0,2},{1,3},{2,0},{3,1},{4,6},{5,7},{6,4},{7,5},{8,10},{9,11},{10,... | collective-permute-start | bytes 1376264 | tf_op jit(solution)/shard_map/ppermute | solution.py:167
  38.5 8.3 %collective-permute-start.3 = (bf16[64,3584]{1,0:T(8,128)(2,1)S(1)}, bf16[64,3584]{1,0:T(8,128)(2,1)S(1)}, u32[]{:S(2)}, u32[]{:S(2)}) collective-permute-start(bf16[64,3584]{1,0:T(8,128)(2,1)S(1)} %get-tuple-element.31.p0), channel_id=1, source_target_pairs={{0,1},{1,0},{2,3},{3,2},{4,5},{5,4},{6,7},{7,6},{8,9},{9,8},{10,11... | collective-permute-start | bytes 1376264 | tf_op jit(solution)/shard_map/ppermute | solution.py:167
  38.5 8.3 %collective-permute-start.4 = (bf16[64,3584]{1,0:T(8,128)(2,1)S(1)}, bf16[64,3584]{1,0:T(8,128)(2,1)S(1)}, u32[]{:S(2)}, u32[]{:S(2)}) collective-permute-start(bf16[64,3584]{1,0:T(8,128)(2,1)S(1)} %get-tuple-element.40.p0), channel_id=1, source_target_pairs={{0,1},{1,0},{2,3},{3,2},{4,5},{5,4},{6,7},{7,6},{8,9},{9,8},{10,11... | collective-permute-start | bytes 1376264 | tf_op jit(solution)/shard_map/ppermute | solution.py:167
  46.8 1.8 %collective-permute-start.5 = (bf16[64,3584]{1,0:T(8,128)(2,1)S(1)}, bf16[64,3584]{1,0:T(8,128)(2,1)S(1)}, u32[]{:S(2)}, u32[]{:S(2)}) collective-permute-start(bf16[64,3584]{1,0:T(8,128)(2,1)S(1)} %collective-permute-done.2.p1), channel_id=1, source_target_pairs={{0,1},{1,0},{2,3},{3,2},{4,5},{5,4},{6,7},{7,6},{8,9},{9,8},{10,11... | collective-permute-start | bytes 1376264 | tf_op jit(solution)/shard_map/ppermute | solution.py:167
  46.8 12.9 %collective-permute-start.8 = (bf16[64,3584]{1,0:T(8,128)(2,1)S(1)}, bf16[64,3584]{1,0:T(8,128)(2,1)S(1)}, u32[]{:S(2)}, u32[]{:S(2)}) collective-permute-start(bf16[64,3584]{1,0:T(8,128)(2,1)S(1)} %get-tuple-element.40.p0), channel_id=1, source_target_pairs={{0,2},{1,3},{2,0},{3,1},{4,6},{5,7},{6,4},{7,5},{8,10},{9,11},{10,... | collective-permute-start | bytes 1376264 | tf_op jit(solution)/shard_map/ppermute | solution.py:167
  48.6 1.8 %copy-start.1 = (bf16[1,3584,384]{2,1,0:T(8,128)(2,1)S(1)}, bf16[1,3584,384]{2,1,0:T(8,128)(2,1)}, u32[]{:S(2)}) copy-start(bf16[1,3584,384]{2,1,0:T(8,128)(2,1)} %param.11) | copy-start | bytes 8257540
  50.4 1.8 %copy-start.3 = (bf16[1,3584,384]{2,1,0:T(8,128)(2,1)S(1)}, bf16[1,3584,384]{2,1,0:T(8,128)(2,1)}, u32[]{:S(2)}) copy-start(bf16[1,3584,384]{2,1,0:T(8,128)(2,1)} %param.12) | copy-start | bytes 8257540
  52.2 1.8 %copy-start.5 = (bf16[1,384,3584]{2,1,0:T(8,128)(2,1)S(1)}, bf16[1,384,3584]{2,1,0:T(8,128)(2,1)}, u32[]{:S(2)}) copy-start(bf16[1,384,3584]{2,1,0:T(8,128)(2,1)} %param.13) | copy-start | bytes 8257540
  54.0 7.6 %copy-start.2 = (bf16[1,3584,384]{2,1,0:T(8,128)(2,1)S(1)}, bf16[1,3584,384]{2,1,0:T(8,128)(2,1)}, u32[]{:S(2)}) copy-start(bf16[1,3584,384]{2,1,0:T(8,128)(2,1)} %param.11) | copy-start | bytes 8257540
  54.0 7.6 %copy-start.4 = (bf16[1,3584,384]{2,1,0:T(8,128)(2,1)S(1)}, bf16[1,3584,384]{2,1,0:T(8,128)(2,1)}, u32[]{:S(2)}) copy-start(bf16[1,3584,384]{2,1,0:T(8,128)(2,1)} %param.12) | copy-start | bytes 8257540
  54.0 7.6 %copy-start.6 = (bf16[1,384,3584]{2,1,0:T(8,128)(2,1)S(1)}, bf16[1,384,3584]{2,1,0:T(8,128)(2,1)}, u32[]{:S(2)}) copy-start(bf16[1,384,3584]{2,1,0:T(8,128)(2,1)} %param.13) | copy-start | bytes 8257540
  57.4 2.4 %collective-permute-start.7 = (bf16[64,3584]{1,0:T(8,128)(2,1)S(1)}, bf16[64,3584]{1,0:T(8,128)(2,1)S(1)}, u32[]{:S(2)}, u32[]{:S(2)}) collective-permute-start(bf16[64,3584]{1,0:T(8,128)(2,1)S(1)} %get-tuple-element.37), channel_id=1, source_target_pairs={{0,1},{1,0},{2,3},{3,2},{4,5},{5,4},{6,7},{7,6},{8,9},{9,8},{10,11... | collective-permute-start | bytes 1376264 | tf_op jit(solution)/shard_map/ppermute | solution.py:167
  59.8 1.8 %collective-permute-start.9 = (bf16[64,3584]{1,0:T(8,128)(2,1)S(1)}, bf16[64,3584]{1,0:T(8,128)(2,1)S(1)}, u32[]{:S(2)}, u32[]{:S(2)}) collective-permute-start(bf16[64,3584]{1,0:T(8,128)(2,1)S(1)} %collective-permute-done.8.p1), channel_id=1, source_target_pairs={{0,1},{1,0},{2,3},{3,2},{4,5},{5,4},{6,7},{7,6},{8,9},{9,8},{10,11... | collective-permute-start | bytes 1376264 | tf_op jit(solution)/shard_map/ppermute | solution.py:167
  64.8 2.2 %collective-permute-start.12 = (bf16[64,3584]{1,0:T(8,128)(2,1)S(1)}, bf16[64,3584]{1,0:T(8,128)(2,1)S(1)}, u32[]{:S(2)}, u32[]{:S(2)}) collective-permute-start(bf16[64,3584]{1,0:T(8,128)(2,1)S(1)} %get-tuple-element.50), channel_id=1, source_target_pairs={{0,1},{1,0},{2,3},{3,2},{4,5},{5,4},{6,7},{7,6},{8,9},{9,8},{10,11... | collective-permute-start | bytes 1376264 | tf_op jit(solution)/shard_map/ppermute | solution.py:167
  65.0 4.1 %collective-permute-start.6 = (bf16[64,3584]{1,0:T(8,128)(2,1)S(1)}, bf16[64,3584]{1,0:T(8,128)(2,1)S(1)}, u32[]{:S(2)}, u32[]{:S(2)}) collective-permute-start(bf16[64,3584]{1,0:T(8,128)(2,1)S(1)} %get-tuple-element.35), channel_id=1, source_target_pairs={{0,1},{1,0},{2,3},{3,2},{4,5},{5,4},{6,7},{7,6},{8,9},{9,8},{10,11... | collective-permute-start | bytes 1376264 | tf_op jit(solution)/shard_map/ppermute | solution.py:167
  65.4 13.4 %collective-permute-start.10 = (bf16[64,3584]{1,0:T(8,128)(2,1)S(1)}, bf16[64,3584]{1,0:T(8,128)(2,1)S(1)}, u32[]{:S(2)}, u32[]{:S(2)}) collective-permute-start(bf16[64,3584]{1,0:T(8,128)(2,1)S(1)} %add_convert_fusion.3), channel_id=1, source_target_pairs={{0,2},{1,3},{2,0},{3,1},{4,6},{5,7},{6,4},{7,5},{8,10},{9,11},{10,... | collective-permute-start | bytes 1376264 | tf_op jit(solution)/shard_map/ppermute | solution.py:167
  67.0 20.2 %collective-permute-start.11 = (bf16[64,3584]{1,0:T(8,128)(2,1)S(1)}, bf16[64,3584]{1,0:T(8,128)(2,1)S(1)}, u32[]{:S(2)}, u32[]{:S(2)}) collective-permute-start(bf16[64,3584]{1,0:T(8,128)(2,1)S(1)} %get-tuple-element.48), channel_id=1, source_target_pairs={{0,1},{1,0},{2,3},{3,2},{4,5},{5,4},{6,7},{7,6},{8,9},{9,8},{10,11... | collective-permute-start | bytes 1376264 | tf_op jit(solution)/shard_map/ppermute | solution.py:167
  67.9 19.9 %collective-permute-start.13 = (bf16[64,3584]{1,0:T(8,128)(2,1)}, bf16[64,3584]{1,0:T(8,128)(2,1)S(1)}, u32[]{:S(2)}, u32[]{:S(2)}) collective-permute-start(bf16[64,3584]{1,0:T(8,128)(2,1)} %add_convert_fusion.1), channel_id=1, source_target_pairs={{0,2},{1,3},{2,0},{3,1},{4,6},{5,7},{6,4},{7,5},{8,10},{9,11},{10,... | collective-permute-start | bytes 1376264 | tf_op jit(solution)/shard_map/ppermute | solution.py:167
  79.7 21.0 %all-to-all-start.1 = ((bf16[8,8,3584]{2,1,0:T(8,128)(2,1)}), bf16[8,8,3584]{2,1,0:T(8,128)(2,1)S(1)}, u32[]{:S(2)}, u32[]{:S(2)}) async-start(bf16[8,8,3584]{2,1,0:T(8,128)(2,1)} %fusion.1), calls=%async_computation.1 | async-start | bytes 917504 | tf_op jit(solution)/shard_map/all_to_all | solution.py:38
  88.0 14.5 %collective-permute-start.14 = (bf16[64,3584]{1,0:T(8,128)(2,1)S(1)}, bf16[64,3584]{1,0:T(8,128)(2,1)}, u32[]{:S(2)}, u32[]{:S(2)}) collective-permute-start(bf16[64,3584]{1,0:T(8,128)(2,1)S(1)} %add_convert_fusion), channel_id=1, source_target_pairs={{0,226},{1,227},{2,224},{3,225},{4,230},{5,231},{6,228},{7,229},{8... | collective-permute-start | bytes 1376264 | tf_op jit(solution)/shard_map/ppermute | solution.py:167
  102.5 23.3 %all-to-all-start.2 = ((bf16[8,8,3584]{2,1,0:T(8,128)(2,1)}), bf16[8,8,3584]{2,1,0:T(8,128)(2,1)S(1)}, u32[]{:S(2)}, u32[]{:S(2)}) async-start(bf16[8,8,3584]{2,1,0:T(8,128)(2,1)} %bitcast.13), calls=%async_computation.2 | async-start | bytes 917504 | tf_op jit(solution)/shard_map/all_to_all | solution.py:38
  109.9 14.7 %collective-permute-start.15 = (bf16[64,3584]{1,0:T(8,128)(2,1)S(1)}, bf16[64,3584]{1,0:T(8,128)(2,1)S(1)}, u32[]{:S(2)}, u32[]{:S(2)}) collective-permute-start(bf16[64,3584]{1,0:T(8,128)(2,1)S(1)} %bitcast.32), channel_id=1, source_target_pairs={{0,34},{1,35},{2,32},{3,33},{4,38},{5,39},{6,36},{7,37},{8,42},{9,... | collective-permute-start | bytes 1376264 | tf_op jit(solution)/shard_map/ppermute | solution.py:167
